TPU v7x, 32 devices: a whole 2x2x4 slice. The times are simulated.
32 devices in a mesh: seq: 8 (over z, x), tp: 4 (over y, core).
Axes of the slice: x: 2, y: 2, z: 4, core: 2. Of those that a mesh axis runs over, the one named last changes fastest.
Arguments:
- enc_input: bfloat16 [4096, 1024], P('seq'), may hold values from -6 to 6
- dec_input: bfloat16 [3, 4096, 1024], P(None, 'seq'), may hold values from -6 to 6
- enc_cotan: bfloat16 [4096, 1024], P('seq'), may hold values from -6 to 6
- dec_cotan: bfloat16 [3, 4096, 1024], P(None, 'seq'), may hold values from -6 to 6
- doc_lengths: int32 [16], replicated, may hold values from 64 to 512, as said below
- src_padding: int32 [4096], replicated, may hold values 0 or 1
- enc_qkv: bfloat16 [3, 1024, 1024], P(None, None, 'tp'), may hold values from -0.1875 to 0.1875
- enc_wout: bfloat16 [1024, 1024], P('tp'), may hold values from -1.5 to 1.5
- enc_gain: float32 [1024], replicated, may hold values from 0.1 to 1.9
- enc_bias: float32 [1024], replicated, may hold values from -2.5 to 2.5
- enc_up: bfloat16 [1024, 4096], P(None, 'tp'), may hold values from -0.1875 to 0.1875
- enc_down: bfloat16 [4096, 1024], P('tp'), may hold values from -0.1875 to 0.1875
- post_gain: float32 [1024], replicated, may hold values from 0.1 to 1.9
- post_bias: float32 [1024], replicated, may hold values from -2.5 to 2.5
- self_qkv: bfloat16 [3, 1024, 1024], P(None, None, 'tp'), may hold values from -0.1875 to 0.1875
- self_rel: bfloat16 [1024, 512], P(None, 'tp'), may hold values from -0.1875 to 0.1875
- self_wout: bfloat16 [1024, 1024], P('tp'), may hold values from -1.5 to 1.5
- self_gain: float32 [1024], replicated, may hold values from 0.1 to 1.9
- self_bias: float32 [1024], replicated, may hold values from -2.5 to 2.5
- cross_wq: bfloat16 [1024, 1024], P(None, 'tp'), may hold values from -0.1875 to 0.1875
- cross_wkv: bfloat16 [2, 1024, 1024], P(None, None, 'tp'), may hold values from -0.1875 to 0.1875
- cross_wout: bfloat16 [1024, 1024], P('tp'), may hold values from -1.5 to 1.5
- cross_gain: float32 [1024], replicated, may hold values from 0.1 to 1.9
- cross_bias: float32 [1024], replicated, may hold values from -2.5 to 2.5
- ffn_up: bfloat16 [1024, 4096], P(None, 'tp'), may hold values from -0.1875 to 0.1875
- ffn_down: bfloat16 [4096, 1024], P('tp'), may hold values from -0.1875 to 0.1875
- ffn_gain: float32 [1024], replicated, may hold values from 0.1 to 1.9
- ffn_bias: float32 [1024], replicated, may hold values from -2.5 to 2.5
Outputs:
- enc_output: bfloat16 [4096, 1024], P('seq')
- dec_output: bfloat16 [3, 4096, 1024], P(None, 'seq')
- enc_grad: bfloat16 [4096, 1024], P('seq')
- dec_grad: bfloat16 [3, 4096, 1024], P(None, 'seq')
- grad_enc_qkv: float32 [3, 1024, 1024], P(None, None, 'tp')
- grad_enc_wout: float32 [1024, 1024], P('tp')
- grad_enc_gain: float32 [1024], replicated
- grad_enc_bias: float32 [1024], replicated
- grad_enc_up: float32 [1024, 4096], P(None, 'tp')
- grad_enc_down: float32 [4096, 1024], P('tp')
- grad_post_gain: float32 [1024], replicated
- grad_post_bias: float32 [1024], replicated
- grad_self_qkv: float32 [3, 1024, 1024], P(None, None, 'tp')
- grad_self_rel: float32 [1024, 512], P(None, 'tp')
- grad_self_wout: float32 [1024, 1024], P('tp')
- grad_self_gain: float32 [1024], replicated
- grad_self_bias: float32 [1024], replicated
- grad_cross_wq: float32 [1024, 1024], P(None, 'tp')
- grad_cross_wkv: float32 [2, 1024, 1024], P(None, None, 'tp')
- grad_cross_wout: float32 [1024, 1024], P('tp')
- grad_cross_gain: float32 [1024], replicated
- grad_cross_bias: float32 [1024], replicated
- grad_ffn_up: float32 [1024, 4096], P(None, 'tp')
- grad_ffn_down: float32 [4096, 1024], P('tp')
- grad_ffn_gain: float32 [1024], replicated
- grad_ffn_bias: float32 [1024], replicated
Inputs may be any that keep to these rules, and one draw needn't show every extreme that they name: `doc_lengths`: the lengths of the 16 documents in pack order; they sum to 4096, one is exactly 512 and one exactly 64.
All inputs are finite; a program needn't handle non-finite values.
Results may differ from a plain program's by a relative error of at most 0.03.
Values may be sent and summed in bfloat16 or wider, within the bound.
A program may use at most 384 MiB of HBM per device.

v0:
```python
import math

import jax
import jax.numpy as jnp
from jax import lax
from jax.sharding import PartitionSpec as P

HD = 64
BUCKETS = 32
DOC_MAX = 512


def with_halo(cells, sides, width):
    for axis, dim in sides:
        count = lax.axis_size(axis)
        ends = count - 1
        head = lax.slice_in_dim(cells, 0, width, axis=dim)
        tail = lax.slice_in_dim(cells, cells.shape[dim] - width, cells.shape[dim], axis=dim)
        cells = jnp.concatenate(
            [
                lax.ppermute(tail, axis, [(i, (i + 1) % count) for i in range(ends)]),
                cells,
                lax.ppermute(head, axis, [((i + 1) % count, i) for i in range(ends)]),
            ],
            axis=dim,
        )
    return cells


def passed_along(value, axis, steps):
    count = lax.axis_size(axis)
    leading, last = (max(0, -steps), min(count, count - steps))
    return lax.ppermute(value, axis, [(source, source + steps) for source in range(leading, last)])


def bucket_of(offset):
    exact = BUCKETS // 2
    total = jnp.zeros(offset.shape, jnp.int32)
    for level in range(1, BUCKETS):
        if level < exact:
            bound = level
        else:
            bound = int(math.ceil(exact * (128.0 / exact) ** ((level - exact) / exact)))
        total = total + (offset >= bound).astype(jnp.int32)
    return total


def doc_index(positions, ends):
    return jnp.sum((positions[:, None] >= ends[None, :]).astype(jnp.int32), 1)


def first_of(positions, starts, ends):
    owner = doc_index(positions, ends)
    match = owner[:, None] == jnp.arange(ends.shape[0], dtype=jnp.int32)[None, :]
    return jnp.sum(jnp.where(match, starts[None, :], 0), 1)


def bucket_onehot(buckets):
    levels = jnp.arange(BUCKETS, dtype=jnp.int32)
    return (buckets[:, :, None] == levels[None, None, :]).astype(jnp.bfloat16)


def spread_bias(table, onehot):
    return jnp.einsum(
        "qhb,qkb->hqk",
        table,
        onehot,
        precision=lax.Precision.HIGHEST,
        preferred_element_type=jnp.float32,
    )


def collect_bias(score_grad, onehot):
    return jnp.einsum(
        "hqk,qkb->qhb",
        score_grad,
        onehot,
        precision=lax.Precision.HIGHEST,
        preferred_element_type=jnp.float32,
    )


def project(rows, weight):
    return jnp.einsum("gsd,df->gsf", rows, weight, preferred_element_type=jnp.float32)


def back_project(grads, weight):
    return jnp.einsum("gsf,df->gsd", grads, weight, preferred_element_type=jnp.float32)


def weight_grad(rows, grads):
    return jnp.einsum("gsd,gsf->df", rows, grads, preferred_element_type=jnp.float32)


def gelu_back(hidden, grad_act):
    return jax.vjp(lambda value: jax.nn.gelu(value, approximate=False), hidden)[1](grad_act)[0]


def take_share(rows):
    count = rows.shape[1] // lax.axis_size("tp")
    return lax.dynamic_slice_in_dim(rows, lax.axis_index("tp") * count, count, 1)


def layout_rows(rows):
    return take_share(rows)


def reduce_rows(partial_value):
    return lax.psum_scatter(partial_value, "tp", scatter_dimension=1, tiled=True)


def spread_rows(rows_low):
    return lax.all_gather(rows_low, "tp", axis=1, tiled=True)


def norm_forward(resid, gain, shift):
    mean = jnp.mean(resid, -1, keepdims=True)
    centred = resid - mean
    inverse = lax.rsqrt(jnp.mean(centred * centred, -1, keepdims=True) + 1e-05)
    normed = centred * inverse
    return (normed * gain + shift, normed, inverse)


def close_branch(resid, partial_value, gain, shift):
    summed = reduce_rows(partial_value)
    output, normed, inverse = norm_forward(resid + summed, gain, shift)
    return (output, spread_rows(output.astype(jnp.bfloat16)), (normed, inverse))


def open_branch(grad_out, saved, gain):
    normed, inverse = saved
    grad_normed = grad_out * gain
    grad_resid = inverse * (
        grad_normed
        - jnp.mean(grad_normed, -1, keepdims=True)
        - normed * jnp.mean(grad_normed * normed, -1, keepdims=True)
    )
    gain_grad = jnp.sum(grad_out * normed, (0, 1))
    shift_grad = jnp.sum(grad_out, (0, 1))
    return (grad_resid, spread_rows(grad_resid.astype(jnp.bfloat16)), gain_grad, shift_grad)


def with_rims(pair, width):
    return with_halo(pair, (("seq", 1),), width)


def fold_window(window, rows, width, both):
    local = window[:, width : width + rows]
    from_above = passed_along(window[:, :width], "seq", -1)
    local = local.at[:, rows - width :].add(from_above)
    if both:
        from_below = passed_along(window[:, width + rows :], "seq", 1)
        local = local.at[:, :width].add(from_below)
    return local


def score_block(queries, keys, bias, allowed):
    scale = queries.shape[-1] ** (-0.5)
    raw = jnp.einsum("qhe,khe->hqk", queries, keys, preferred_element_type=jnp.float32) * scale
    if bias is not None:
        raw = raw + bias
    return jnp.where(allowed[None], raw, -1e30)


def attend_forward(queries, keys, values, bias, allowed, own_score, own_value):
    scores = score_block(queries, keys, bias, allowed)
    top = jnp.max(scores, 2)
    if own_score is not None:
        top = jnp.maximum(top, own_score)
    total = jnp.sum(jnp.exp(scores - top[:, :, None]), 2)
    if own_score is not None:
        total = total + jnp.exp(own_score - top)
    log_total = top + jnp.log(total)
    probs = jnp.exp(scores - log_total[:, :, None]).astype(jnp.bfloat16)
    result = jnp.einsum("hqk,khe->qhe", probs, values, preferred_element_type=jnp.float32)
    if own_score is not None:
        own_prob = jnp.exp(own_score - log_total).astype(jnp.bfloat16).astype(jnp.float32)
        result = result + own_prob.T[:, :, None] * own_value.astype(jnp.float32)
    return (result, log_total)


def attend_backward(
    queries,
    keys,
    values,
    bias,
    allowed,
    own_score,
    own_key,
    own_value,
    log_total,
    result,
    grad_result,
):
    scale = queries.shape[-1] ** (-0.5)
    scores = score_block(queries, keys, bias, allowed)
    probs = jnp.exp(scores - log_total[:, :, None])
    grad_wide = grad_result.astype(jnp.float32)
    delta = jnp.sum(grad_wide * result, 2).T
    grad_probs = jnp.einsum("qhe,khe->hqk", grad_result, values, preferred_element_type=jnp.float32)
    score_grad = probs * (grad_probs - delta[:, :, None])
    score_low = score_grad.astype(jnp.bfloat16)
    query_grad = (
        jnp.einsum("hqk,khe->qhe", score_low, keys, preferred_element_type=jnp.float32) * scale
    )
    key_grad = (
        jnp.einsum("hqk,qhe->khe", score_low, queries, preferred_element_type=jnp.float32) * scale
    )
    value_grad = jnp.einsum(
        "hqk,qhe->khe", probs.astype(jnp.bfloat16), grad_result, preferred_element_type=jnp.float32
    )
    if own_score is None:
        return (query_grad, key_grad, value_grad, score_grad, None, None, None)
    own_prob = jnp.exp(own_score - log_total)
    own_low = own_prob.astype(jnp.bfloat16).astype(jnp.float32)
    own_grad = own_prob * (jnp.sum(grad_wide * own_value.astype(jnp.float32), 2).T - delta)
    own_grad_low = own_grad.astype(jnp.bfloat16).astype(jnp.float32).T[:, :, None]
    query_grad = query_grad + own_grad_low * own_key.astype(jnp.float32) * scale
    own_key_grad = own_grad_low * queries.astype(jnp.float32) * scale
    own_value_grad = own_low.T[:, :, None] * grad_wide
    return (query_grad, key_grad, value_grad, score_grad, own_grad, own_key_grad, own_value_grad)


def per_device(
    enc_input,
    dec_input,
    enc_cotan,
    dec_cotan,
    doc_lengths,
    src_padding,
    enc_qkv,
    enc_wout,
    enc_gain,
    enc_bias,
    enc_up,
    enc_down,
    post_gain,
    post_bias,
    self_qkv,
    self_rel,
    self_wout,
    self_gain,
    self_bias,
    cross_wq,
    cross_wkv,
    cross_wout,
    cross_gain,
    cross_bias,
    ffn_up,
    ffn_down,
    ffn_gain,
    ffn_bias,
):
    rows = enc_input.shape[0]
    width = DOC_MAX - 1
    local_heads = enc_wout.shape[0] // HD
    streams = dec_input.shape[0]
    base = lax.axis_index("seq") * rows
    total_rows = rows * lax.axis_size("seq")
    ends = jnp.cumsum(doc_lengths)
    starts = ends - doc_lengths
    query_pos = base + jnp.arange(rows, dtype=jnp.int32)
    key_pos = base - width + jnp.arange(rows + 2 * width, dtype=jnp.int32)
    key_valid = (key_pos >= 0) & (key_pos < total_rows)
    key_doc = jnp.where(key_valid, doc_index(key_pos, ends), -1)
    key_pad = (
        lax.dynamic_slice_in_dim(jnp.pad(src_padding, (width, width)), base, rows + 2 * width) == 1
    )
    key_first = key_pos == first_of(key_pos, starts, ends)
    same_doc = doc_index(query_pos, ends)[:, None] == key_doc[None, :]
    enc_allowed = same_doc & (key_pad[None, :] | (key_pos[None, :] == query_pos[:, None]))
    cross_allowed = same_doc & (key_pad[None, :] | key_first[None, :])
    left_pos = key_pos[: width + rows]
    main_allowed = same_doc[:, : width + rows] & (left_pos[None, :] <= query_pos[:, None])
    pred_allowed = same_doc[:, : width + rows] & (left_pos[None, :] < query_pos[:, None])
    onehot = bucket_onehot(bucket_of(query_pos[:, None] - left_pos[None, :]))
    scale = HD ** (-0.5)

    def heads_of(flat):
        return flat.reshape(flat.shape[0], local_heads, HD)

    enc_rows = enc_input[None]
    enc_resid = layout_rows(enc_rows.astype(jnp.float32))
    enc_proj = jnp.einsum(
        "gsd,cdf->cgsf", enc_rows, enc_qkv, preferred_element_type=jnp.float32
    ).astype(jnp.bfloat16)
    enc_window = with_rims(enc_proj[1:, 0], width)
    enc_query = heads_of(enc_proj[0, 0])
    enc_keys = heads_of(enc_window[0])
    enc_values = heads_of(enc_window[1])
    enc_att, enc_lse = attend_forward(
        enc_query, enc_keys, enc_values, None, enc_allowed, None, None
    )
    enc_att_low = enc_att.reshape(1, rows, -1).astype(jnp.bfloat16)
    enc_resid, enc_middle, enc_saved_attn = close_branch(
        enc_resid, project(enc_att_low, enc_wout), enc_gain, enc_bias
    )
    enc_hidden = project(enc_middle, enc_up)
    enc_act = jax.nn.gelu(enc_hidden, approximate=False).astype(jnp.bfloat16)
    enc_resid, enc_final, enc_saved_ffn = close_branch(
        enc_resid, project(enc_act, enc_down), post_gain, post_bias
    )
    cross_proj = jnp.einsum(
        "sd,cdf->csf", enc_final[0], cross_wkv, preferred_element_type=jnp.float32
    ).astype(jnp.bfloat16)
    cross_window = with_rims(cross_proj, width)
    cross_keys = heads_of(cross_window[0])
    cross_values = heads_of(cross_window[1])
    dec_resid = layout_rows(dec_input.astype(jnp.float32))
    dec_proj = jnp.einsum(
        "gsd,cdf->cgsf", dec_input, self_qkv, preferred_element_type=jnp.float32
    ).astype(jnp.bfloat16)
    tables = project(dec_input, self_rel).reshape(streams, rows, local_heads, BUCKETS)
    tail = passed_along(dec_proj[1:, 0, rows - width :], "seq", 1)
    main_pair = jnp.concatenate([tail, dec_proj[1:, 0]], 1)
    main_keys = heads_of(main_pair[0])
    main_values = heads_of(main_pair[1])

    def stream_inputs(stream):
        queries = heads_of(dec_proj[0, stream])
        if stream == 0:
            return (queries, None, None, None, main_allowed)
        own_key = heads_of(dec_proj[1, stream])
        own_value = heads_of(dec_proj[2, stream])
        own_score = (
            jnp.einsum("qhe,qhe->hq", queries, own_key, preferred_element_type=jnp.float32) * scale
            + tables[stream][:, :, 0].T
        )
        return (queries, own_score, own_key, own_value, pred_allowed)

    self_att = []
    self_lse = []
    for stream in range(streams):
        queries, own_score, own_key, own_value, allowed = stream_inputs(stream)
        bias = spread_bias(tables[stream], onehot)
        result, log_total = attend_forward(
            queries, main_keys, main_values, bias, allowed, own_score, own_value
        )
        self_att.append(result)
        self_lse.append(log_total)
    self_low = jnp.stack([item.reshape(rows, -1) for item in self_att]).astype(jnp.bfloat16)
    dec_resid, dec_first, dec_saved_self = close_branch(
        dec_resid, project(self_low, self_wout), self_gain, self_bias
    )
    cross_query = project(dec_first, cross_wq).astype(jnp.bfloat16)
    cross_att = []
    cross_lse = []
    for stream in range(streams):
        result, log_total = attend_forward(
            heads_of(cross_query[stream]), cross_keys, cross_values, None, cross_allowed, None, None
        )
        cross_att.append(result)
        cross_lse.append(log_total)
    cross_low = jnp.stack([item.reshape(rows, -1) for item in cross_att]).astype(jnp.bfloat16)
    dec_resid, dec_second, dec_saved_cross = close_branch(
        dec_resid, project(cross_low, cross_wout), cross_gain, cross_bias
    )
    dec_hidden = project(dec_second, ffn_up)
    dec_act = jax.nn.gelu(dec_hidden, approximate=False).astype(jnp.bfloat16)
    dec_resid, dec_final, dec_saved_ffn = close_branch(
        dec_resid, project(dec_act, ffn_down), ffn_gain, ffn_bias
    )
    grad = layout_rows(dec_cotan.astype(jnp.float32))
    grad, grad_branch, ffn_gain_grad, ffn_bias_grad = open_branch(grad, dec_saved_ffn, ffn_gain)
    ffn_down_grad = weight_grad(dec_act, grad_branch)
    grad_act = jnp.einsum("gsd,fd->gsf", grad_branch, ffn_down, preferred_element_type=jnp.float32)
    grad_hidden = gelu_back(dec_hidden, grad_act).astype(jnp.bfloat16)
    ffn_up_grad = weight_grad(dec_second, grad_hidden)
    grad = grad + reduce_rows(back_project(grad_hidden, ffn_up))
    grad, grad_branch, cross_gain_grad, cross_bias_grad = open_branch(
        grad, dec_saved_cross, cross_gain
    )
    cross_wout_grad = weight_grad(cross_low, grad_branch)
    grad_cross_att = jnp.einsum(
        "gsd,fd->gsf", grad_branch, cross_wout, preferred_element_type=jnp.float32
    ).astype(jnp.bfloat16)
    cross_window_grad = jnp.zeros((2, rows + 2 * width, local_heads * HD), jnp.float32)
    query_grads = []
    for stream in range(streams):
        query_grad, key_grad, value_grad, _, _, _, _ = attend_backward(
            heads_of(cross_query[stream]),
            cross_keys,
            cross_values,
            None,
            cross_allowed,
            None,
            None,
            None,
            cross_lse[stream],
            cross_att[stream],
            heads_of(grad_cross_att[stream]),
        )
        query_grads.append(query_grad.reshape(rows, -1))
        cross_window_grad = cross_window_grad + jnp.stack(
            [key_grad.reshape(rows + 2 * width, -1), value_grad.reshape(rows + 2 * width, -1)]
        )
    cross_query_grad = jnp.stack(query_grads).astype(jnp.bfloat16)
    cross_wq_grad = weight_grad(dec_first, cross_query_grad)
    grad = grad + reduce_rows(back_project(cross_query_grad, cross_wq))
    cross_pair_grad = fold_window(cross_window_grad, rows, width, True).astype(jnp.bfloat16)
    cross_wkv_grad = jnp.einsum(
        "sd,csf->cdf", enc_final[0], cross_pair_grad, preferred_element_type=jnp.float32
    )
    enc_extra = jnp.einsum(
        "csf,cdf->sd", cross_pair_grad, cross_wkv, preferred_element_type=jnp.float32
    )[None]
    grad, grad_branch, self_gain_grad, self_bias_grad = open_branch(grad, dec_saved_self, self_gain)
    self_wout_grad = weight_grad(self_low, grad_branch)
    grad_self_att = jnp.einsum(
        "gsd,fd->gsf", grad_branch, self_wout, preferred_element_type=jnp.float32
    ).astype(jnp.bfloat16)
    main_window_grad = jnp.zeros((2, width + rows, local_heads * HD), jnp.float32)
    query_grads = []
    own_key_grads = []
    own_value_grads = []
    table_grads = []
    for stream in range(streams):
        queries, own_score, own_key, own_value, allowed = stream_inputs(stream)
        bias = spread_bias(tables[stream], onehot)
        query_grad, key_grad, value_grad, score_grad, own_grad, own_key_grad, own_value_grad = (
            attend_backward(
                queries,
                main_keys,
                main_values,
                bias,
                allowed,
                own_score,
                own_key,
                own_value,
                self_lse[stream],
                self_att[stream],
                heads_of(grad_self_att[stream]),
            )
        )
        table_grad = collect_bias(score_grad, onehot)
        if stream > 0:
            table_grad = table_grad.at[:, :, 0].add(own_grad.T)
            own_key_grads.append(own_key_grad.reshape(rows, -1))
            own_value_grads.append(own_value_grad.reshape(rows, -1))
        table_grads.append(table_grad.reshape(rows, -1))
        query_grads.append(query_grad.reshape(rows, -1))
        main_window_grad = main_window_grad + jnp.stack(
            [key_grad.reshape(width + rows, -1), value_grad.reshape(width + rows, -1)]
        )
    main_pair_grad = fold_window(main_window_grad, rows, width, False)
    key_grads = jnp.stack([main_pair_grad[0]] + own_key_grads)
    value_grads = jnp.stack([main_pair_grad[1]] + own_value_grads)
    proj_grad = jnp.stack([jnp.stack(query_grads), key_grads, value_grads]).astype(jnp.bfloat16)
    self_qkv_grad = jnp.einsum(
        "gsd,cgsf->cdf", dec_input, proj_grad, preferred_element_type=jnp.float32
    )
    table_low = jnp.stack(table_grads).astype(jnp.bfloat16)
    self_rel_grad = weight_grad(dec_input, table_low)
    partial_value = jnp.einsum(
        "cgsf,cdf->gsd", proj_grad, self_qkv, preferred_element_type=jnp.float32
    ) + back_project(table_low, self_rel)
    dec_grad = spread_rows((grad + reduce_rows(partial_value)).astype(jnp.bfloat16))
    grad = layout_rows(enc_cotan[None].astype(jnp.float32)) + reduce_rows(enc_extra)
    grad, grad_branch, post_gain_grad, post_bias_grad = open_branch(grad, enc_saved_ffn, post_gain)
    enc_down_grad = weight_grad(enc_act, grad_branch)
    grad_act = jnp.einsum("gsd,fd->gsf", grad_branch, enc_down, preferred_element_type=jnp.float32)
    grad_hidden = gelu_back(enc_hidden, grad_act).astype(jnp.bfloat16)
    enc_up_grad = weight_grad(enc_middle, grad_hidden)
    grad = grad + reduce_rows(back_project(grad_hidden, enc_up))
    grad, grad_branch, enc_gain_grad, enc_bias_grad = open_branch(grad, enc_saved_attn, enc_gain)
    enc_wout_grad = weight_grad(enc_att_low, grad_branch)
    grad_enc_att = jnp.einsum(
        "gsd,fd->gsf", grad_branch, enc_wout, preferred_element_type=jnp.float32
    ).astype(jnp.bfloat16)
    query_grad, key_grad, value_grad, _, _, _, _ = attend_backward(
        enc_query,
        enc_keys,
        enc_values,
        None,
        enc_allowed,
        None,
        None,
        None,
        enc_lse,
        enc_att,
        heads_of(grad_enc_att[0]),
    )
    pair_grad = fold_window(
        jnp.stack(
            [key_grad.reshape(rows + 2 * width, -1), value_grad.reshape(rows + 2 * width, -1)]
        ),
        rows,
        width,
        True,
    )
    enc_proj_grad = jnp.concatenate([query_grad.reshape(1, rows, -1), pair_grad], 0)[
        :, None
    ].astype(jnp.bfloat16)
    enc_qkv_grad = jnp.einsum(
        "gsd,cgsf->cdf", enc_rows, enc_proj_grad, preferred_element_type=jnp.float32
    )
    grad = grad + reduce_rows(
        jnp.einsum("cgsf,cdf->gsd", enc_proj_grad, enc_qkv, preferred_element_type=jnp.float32)
    )
    enc_grad = spread_rows(grad.astype(jnp.bfloat16))[0]
    (
        enc_qkv_grad,
        enc_wout_grad,
        enc_up_grad,
        enc_down_grad,
        self_qkv_grad,
        self_rel_grad,
        self_wout_grad,
        cross_wq_grad,
        cross_wkv_grad,
        cross_wout_grad,
        ffn_up_grad,
        ffn_down_grad,
    ) = lax.psum(
        (
            enc_qkv_grad,
            enc_wout_grad,
            enc_up_grad,
            enc_down_grad,
            self_qkv_grad,
            self_rel_grad,
            self_wout_grad,
            cross_wq_grad,
            cross_wkv_grad,
            cross_wout_grad,
            ffn_up_grad,
            ffn_down_grad,
        ),
        "seq",
    )
    (
        enc_gain_grad,
        enc_bias_grad,
        post_gain_grad,
        post_bias_grad,
        self_gain_grad,
        self_bias_grad,
        cross_gain_grad,
        cross_bias_grad,
        ffn_gain_grad,
        ffn_bias_grad,
    ) = lax.psum(
        (
            enc_gain_grad,
            enc_bias_grad,
            post_gain_grad,
            post_bias_grad,
            self_gain_grad,
            self_bias_grad,
            cross_gain_grad,
            cross_bias_grad,
            ffn_gain_grad,
            ffn_bias_grad,
        ),
        ("seq", "tp"),
    )
    return (
        enc_final[0],
        dec_final,
        enc_grad,
        dec_grad,
        enc_qkv_grad,
        enc_wout_grad,
        enc_gain_grad,
        enc_bias_grad,
        enc_up_grad,
        enc_down_grad,
        post_gain_grad,
        post_bias_grad,
        self_qkv_grad,
        self_rel_grad,
        self_wout_grad,
        self_gain_grad,
        self_bias_grad,
        cross_wq_grad,
        cross_wkv_grad,
        cross_wout_grad,
        cross_gain_grad,
        cross_bias_grad,
        ffn_up_grad,
        ffn_down_grad,
        ffn_gain_grad,
        ffn_bias_grad,
    )


def solution(mesh):
    in_specs = (
        P("seq", None),
        P(None, "seq", None),
        P("seq", None),
        P(None, "seq", None),
        P(),
        P(),
        P(None, None, "tp"),
        P("tp", None),
        P(),
        P(),
        P(None, "tp"),
        P("tp", None),
        P(),
        P(),
        P(None, None, "tp"),
        P(None, "tp"),
        P("tp", None),
        P(),
        P(),
        P(None, "tp"),
        P(None, None, "tp"),
        P("tp", None),
        P(),
        P(),
        P(None, "tp"),
        P("tp", None),
        P(),
        P(),
    )
    out_specs = (
        P("seq", None),
        P(None, "seq", None),
        P("seq", None),
        P(None, "seq", None),
        P(None, None, "tp"),
        P("tp", None),
        P(),
        P(),
        P(None, "tp"),
        P("tp", None),
        P(),
        P(),
        P(None, None, "tp"),
        P(None, "tp"),
        P("tp", None),
        P(),
        P(),
        P(None, "tp"),
        P(None, None, "tp"),
        P("tp", None),
        P(),
        P(),
        P(None, "tp"),
        P("tp", None),
        P(),
        P(),
    )
    return jax.shard_map(
        per_device, mesh=mesh, in_specs=in_specs, out_specs=out_specs, check_vma=False
    )
```

profile of v0, /device:TPU:0, one launch (start us, length us, event | category | flops | bytes accessed | tf_op | source)
XLA Modules:
  0.0 2464.6 jit_solution(14379923595299335802)
XLA Ops:
  44.5 23.6 fusion.3
  96.6 22.2 fusion.4
  118.9 22.4 fusion.5
  235.7 54.3 %reduce-scatter.16.cloned.1.call-done = f32[3,128,1024]{2,1,0:T(8,128)} async-done(((f32[3,512,1024]{2,1,0:T(8,128)}), f32[3,128,1024]{2,1,0:T(8,128)}) %reduce-scatter.16.cloned.1.call-update) | async-done | bytes 1572880 | tf_op jit(solution)/shard_map/reduce_scatter | solution.py:109
  430.4 58.6 %reduce-scatter.18.cloned.1.call-done = f32[3,128,1024]{2,1,0:T(8,128)} async-done(((f32[3,512,1024]{2,1,0:T(8,128)}), f32[3,128,1024]{2,1,0:T(8,128)}) %reduce-scatter.18.cloned.1.call-update) | async-done | bytes 1572880 | tf_op jit(solution)/shard_map/reduce_scatter | solution.py:109
  494.2 28.3 %all-gather.19.cloned.1.call-done = bf16[3,512,1024]{2,1,0:T(8,128)(2,1)} async-done(((bf16[3,128,1024]{2,1,0:T(8,128)(2,1)}), bf16[3,512,1024]{2,1,0:T(8,128)(2,1)}) %all-gather.19.cloned.1.call-update) | async-done | bytes 3145744 | tf_op jit(solution)/shard_map/all_gather | solution.py:113
  529.7 15.1 multiply_convert_fusion.4
  551.8 58.5 %reduce-scatter.20.cloned.1.call-done = f32[3,128,1024]{2,1,0:T(8,128)} async-done(((f32[3,512,1024]{2,1,0:T(8,128)}), f32[3,128,1024]{2,1,0:T(8,128)}) %reduce-scatter.20.cloned.1.call-update) | async-done | bytes 1572880 | tf_op jit(solution)/shard_map/reduce_scatter | solution.py:109
  616.0 28.5 %all-gather.23.cloned.1.call-done = bf16[3,512,1024]{2,1,0:T(8,128)(2,1)} async-done(((bf16[3,128,1024]{2,1,0:T(8,128)(2,1)}), bf16[3,512,1024]{2,1,0:T(8,128)(2,1)}) %all-gather.23.cloned.1.call-update) | async-done | bytes 3145744 | tf_op jit(solution)/shard_map/all_gather | solution.py:113
  663.2 58.5 %reduce-scatter.22.cloned.1.call-done = f32[3,128,1024]{2,1,0:T(8,128)} async-done(((f32[3,512,1024]{2,1,0:T(8,128)}), f32[3,128,1024]{2,1,0:T(8,128)}) %reduce-scatter.22.cloned.1.call-update) | async-done | bytes 1572880 | tf_op jit(solution)/shard_map/reduce_scatter | solution.py:109
  729.2 28.6 %all-gather.25.cloned.1.call-done = bf16[3,512,1024]{2,1,0:T(8,128)(2,1)} async-done(((bf16[3,128,1024]{2,1,0:T(8,128)(2,1)}), bf16[3,512,1024]{2,1,0:T(8,128)(2,1)}) %all-gather.25.cloned.1.call-update) | async-done | bytes 3145744 | tf_op jit(solution)/shard_map/all_gather | solution.py:113
  862.1 20.7 collective-permute-done.5
  883.4 21.7 collective-permute-done.6
  910.5 31.6 %reduce-scatter.24.cloned.1.call-done = f32[1,128,1024]{2,1,0:T(8,128)} async-done(((f32[1,512,1024]{2,1,0:T(8,128)}), f32[1,128,1024]{2,1,0:T(8,128)}) %reduce-scatter.24.cloned.1.call-update) | async-done | bytes 524304 | tf_op jit(solution)/shard_map/reduce_scatter | solution.py:109
  945.2 16.8 all-gather.27.cloned.1.call-done
  970.8 31.5 %reduce-scatter.26.cloned.1.call-done = f32[1,128,1024]{2,1,0:T(8,128)} async-done(((f32[1,512,1024]{2,1,0:T(8,128)}), f32[1,128,1024]{2,1,0:T(8,128)}) %reduce-scatter.26.cloned.1.call-update) | async-done | bytes 524304 | tf_op jit(solution)/shard_map/reduce_scatter | solution.py:109
  1028.4 55.6 %reduce-scatter.30.cloned.1.call-done = f32[3,128,1024]{2,1,0:T(8,128)} async-done(((f32[3,512,1024]{2,1,0:T(8,128)}), f32[3,128,1024]{2,1,0:T(8,128)}) %reduce-scatter.30.cloned.1.call-update) | async-done | bytes 1572880 | tf_op jit(solution)/shard_map/reduce_scatter | solution.py:109
  1117.6 25.5 %collective-permute-done.7 = f32[2,511,256]{2,0,1:T(2,128)S(1)} collective-permute-done((f32[2,511,256]{2,0,1:T(2,128)S(1)}, f32[2,511,256]{2,0,1:T(2,128)S(1)}, u32[]{:S(2)}, u32[]{:S(2)}) %collective-permute-start.7) | collective-permute-done | bytes 1046560 | tf_op jit(solution)/shard_map/ppermute | solution.py:33
  1197.4 36.8 %fusion = f32[512,4,32]{2,1,0:T(4,128)} fusion(s32[512,1023]{1,0:T(8,128)} %convert_add_fusion, f32[4,512,1023]{2,1,0:T(8,128)} %copy-done.10), kind=kOutput, calls=%fused_computation.1 | convolution fusion | flops 821280768 | bytes 10737664 | tf_op jit(solution)/shard_map/hqk,qkb->qhb/dot_general | solution.py:74
  1251.2 36.1 %fusion.1 = f32[512,4,32]{2,1,0:T(4,128)} fusion(s32[512,1023]{1,0:T(8,128)} %convert_add_fusion, f32[4,512,1023]{2,1,0:T(8,128)S(1)} %subtract_multiply_fusion.1), kind=kOutput, calls=%fused_computation.2 | convolution fusion | flops 821280768 | bytes 10737664 | tf_op jit(solution)/shard_map/hqk,qkb->qhb/dot_general | solution.py:74
  1301.6 35.5 %fusion.95 = bf16[512,4,32]{2,1,0:T(4,128)(2,1)S(1)} fusion(s32[512,1023]{1,0:T(8,128)} %convert_add_fusion, f32[4,512,1023]{2,1,0:T(8,128)} %copy-done.9), kind=kOutput, calls=%fused_computation.230 | convolution fusion | flops 821346304 | bytes 10606592 | tf_op jit(solution)/shard_map/hqk,qkb->qhb/dot_general | solution.py:74
  1374.3 59.1 %reduce-scatter.32.cloned.1.call-done = f32[3,128,1024]{2,1,0:T(8,128)} async-done(((f32[3,512,1024]{2,1,0:T(8,128)}), f32[3,128,1024]{2,1,0:T(8,128)}) %reduce-scatter.32.cloned.1.call-update) | async-done | bytes 1572880 | tf_op jit(solution)/shard_map/reduce_scatter | solution.py:109
  1477.3 40.9 %all-reduce.1 = (f32[1024]{0:T(1024)}, f32[1024]{0:T(1024)}, f32[1024]{0:T(1024)}, f32[1024]{0:T(1024)}, f32[1024]{0:T(1024)}, /*index=5*/f32[1024]{0:T(1024)}, ...) all-reduce(f32[1024]{0:T(1024)S(1)} %copy-done.176, ...), channel_id=1, replica_groups=mesh['seq'=8,'tp'=4] {'seq','tp'}, use_global_device_ids=true, to_apply=%region_61.62 | all-reduce | flops 10240 | bytes 81920 | tf_op jit(solution)/shard_map/psum | solution.py:542
  1518.3 902.9 %all-reduce.5.cloned.1.call-done = (f32[3,1024,256]{1,2,0:T(8,128)}, f32[256,1024]{1,0:T(8,128)}, f32[1024,1024]{1,0:T(8,128)}, f32[1024,1024]{1,0:T(8,128)}, f3...) async-done(((f32[3,1024,256]{1,2,0:T(8,128)}, ...) | async-done | bytes 29884432 | tf_op jit(solution)/shard_map/psum | solution.py:514
  (789 shorter events, 734.2 us)
Async XLA Ops:
  7.2 151.6 %reduce-scatter.12.cloned.1.call-start = ((), (), s32[]{:S(2)}) async-start(), calls=%async_computation.11 | async-start | bytes 2621440 | tf_op jit(solution)/shard_map/reduce_scatter | solution.py:109
  11.5 59.2 %collective-permute-start.1 = (bf16[2,511,256]{1,2,0:T(8,128)(2,1)}, bf16[2,511,256]{1,2,0:T(8,128)(2,1)}, u32[]{:S(2)}, u32[]{:S(2)}) collective-permute-start(bf16[2,511,256]{1,2,0:T(8,128)(2,1)} %get-tuple-element.387), channel_id=1, source_target_pairs={{4,0},{8,4},{12,8},{16,12},{20,16},{24,20},{28,24},{5,1},{9,5},{13... | collective-permute-start | bytes 1569800 | tf_op jit(solution)/shard_map/ppermute | solution.py:23
  24.6 120.4 %collective-permute-start.2 = (bf16[2,511,256]{1,2,0:T(8,128)(2,1)}, bf16[2,511,256]{1,2,0:T(8,128)(2,1)}, u32[]{:S(2)}, u32[]{:S(2)}) collective-permute-start(bf16[2,511,256]{1,2,0:T(8,128)(2,1)} %slice_bitcast_fusion.1), channel_id=1, source_target_pairs={{0,4},{4,8},{8,12},{12,16},{16,20},{20,24},{24,28},{1,5},{5,9},{9,... | collective-permute-start | bytes 1569800 | tf_op jit(solution)/shard_map/ppermute | solution.py:33
  89.5 89.5 %all-gather.13.cloned.1.call-start = ((), (), s32[]{:S(2)}) async-start(), calls=%async_computation.12 | async-start | bytes 1310720 | tf_op jit(solution)/shard_map/all_gather | solution.py:113
  161.8 69.9 %reduce-scatter.14.cloned.1.call-start = ((), (), s32[]{:S(2)}) async-start(), calls=%async_computation.13 | async-start | bytes 2621440 | tf_op jit(solution)/shard_map/reduce_scatter | solution.py:109
  191.0 99.0 %reduce-scatter.16.cloned.1.call-start = ((), (), s32[]{:S(2)}) async-start(), calls=%async_computation.15 | async-start | bytes 7864320 | tf_op jit(solution)/shard_map/reduce_scatter | solution.py:109
  231.6 77.2 %all-gather.15.cloned.1.call-start = ((), (), s32[]{:S(2)}) async-start(), calls=%async_computation.14 | async-start | bytes 1310720 | tf_op jit(solution)/shard_map/all_gather | solution.py:113
  235.7 119.4 %all-gather.17.cloned.1.call-start = ((), (), s32[]{:S(2)}) async-start(), calls=%async_computation.16 | async-start | bytes 3932160 | tf_op jit(solution)/shard_map/all_gather | solution.py:113
  294.2 194.8 %reduce-scatter.18.cloned.1.call-start = ((), (), s32[]{:S(2)}) async-start(), calls=%async_computation.17 | async-start | bytes 7864320 | tf_op jit(solution)/shard_map/reduce_scatter | solution.py:109
  430.3 92.2 %all-gather.19.cloned.1.call-start = ((), (), s32[]{:S(2)}) async-start(), calls=%async_computation.18 | async-start | bytes 3932160 | tf_op jit(solution)/shard_map/all_gather | solution.py:113
  493.8 116.5 %reduce-scatter.20.cloned.1.call-start = ((), (), s32[]{:S(2)}) async-start(), calls=%async_computation.19 | async-start | bytes 7864320 | tf_op jit(solution)/shard_map/reduce_scatter | solution.py:109
  551.7 92.8 %all-gather.23.cloned.1.call-start = ((), (), s32[]{:S(2)}) async-start(), calls=%async_computation.21 | async-start | bytes 3932160 | tf_op jit(solution)/shard_map/all_gather | solution.py:113
  615.8 105.8 %reduce-scatter.22.cloned.1.call-start = ((), (), s32[]{:S(2)}) async-start(), calls=%async_computation.22 | async-start | bytes 7864320 | tf_op jit(solution)/shard_map/reduce_scatter | solution.py:109
  663.1 94.7 %all-gather.25.cloned.1.call-start = ((), (), s32[]{:S(2)}) async-start(), calls=%async_computation.23 | async-start | bytes 3932160 | tf_op jit(solution)/shard_map/all_gather | solution.py:113
  729.1 213.0 %reduce-scatter.24.cloned.1.call-start = ((), (), s32[]{:S(2)}) async-start(), calls=%async_computation.24 | async-start | bytes 2621440 | tf_op jit(solution)/shard_map/reduce_scatter | solution.py:109
  1005.4 78.6 %reduce-scatter.30.cloned.1.call-start = ((), (), s32[]{:S(2)}) async-start(), calls=%async_computation.30 | async-start | bytes 7864320 | tf_op jit(solution)/shard_map/reduce_scatter | solution.py:109
  1025.5 156.5 %all-gather.33.cloned.1.call-start = ((), (), s32[]{:S(2)}) async-start(), calls=%async_computation.31 | async-start | bytes 3932160 | tf_op jit(solution)/shard_map/all_gather | solution.py:113
  1090.8 281.4 %reduce-scatter.28.cloned.1.call-start = ((), (), s32[]{:S(2)}) async-start(), calls=%async_computation.28 | async-start | bytes 2621440 | tf_op jit(solution)/shard_map/reduce_scatter | solution.py:109
  1182.0 251.5 %reduce-scatter.32.cloned.1.call-start = ((), (), s32[]{:S(2)}) async-start(), calls=%async_computation.32 | async-start | bytes 7864320 | tf_op jit(solution)/shard_map/reduce_scatter | solution.py:109
  1292.4 60.6 %collective-permute-start.9 = (f32[2,511,256]{2,0,1:T(2,128)}, f32[2,511,256]{2,0,1:T(2,128)}, u32[]{:S(2)}, u32[]{:S(2)}) collective-permute-start(f32[2,511,256]{2,0,1:T(2,128)} %copy.403), channel_id=1, source_target_pairs={{4,0},{8,4},{12,8},{16,12},{20,16},{24,20},{28,24},{5,1},{9,5},{13... | collective-permute-start | bytes 3139592 | tf_op jit(solution)/shard_map/ppermute | solution.py:33
  1371.4 105.2 %all-gather.21.cloned.1.call-start = ((), (), s32[]{:S(2)}) async-start(), calls=%async_computation.20 | async-start | bytes 3932160 | tf_op jit(solution)/shard_map/all_gather | solution.py:113
  1372.2 146.1 %all-gather.31.cloned.1.call-start = ((), (), s32[]{:S(2)}) async-start(), calls=%async_computation.29 | async-start | bytes 1310720 | tf_op jit(solution)/shard_map/all_gather | solution.py:113
  1374.3 144.0 %all-gather.35.cloned.1.call-start = ((), (), s32[]{:S(2)}) async-start(), calls=%async_computation.33 | async-start | bytes 3932160 | tf_op jit(solution)/shard_map/all_gather | solution.py:113
  1436.8 984.4 %all-reduce.5.cloned.1.call-start = ((), (), s32[]{:S(2)}) async-start(), calls=%async_computation.34 | async-start | bytes 59768832 | tf_op jit(solution)/shard_map/psum | solution.py:514
  (232 other events, 3701.6 us)
Sparse Core Ops, SparseCore 0:
  89.6 30.7 reduce-scatter.11
  161.9 16.3 all-gather.12
  191.1 31.0 reduce-scatter.13
  231.7 58.2 reduce-scatter.15
  292.0 16.7 all-gather.14
  310.8 28.5 all-gather.16
  430.4 58.5 reduce-scatter.17
  493.9 28.5 all-gather.18
  551.8 58.3 reduce-scatter.19
  615.9 28.5 all-gather.22
  663.3 58.3 reduce-scatter.21
  729.3 28.5 all-gather.24
  910.6 31.5 reduce-scatter.23
  945.2 16.7 all-gather.26
  970.9 31.4 reduce-scatter.25
  1005.5 16.7 all-gather.28
  1025.6 58.3 reduce-scatter.29
  1091.0 28.5 all-gather.32
  1182.1 31.6 reduce-scatter.27
  1371.6 61.8 reduce-scatter.31
  1435.1 28.5 all-gather.20
  1465.3 16.7 all-gather.30
  1484.3 28.6 all-gather.34
  1522.1 899.0 all-reduce.4
where the time goes:
time: 2470 us; the launch traced here: 2460 us
  waiting for transfers between devices  1530 us (62%)
  matrix products  546 us (22%)
  local copies, waits for them, and re-layouts  174 us (7%)
  other arithmetic  122 us (5%)
  blocking collectives  40.9 us (2%)
  starting transfers between devices  36 us (1%)
    psum x1, waiting for transfers between devices, per_device(): lax.psum((enc_qkv_grad, enc_wout_grad, enc_up_grad, enc_down_grad, self_q...  903 us
    reduce_scatter x11, waiting for transfers between devices, reduce_rows(): lax.psum_scatter(partial_value, 'tp', scatter_dimension=1, tiled=True)  408 us
    all_gather x12, waiting for transfers between devices, spread_rows(): return lax.all_gather(rows_low, 'tp', axis=1, tiled=True)  117 us
    dot_general x3, matrix products, collect_bias(): jnp.einsum('hqk,qkb->qhb', score_grad, onehot, precision=lax.Precision.HI...  108 us
    ppermute x6, waiting for transfers between devices, passed_along(): lax.ppermute(value, axis, [(source, source + steps) for source in range(l...  80.2 us
    dot_general x3, matrix products, spread_bias(): jnp.einsum('qhb,qkb->hqk', table, onehot, precision=lax.Precision.HIGHEST...  68.1 us
    unnamed x460, local copies, waits for them, and re-layouts  65.4 us
    dot_general x7, matrix products, score_block(): jnp.einsum('qhe,khe->hqk', queries, keys, preferred_element_type=jnp.floa...  64.7 us
  transfers between devices with their start and end apart: 34, of which 20 were waited for; matrix products, arithmetic and copies ran while one was open for 20% of the time, Pallas kernels for 0%

commit v1 on v0

v1 whole, which is shorter than its diff:
```python
import functools
import math

import jax
import jax.numpy as jnp
import numpy as np
from jax import lax
from jax.experimental import pallas as pl
from jax.experimental.pallas import tpu as pltpu
from jax.sharding import PartitionSpec as P

HD = 64
BUCKETS = 32
DOC_MAX = 512
PAIR = 2 * HD
BQ = 128
BK = 256
NEG = -1e30
VMEM_BYTES = 40 * 1024 * 1024

LOW = jnp.bfloat16
WIDE = jnp.float32


def bucket_bounds():
    exact = BUCKETS // 2
    bounds = []
    for level in range(1, BUCKETS):
        if level < exact:
            bounds.append(level)
        else:
            bounds.append(int(math.ceil(exact * (128.0 / exact) ** ((level - exact) / exact))))
    return bounds


def bucket_table(offsets):
    return sum((offsets >= bound).astype(np.int32) for bound in bucket_bounds())


def dot_nt(left, right):
    return lax.dot_general(left, right, (((1,), (1,)), ((), ())), preferred_element_type=WIDE)


def dot_nn(left, right):
    return lax.dot_general(left, right, (((1,), (0,)), ((), ())), preferred_element_type=WIDE)


def stack_heads(cells):
    lane = lax.broadcasted_iota(jnp.int32, cells.shape, 1)
    wide = cells.astype(WIDE)
    first = jnp.where(lane < HD, wide, 0.0)
    return jnp.concatenate([first, wide - first], 0)


def merge_heads(cells):
    half = cells.shape[0] // 2
    lane = lax.broadcasted_iota(jnp.int32, (half, cells.shape[1]), 1)
    return jnp.where(lane < HD, cells[:half], cells[half:])


def both_heads(mask, cells):
    return jnp.where(mask[None], cells.reshape(2, BQ, cells.shape[1]), NEG).reshape(cells.shape)


def pair_columns(cells, pair):
    return jnp.concatenate([cells[:, 2 * pair : 2 * pair + 1], cells[:, 2 * pair + 1 : 2 * pair + 2]], 0)


def put_columns(store, pair, column):
    lane = lax.broadcasted_iota(jnp.int32, store.shape, 1)
    store = jnp.where(lane == 2 * pair, column[:BQ], store)
    return jnp.where(lane == 2 * pair + 1, column[BQ:], store)


def fill_window(window, parts):
    rows = parts[0].shape[1]
    for place, part in enumerate(parts):
        window[:, place * rows : (place + 1) * rows, :] = part[...]


def full_mask(with_self, qdoc, kdoc_ref, block, query_at):
    allowed = qdoc == kdoc_ref[block]
    if with_self:
        row = lax.broadcasted_iota(jnp.int32, allowed.shape, 0) + query_at
        column = lax.broadcasted_iota(jnp.int32, allowed.shape, 1) + block * BK
        allowed = allowed | (row == column)
    return allowed


def full_forward_kernel(
    with_self,
    bounds_ref,
    q_ref,
    before_ref,
    here_ref,
    after_ref,
    qdoc_ref,
    kdoc_ref,
    att_ref,
    wide_ref,
    lse_ref,
    window,
    scores,
    top,
    total,
    gathered,
):
    stream, step = pl.program_id(0), pl.program_id(1)
    rows = here_ref.shape[1]
    pairs = here_ref.shape[2] // PAIR

    @pl.when((stream == 0) & (step == 0))
    def _():
        fill_window(window, (before_ref, here_ref, after_ref))

    low_block, high_block = bounds_ref[0, step], bounds_ref[1, step]
    qdoc = qdoc_ref[...]
    queries = [
        (stack_heads(q_ref[:, pair * PAIR : (pair + 1) * PAIR]) * HD**-0.5).astype(LOW)
        for pair in range(pairs)
    ]
    top[...] = jnp.full(top.shape, NEG, WIDE)
    total[...] = jnp.zeros(total.shape, WIDE)
    gathered[...] = jnp.zeros(gathered.shape, WIDE)

    def score_step(block, carry):
        allowed = full_mask(with_self, qdoc, kdoc_ref, block, rows + step * BQ)
        at = pl.ds(pl.multiple_of(block * BK, BK), BK)
        for pair in range(pairs):
            keys = window[0, at, pair * PAIR : (pair + 1) * PAIR]
            found = both_heads(allowed, dot_nt(queries[pair], keys))
            scores[block, pair] = found
            top[pair] = jnp.maximum(top[pair], jnp.maximum(found[:, :128], found[:, 128:]))
        return carry

    lax.fori_loop(low_block, high_block, score_step, 0)
    peaks = [jnp.max(top[pair], 1, keepdims=True) for pair in range(pairs)]

    def value_step(block, carry):
        at = pl.ds(pl.multiple_of(block * BK, BK), BK)
        for pair in range(pairs):
            values = window[1, at, pair * PAIR : (pair + 1) * PAIR]
            weights = jnp.exp(scores[block, pair] - peaks[pair])
            total[pair] += weights[:, :128] + weights[:, 128:]
            gathered[pair] += dot_nn(weights.astype(LOW), values)
        return carry

    lax.fori_loop(low_block, high_block, value_step, 0)
    lse = jnp.zeros((BQ, 128), WIDE)
    for pair in range(pairs):
        weight = jnp.sum(total[pair], 1, keepdims=True)
        result = merge_heads(gathered[pair] / weight)
        att_ref[:, pair * PAIR : (pair + 1) * PAIR] = result.astype(LOW)
        wide_ref[:, pair * PAIR : (pair + 1) * PAIR] = result
        lse = put_columns(lse, pair, peaks[pair] + jnp.log(weight))
    lse_ref[...] = lse


def full_backward_kernel(
    with_self,
    bounds_ref,
    q_ref,
    grad_ref,
    att_ref,
    lse_ref,
    before_ref,
    here_ref,
    after_ref,
    qdoc_ref,
    kdoc_ref,
    qgrad_ref,
    gbefore_ref,
    ghere_ref,
    gafter_ref,
    window,
    wgrad,
    qgrad,
):
    stream, step = pl.program_id(0), pl.program_id(1)
    rows = here_ref.shape[1]
    pairs = here_ref.shape[2] // PAIR

    @pl.when((stream == 0) & (step == 0))
    def _():
        fill_window(window, (before_ref, here_ref, after_ref))
        wgrad[...] = jnp.zeros(wgrad.shape, WIDE)

    low_block, high_block = bounds_ref[0, step], bounds_ref[1, step]
    qdoc = qdoc_ref[...]
    lse_all = lse_ref[...]
    queries, grads, queries_t, grads_t, deltas, logs = [], [], [], [], [], []
    for pair in range(pairs):
        cut = slice(pair * PAIR, (pair + 1) * PAIR)
        query = stack_heads(q_ref[:, cut]) * HD**-0.5
        grad = stack_heads(grad_ref[:, cut])
        att = att_ref[:, cut]
        deltas.append(jnp.sum(grad * jnp.concatenate([att, att], 0), 1, keepdims=True))
        logs.append(pair_columns(lse_all, pair))
        queries.append(query.astype(LOW))
        grads.append(grad.astype(LOW))
        queries_t.append(query.T.astype(LOW))
        grads_t.append(grad.T.astype(LOW))
    qgrad[...] = jnp.zeros(qgrad.shape, WIDE)

    def block_step(block, carry):
        allowed = full_mask(with_self, qdoc, kdoc_ref, block, rows + step * BQ)
        at = pl.ds(pl.multiple_of(block * BK, BK), BK)
        for pair in range(pairs):
            cut = slice(pair * PAIR, (pair + 1) * PAIR)
            keys = window[0, at, cut]
            values = window[1, at, cut]
            probs = jnp.exp(both_heads(allowed, dot_nt(queries[pair], keys)) - logs[pair])
            slopes = probs * (dot_nt(grads[pair], values) - deltas[pair])
            slopes = slopes.astype(LOW)
            qgrad[pair] += dot_nn(slopes, keys)
            wgrad[0, cut, at] += dot_nn(queries_t[pair], slopes)
            wgrad[1, cut, at] += dot_nn(grads_t[pair], probs.astype(LOW))
        return carry

    lax.fori_loop(low_block, high_block, block_step, 0)
    for pair in range(pairs):
        qgrad_ref[:, pair * PAIR : (pair + 1) * PAIR] = (
            merge_heads(qgrad[pair]) * HD**-0.5
        ).astype(LOW)

    @pl.when((stream == pl.num_programs(0) - 1) & (step == pl.num_programs(1) - 1))
    def _():
        gbefore_ref[...] = wgrad[:, :, :rows].astype(LOW)
        ghere_ref[...] = wgrad[:, :, rows : 2 * rows]
        gafter_ref[...] = wgrad[:, :, 2 * rows :].astype(LOW)


def causal_parts(own, table, gidx, pair):
    lane = lax.broadcasted_iota(jnp.int32, (BQ, 128), 1)
    row = lax.broadcasted_iota(jnp.int32, (BQ, 128), 0)
    near, far = [], []
    for head in (2 * pair, 2 * pair + 1):
        spread = jnp.take_along_axis(
            table, gidx + head * BUCKETS, axis=1, mode="promise_in_bounds"
        )
        last = table[:, head * BUCKETS + BUCKETS - 1 : head * BUCKETS + BUCKETS]
        near.append((jnp.where(lane > row, spread, last), spread))
        far.append(last)
    bias_before = jnp.concatenate([near[0][0], near[1][0]], 0)
    bias_here = jnp.concatenate([near[0][1], near[1][1]], 0)
    return bias_before, bias_here, jnp.concatenate(far, 0)


def own_column(table, pair):
    first, second = 2 * pair * BUCKETS, (2 * pair + 1) * BUCKETS
    return jnp.concatenate([table[:, first : first + 1], table[:, second : second + 1]], 0)


def causal_masks(own, qdoc, kdoc_ref, near):
    lane = lax.broadcasted_iota(jnp.int32, (BQ, 128), 1)
    row = lax.broadcasted_iota(jnp.int32, (BQ, 128), 0)
    earlier = (lane < row) if own else (lane <= row)
    return qdoc == kdoc_ref[near - 1], (qdoc == kdoc_ref[near]) & earlier


def causal_forward_kernel(own, *refs):
    bounds_ref, q_ref, before_ref, here_ref, qdoc_ref, kdoc_ref, table_ref, gidx_ref = refs[:8]
    refs = refs[8:]
    if own:
        own_ref, refs = refs[0], refs[1:]
    att_ref, wide_ref, lse_ref, window, scores, top, total, gathered = refs
    stream, step = pl.program_id(0), pl.program_id(1)
    rows = here_ref.shape[1]
    pairs = here_ref.shape[2] // PAIR

    @pl.when((stream == 0) & (step == 0))
    def _():
        fill_window(window, (before_ref, here_ref))

    near = rows // 128 + step
    low_block = bounds_ref[step]
    qdoc = qdoc_ref[...]
    table = table_ref[...]
    gidx = gidx_ref[...]
    queries, fars, peaks, owns = [], [], [], []
    mask_before, mask_here = causal_masks(own, qdoc, kdoc_ref, near)
    near_at = pl.ds(pl.multiple_of((near - 1) * 128, 128), 256)
    for pair in range(pairs):
        cut = slice(pair * PAIR, (pair + 1) * PAIR)
        query = stack_heads(q_ref[:, cut]) * HD**-0.5
        queries.append(query.astype(LOW))
        bias_before, bias_here, far = causal_parts(own, table, gidx, pair)
        fars.append(far)
        found = dot_nt(queries[pair], window[0, near_at, cut])
        found_before = both_heads(mask_before, found[:, :128] + bias_before)
        found_here = both_heads(mask_here, found[:, 128:] + bias_here)
        scores[near - 1, pair] = found_before
        scores[near, pair] = found_here
        top[pair] = jnp.maximum(found_before, found_here)
        if own:
            keys = own_ref[0, :, cut].astype(WIDE)
            owns.append(
                jnp.sum(query * jnp.concatenate([keys, keys], 0), 1, keepdims=True)
                + own_column(table, pair)
            )

    def score_step(block, carry):
        allowed = qdoc == kdoc_ref[block]
        at = pl.ds(pl.multiple_of(block * 128, 128), 128)
        for pair in range(pairs):
            keys = window[0, at, pair * PAIR : (pair + 1) * PAIR]
            found = both_heads(allowed, dot_nt(queries[pair], keys) + fars[pair])
            scores[block, pair] = found
            top[pair] = jnp.maximum(top[pair], found)
        return carry

    lax.fori_loop(low_block, near - 1, score_step, 0)
    for pair in range(pairs):
        cut = slice(pair * PAIR, (pair + 1) * PAIR)
        peak = jnp.max(top[pair], 1, keepdims=True)
        if own:
            peak = jnp.maximum(peak, owns[pair])
        peaks.append(peak)
        weights_before = jnp.exp(scores[near - 1, pair] - peak)
        weights_here = jnp.exp(scores[near, pair] - peak)
        total[pair] = weights_before + weights_here
        weights = jnp.concatenate([weights_before, weights_here], 1).astype(LOW)
        gathered[pair] = dot_nn(weights, window[1, near_at, cut])

    def value_step(block, carry):
        at = pl.ds(pl.multiple_of(block * 128, 128), 128)
        for pair in range(pairs):
            values = window[1, at, pair * PAIR : (pair + 1) * PAIR]
            weights = jnp.exp(scores[block, pair] - peaks[pair])
            total[pair] += weights
            gathered[pair] += dot_nn(weights.astype(LOW), values)
        return carry

    lax.fori_loop(low_block, near - 1, value_step, 0)
    lse = jnp.zeros((BQ, 128), WIDE)
    for pair in range(pairs):
        cut = slice(pair * PAIR, (pair + 1) * PAIR)
        weight = jnp.sum(total[pair], 1, keepdims=True)
        result = gathered[pair]
        if own:
            own_weight = jnp.exp(owns[pair] - peaks[pair])
            weight = weight + own_weight
            values = own_ref[1, :, cut].astype(WIDE)
            result = result + own_weight * jnp.concatenate([values, values], 0)
        result = merge_heads(result / weight)
        att_ref[:, cut] = result.astype(LOW)
        wide_ref[:, cut] = result
        lse = put_columns(lse, pair, peaks[pair] + jnp.log(weight))
    lse_ref[...] = lse


def causal_backward_kernel(own, *refs):
    bounds_ref, q_ref, grad_ref, att_ref, lse_ref, before_ref, here_ref = refs[:7]
    qdoc_ref, kdoc_ref, table_ref, gidx_ref, sidx_ref, hot_ref = refs[7:13]
    refs = refs[13:]
    if own:
        own_ref, refs = refs[0], refs[1:]
    qgrad_ref, tgrad_ref, gbefore_ref, ghere_ref = refs[:4]
    refs = refs[4:]
    if own:
        ograd_ref, refs = refs[0], refs[1:]
    window, wgrad, qgrad, farsum = refs
    stream, step = pl.program_id(0), pl.program_id(1)
    rows = here_ref.shape[1]
    pairs = here_ref.shape[2] // PAIR

    @pl.when((stream == 0) & (step == 0))
    def _():
        fill_window(window, (before_ref, here_ref))
        wgrad[...] = jnp.zeros(wgrad.shape, WIDE)

    near = rows // 128 + step
    low_block = bounds_ref[step]
    qdoc = qdoc_ref[...]
    table = table_ref[...]
    gidx = gidx_ref[...]
    sidx = sidx_ref[...]
    lse_all = lse_ref[...]
    lane = lax.broadcasted_iota(jnp.int32, (BQ, 128), 1)
    row = lax.broadcasted_iota(jnp.int32, (BQ, 128), 0)
    mask_before, mask_here = causal_masks(own, qdoc, kdoc_ref, near)
    near_at = pl.ds(pl.multiple_of((near - 1) * 128, 128), 256)
    queries, grads, queries_t, grads_t, deltas, logs, fars = [], [], [], [], [], [], []
    tgrad = jnp.zeros((BQ, 128), WIDE)
    for pair in range(pairs):
        cut = slice(pair * PAIR, (pair + 1) * PAIR)
        query = stack_heads(q_ref[:, cut]) * HD**-0.5
        grad = stack_heads(grad_ref[:, cut])
        att = att_ref[:, cut]
        delta = jnp.sum(grad * jnp.concatenate([att, att], 0), 1, keepdims=True)
        log_total = pair_columns(lse_all, pair)
        deltas.append(delta)
        logs.append(log_total)
        queries.append(query.astype(LOW))
        grads.append(grad.astype(LOW))
        queries_t.append(query.T.astype(LOW))
        grads_t.append(grad.T.astype(LOW))
        bias_before, bias_here, far = causal_parts(own, table, gidx, pair)
        fars.append(far)
        keys = window[0, near_at, cut]
        values = window[1, near_at, cut]
        found = dot_nt(queries[pair], keys)
        found_before = both_heads(mask_before, found[:, :128] + bias_before)
        found_here = both_heads(mask_here, found[:, 128:] + bias_here)
        probs = jnp.exp(jnp.concatenate([found_before, found_here], 1) - log_total)
        slopes = probs * (dot_nt(grads[pair], values) - delta)
        slopes_low = slopes.astype(LOW)
        qgrad[pair] = dot_nn(slopes_low, keys)
        wgrad[0, cut, near_at] += dot_nn(queries_t[pair], slopes_low)
        wgrad[1, cut, near_at] += dot_nn(grads_t[pair], probs.astype(LOW))
        rest = []
        for side in range(2):
            part_before = slopes[side * BQ : (side + 1) * BQ, :128]
            part_here = slopes[side * BQ : (side + 1) * BQ, 128:]
            merged = jnp.where(lane <= row, part_here, part_before)
            skewed = jnp.take_along_axis(merged, sidx, axis=1, mode="promise_in_bounds")
            tgrad = tgrad + dot_nn(skewed.astype(LOW), hot_ref[2 * pair + side])
            rest.append(jnp.where(lane <= row, part_before, 0.0))
        farsum[pair] = jnp.concatenate(rest, 0)
        if own:
            own_keys = own_ref[0, :, cut].astype(WIDE)
            own_values = own_ref[1, :, cut].astype(WIDE)
            own_keys = jnp.concatenate([own_keys, own_keys], 0)
            own_values = jnp.concatenate([own_values, own_values], 0)
            own_score = jnp.sum(query * own_keys, 1, keepdims=True) + own_column(table, pair)
            own_prob = jnp.exp(own_score - log_total)
            own_slope = own_prob * (jnp.sum(grad * own_values, 1, keepdims=True) - delta)
            qgrad[pair] += own_slope * own_keys
            key_part = own_slope * query
            value_part = own_prob * grad
            ograd_ref[0, :, cut] = (key_part[:BQ] + key_part[BQ:]).astype(LOW)
            ograd_ref[1, :, cut] = (value_part[:BQ] + value_part[BQ:]).astype(LOW)
            for side in range(2):
                place = (2 * pair + side) * BUCKETS
                tgrad = tgrad + jnp.where(lane == place, own_slope[side * BQ : (side + 1) * BQ], 0.0)

    def block_step(block, carry):
        allowed = qdoc == kdoc_ref[block]
        at = pl.ds(pl.multiple_of(block * 128, 128), 128)
        for pair in range(pairs):
            cut = slice(pair * PAIR, (pair + 1) * PAIR)
            keys = window[0, at, cut]
            values = window[1, at, cut]
            found = both_heads(allowed, dot_nt(queries[pair], keys) + fars[pair])
            probs = jnp.exp(found - logs[pair])
            slopes = probs * (dot_nt(grads[pair], values) - deltas[pair])
            farsum[pair] += slopes
            slopes = slopes.astype(LOW)
            qgrad[pair] += dot_nn(slopes, keys)
            wgrad[0, cut, at] += dot_nn(queries_t[pair], slopes)
            wgrad[1, cut, at] += dot_nn(grads_t[pair], probs.astype(LOW))
        return carry

    lax.fori_loop(low_block, near - 1, block_step, 0)
    for pair in range(pairs):
        qgrad_ref[:, pair * PAIR : (pair + 1) * PAIR] = (
            merge_heads(qgrad[pair]) * HD**-0.5
        ).astype(LOW)
        rest = jnp.sum(farsum[pair], 1, keepdims=True)
        for side in range(2):
            place = (2 * pair + side) * BUCKETS + BUCKETS - 1
            tgrad = tgrad + jnp.where(lane == place, rest[side * BQ : (side + 1) * BQ], 0.0)
    tgrad_ref[...] = tgrad.astype(LOW)

    @pl.when((stream == pl.num_programs(0) - 1) & (step == pl.num_programs(1) - 1))
    def _():
        gbefore_ref[...] = wgrad[:, :, :rows].astype(LOW)
        ghere_ref[...] = wgrad[:, :, rows:]


def whole_spec(shape):
    return pl.BlockSpec(shape, lambda stream, step, bounds: (0,) * len(shape))


def rows_spec(width):
    return pl.BlockSpec((None, BQ, width), lambda stream, step, bounds: (stream, step, 0))


def pair_rows_spec(width):
    return pl.BlockSpec((None, 2, BQ, width), lambda stream, step, bounds: (stream, 0, step, 0))


QDOC_SPEC = pl.BlockSpec((BQ, 1), lambda stream, step, bounds: (step, 0))


def shaped(shape, dtype):
    return jax.ShapeDtypeStruct(shape, dtype)


def local_call(kernel, grid, in_specs, out_specs, out_shape, scratch, cost):
    return pl.pallas_call(
        kernel,
        grid_spec=pltpu.PrefetchScalarGridSpec(
            num_scalar_prefetch=1,
            grid=grid,
            in_specs=in_specs,
            out_specs=out_specs,
            scratch_shapes=scratch,
        ),
        out_shape=out_shape,
        compiler_params=pltpu.CompilerParams(
            vmem_limit_bytes=VMEM_BYTES, dimension_semantics=("arbitrary", "arbitrary")
        ),
        cost_estimate=pl.CostEstimate(
            flops=int(cost), bytes_accessed=4 * 1024 * 1024, transcendentals=0
        ),
    )


def full_forward(with_self, bounds, queries, before, here, after, qdoc, kdoc):
    streams, rows, width = queries.shape
    pairs = width // PAIR
    blocks = 3 * rows // BK
    kv_spec = whole_spec((2, rows, width))
    return local_call(
        functools.partial(full_forward_kernel, with_self),
        (streams, rows // BQ),
        [rows_spec(width), kv_spec, kv_spec, kv_spec, QDOC_SPEC, whole_spec((blocks, 1, BK))],
        [rows_spec(width), rows_spec(width), rows_spec(128)],
        [
            shaped((streams, rows, width), LOW),
            shaped((streams, rows, width), WIDE),
            shaped((streams, rows, 128), WIDE),
        ],
        [
            pltpu.VMEM((2, 3 * rows, width), LOW),
            pltpu.VMEM((blocks, pairs, 2 * BQ, BK), WIDE),
            pltpu.VMEM((pairs, 2 * BQ, 128), WIDE),
            pltpu.VMEM((pairs, 2 * BQ, 128), WIDE),
            pltpu.VMEM((pairs, 2 * BQ, 128), WIDE),
        ],
        streams * 4e9,
    )(bounds, queries, before, here, after, qdoc, kdoc)


def full_backward(with_self, bounds, queries, grads, att, lse, before, here, after, qdoc, kdoc):
    streams, rows, width = queries.shape
    pairs = width // PAIR
    blocks = 3 * rows // BK
    kv_spec = whole_spec((2, rows, width))
    grad_spec = whole_spec((2, width, rows))
    return local_call(
        functools.partial(full_backward_kernel, with_self),
        (streams, rows // BQ),
        [rows_spec(width)] * 3
        + [rows_spec(128), kv_spec, kv_spec, kv_spec, QDOC_SPEC, whole_spec((blocks, 1, BK))],
        [rows_spec(width), grad_spec, grad_spec, grad_spec],
        [
            shaped((streams, rows, width), LOW),
            shaped((2, width, rows), LOW),
            shaped((2, width, rows), WIDE),
            shaped((2, width, rows), LOW),
        ],
        [
            pltpu.VMEM((2, 3 * rows, width), LOW),
            pltpu.VMEM((2, width, 3 * rows), WIDE),
            pltpu.VMEM((pairs, 2 * BQ, 128), WIDE),
        ],
        streams * 8e9,
    )(bounds, queries, grads, att, lse, before, here, after, qdoc, kdoc)


def spread_index():
    row, lane = np.arange(BQ)[:, None], np.arange(128)[None, :]
    return bucket_table((row - lane) % 128).astype(np.int32)


def skew_index():
    row, lane = np.arange(BQ)[:, None], np.arange(128)[None, :]
    return ((row - lane) % 128).astype(np.int32)


def bucket_hot(heads):
    offsets = np.arange(128)
    hot = np.zeros((heads, 128, 128), np.float32)
    for head in range(heads):
        hot[head, offsets, head * BUCKETS + bucket_table(offsets)] = 1.0
    return hot


def causal_forward(own, bounds, queries, before, here, qdoc, kdoc, tables, own_pair):
    streams, rows, width = queries.shape
    pairs = width // PAIR
    blocks = 2 * rows // 128
    kv_spec = whole_spec((2, rows, width))
    specs = [rows_spec(width), kv_spec, kv_spec, QDOC_SPEC, whole_spec((blocks, 1, 128))]
    specs += [rows_spec(128), whole_spec((BQ, 128))]
    operands = [bounds, queries, before, here, qdoc, kdoc, tables, jnp.asarray(spread_index())]
    if own:
        specs.append(pair_rows_spec(width))
        operands.append(own_pair)
    return local_call(
        functools.partial(causal_forward_kernel, own),
        (streams, rows // BQ),
        specs,
        [rows_spec(width), rows_spec(width), rows_spec(128)],
        [
            shaped((streams, rows, width), LOW),
            shaped((streams, rows, width), WIDE),
            shaped((streams, rows, 128), WIDE),
        ],
        [
            pltpu.VMEM((2, 2 * rows, width), LOW),
            pltpu.VMEM((blocks, pairs, 2 * BQ, 128), WIDE),
            pltpu.VMEM((pairs, 2 * BQ, 128), WIDE),
            pltpu.VMEM((pairs, 2 * BQ, 128), WIDE),
            pltpu.VMEM((pairs, 2 * BQ, 128), WIDE),
        ],
        streams * 4e9,
    )(*operands)


def causal_backward(
    own, bounds, queries, grads, att, lse, before, here, qdoc, kdoc, tables, own_pair
):
    streams, rows, width = queries.shape
    pairs = width // PAIR
    blocks = 2 * rows // 128
    kv_spec = whole_spec((2, rows, width))
    grad_spec = whole_spec((2, width, rows))
    specs = [rows_spec(width)] * 3 + [rows_spec(128), kv_spec, kv_spec, QDOC_SPEC]
    specs += [whole_spec((blocks, 1, 128)), rows_spec(128), whole_spec((BQ, 128))]
    specs += [whole_spec((BQ, 128)), whole_spec((2 * pairs, 128, 128))]
    operands = [bounds, queries, grads, att, lse, before, here, qdoc, kdoc, tables]
    operands += [jnp.asarray(spread_index()), jnp.asarray(skew_index())]
    operands += [jnp.asarray(bucket_hot(2 * pairs), LOW)]
    out_specs = [rows_spec(width), rows_spec(128), grad_spec, grad_spec]
    out_shape = [
        shaped((streams, rows, width), LOW),
        shaped((streams, rows, 128), LOW),
        shaped((2, width, rows), LOW),
        shaped((2, width, rows), WIDE),
    ]
    if own:
        specs.append(pair_rows_spec(width))
        operands.append(own_pair)
        out_specs.append(pair_rows_spec(width))
        out_shape.append(shaped((streams, 2, rows, width), LOW))
    return local_call(
        functools.partial(causal_backward_kernel, own),
        (streams, rows // BQ),
        specs,
        out_specs,
        out_shape,
        [
            pltpu.VMEM((2, 2 * rows, width), LOW),
            pltpu.VMEM((2, width, 2 * rows), WIDE),
            pltpu.VMEM((pairs, 2 * BQ, 128), WIDE),
            pltpu.VMEM((pairs, 2 * BQ, 128), WIDE),
        ],
        streams * 8e9,
    )(*operands)


def swap_core(value):
    count = lax.axis_size("tp")
    return lax.ppermute(value, "tp", [(place, place ^ 1) for place in range(count)])


def sum_chips(value):
    count = lax.axis_size("tp")
    hop = 2
    while hop < count:
        low = value.astype(LOW)
        value = low.astype(WIDE) + lax.ppermute(
            low, "tp", [(place, place ^ hop) for place in range(count)]
        ).astype(WIDE)
        hop *= 2
    return value


def core_index():
    return lax.rem(lax.axis_index("tp"), 2)


def half_rows(rows, mine):
    half = rows.shape[1] // 2
    core = core_index() if mine else 1 - core_index()
    return lax.dynamic_slice_in_dim(rows, core * half, half, 1)


def natural_rows(mine, other):
    first = core_index() == 0
    return jnp.concatenate([jnp.where(first, mine, other), jnp.where(first, other, mine)], 1)


def project(rows, weight):
    return jnp.einsum("gsd,df->gsf", rows, weight, preferred_element_type=WIDE)


def back_project(grads, weight):
    return jnp.einsum("gsf,df->gsd", grads, weight, preferred_element_type=WIDE)


def weight_grad(rows, grads):
    return jnp.einsum("gsd,gsf->df", rows, grads, preferred_element_type=WIDE)


def summed_rows(mine, other):
    return sum_chips(mine + swap_core(other.astype(LOW)).astype(WIDE))


def norm_forward(resid, gain, shift):
    mean = jnp.mean(resid, -1, keepdims=True)
    centred = resid - mean
    inverse = lax.rsqrt(jnp.mean(centred * centred, -1, keepdims=True) + 1e-05)
    normed = centred * inverse
    return (normed * gain + shift, normed, inverse)


def close_branch(resid, mine, other, gain, shift):
    output, normed, inverse = norm_forward(resid + summed_rows(mine, other), gain, shift)
    low = output.astype(LOW)
    return (output, low, swap_core(low), (normed, inverse))


def open_branch(grad_out, saved, gain):
    normed, inverse = saved
    grad_normed = grad_out * gain
    grad_resid = inverse * (
        grad_normed
        - jnp.mean(grad_normed, -1, keepdims=True)
        - normed * jnp.mean(grad_normed * normed, -1, keepdims=True)
    )
    low = grad_resid.astype(LOW)
    sums = jnp.stack([jnp.sum(grad_out * normed, (0, 1)), jnp.sum(grad_out, (0, 1))])
    return (grad_resid, low, swap_core(low), sums)


def gelu_both(hidden):
    scaled = hidden * (0.5**0.5)
    half = 0.5 * lax.erf(scaled) + 0.5
    slope = half + hidden * jnp.exp(-(scaled * scaled)) * ((2.0 * math.pi) ** -0.5)
    return ((hidden * half).astype(LOW), slope.astype(LOW))


def passed_along(value, steps):
    count = lax.axis_size("seq")
    if steps > 0:
        pairs = [(place, place + 1) for place in range(count - 1)]
    else:
        pairs = [(place + 1, place) for place in range(count - 1)]
    return lax.ppermute(value, "seq", pairs)


def doc_index(positions, ends):
    return jnp.sum((positions[:, None] >= ends[None, :]).astype(jnp.int32), 1)


def pick(owner, values):
    match = owner[:, None] == jnp.arange(values.shape[0], dtype=jnp.int32)[None, :]
    return jnp.sum(jnp.where(match, values[None, :], 0), 1)


def sum_seq(values, earlier):
    low = tuple(value.astype(LOW) for value in values)
    if earlier is not None:
        low, earlier = lax.optimization_barrier((low, earlier))
    return lax.psum(low, "seq")


def pad_tables(tables):
    missing = 128 - tables.shape[-1]
    return jnp.pad(tables, ((0, 0), (0, 0), (0, missing))) if missing else tables


def per_device(
    enc_input,
    dec_input,
    enc_cotan,
    dec_cotan,
    doc_lengths,
    src_padding,
    enc_qkv,
    enc_wout,
    enc_gain,
    enc_bias,
    enc_up,
    enc_down,
    post_gain,
    post_bias,
    self_qkv,
    self_rel,
    self_wout,
    self_gain,
    self_bias,
    cross_wq,
    cross_wkv,
    cross_wout,
    cross_gain,
    cross_bias,
    ffn_up,
    ffn_down,
    ffn_gain,
    ffn_bias,
):
    rows = enc_input.shape[0]
    half = rows // 2
    streams = dec_input.shape[0]
    table_width = self_rel.shape[1]
    base = lax.axis_index("seq") * rows
    total_rows = rows * lax.axis_size("seq")
    ends = jnp.cumsum(doc_lengths)
    starts = ends - doc_lengths
    key_pos = base - rows + jnp.arange(3 * rows, dtype=jnp.int32)
    key_valid = (key_pos >= 0) & (key_pos < total_rows)
    key_owner = doc_index(key_pos, ends)
    key_doc = jnp.where(key_valid, key_owner, -1)
    key_pad = (
        lax.dynamic_slice_in_dim(jnp.pad(src_padding, (rows, rows)), base, 3 * rows) == 1
    )
    key_first = key_pos == pick(key_owner, starts)
    qdoc = key_doc[rows : 2 * rows][:, None]
    enc_kdoc = jnp.where(key_pad, key_doc, -1).reshape(-1, 1, BK)
    cross_kdoc = jnp.where(key_pad | key_first, key_doc, -1).reshape(-1, 1, BK)
    self_kdoc = key_doc[: 2 * rows].reshape(-1, 1, 128)
    owners = key_owner[rows : 2 * rows]
    block_first = pick(owners[::BQ], starts) - base + rows
    block_end = pick(owners[BQ - 1 :: BQ], ends) - base + rows
    full_bounds = jnp.stack([block_first // BK, (block_end + BK - 1) // BK])
    self_bounds = block_first // 128

    enc_rows = enc_input[None]
    enc_proj = jnp.einsum("sd,cdf->csf", enc_input, enc_qkv, preferred_element_type=WIDE).astype(LOW)
    enc_pair = enc_proj[1:]
    enc_query = enc_proj[:1]
    enc_before = passed_along(enc_pair, 1)
    enc_after = passed_along(enc_pair, -1)
    dec_proj = [
        jnp.einsum("sd,cdf->csf", dec_input[stream], self_qkv, preferred_element_type=WIDE).astype(LOW)
        for stream in range(streams)
    ]
    main_pair = dec_proj[0][1:]
    main_before = passed_along(main_pair, 1)
    tables = pad_tables(project(dec_input, self_rel))

    enc_att, enc_wide, enc_lse = full_forward(
        True, full_bounds, enc_query, enc_before, enc_pair, enc_after, qdoc, enc_kdoc
    )
    enc_resid, enc_mine, enc_other, enc_saved_attn = close_branch(
        half_rows(enc_rows, True).astype(WIDE),
        project(half_rows(enc_att, True), enc_wout),
        project(half_rows(enc_att, False), enc_wout),
        enc_gain,
        enc_bias,
    )
    enc_middle = jnp.concatenate([enc_mine, enc_other], 1)
    enc_act, enc_slope = gelu_both(project(enc_middle, enc_up))

    self_att, self_wide, self_lse = [], [], []
    for stream in range(streams):
        own = stream > 0
        att, wide, lse = causal_forward(
            own,
            self_bounds,
            dec_proj[stream][:1],
            main_before,
            main_pair,
            qdoc,
            self_kdoc,
            tables[stream : stream + 1],
            dec_proj[stream][1:][None] if own else None,
        )
        self_att.append(att)
        self_wide.append(wide)
        self_lse.append(lse)

    enc_resid, enc_mine, enc_other, enc_saved_ffn = close_branch(
        enc_resid,
        project(enc_act[:, :half], enc_down),
        project(enc_act[:, half:], enc_down),
        post_gain,
        post_bias,
    )
    enc_final = natural_rows(enc_mine, enc_other)
    cross_pair = jnp.einsum(
        "sd,cdf->csf", enc_final[0], cross_wkv, preferred_element_type=WIDE
    ).astype(LOW)
    cross_before = passed_along(cross_pair, 1)
    cross_after = passed_along(cross_pair, -1)

    groups = [(stream, stream + 1) for stream in range(streams)]
    first_saved, first_rows, first_resid = [], [], []
    for stream in range(streams):
        resid, mine, other, saved = close_branch(
            half_rows(dec_input[stream][None], True).astype(WIDE),
            project(half_rows(self_att[stream], True), self_wout),
            project(half_rows(self_att[stream], False), self_wout),
            self_gain,
            self_bias,
        )
        first_resid.append(resid)
        first_saved.append(saved)
        first_rows.append((mine, other))
    cross_query, cross_att, cross_wide, cross_lse = [], [], [], []
    for stream in range(streams):
        mine, other = first_rows[stream]
        query = natural_rows(
            project(mine, cross_wq).astype(LOW), project(other, cross_wq).astype(LOW)
        )
        att, wide, lse = full_forward(
            False, full_bounds, query, cross_before, cross_pair, cross_after, qdoc, cross_kdoc
        )
        cross_query.append(query)
        cross_att.append(att)
        cross_wide.append(wide)
        cross_lse.append(lse)
    second_saved, second_rows, second_resid = [], [], []
    for stream in range(streams):
        resid, mine, other, saved = close_branch(
            first_resid[stream],
            project(half_rows(cross_att[stream], True), cross_wout),
            project(half_rows(cross_att[stream], False), cross_wout),
            cross_gain,
            cross_bias,
        )
        second_resid.append(resid)
        second_saved.append(saved)
        second_rows.append(jnp.concatenate([mine, other], 1))
    dec_act, dec_slope = [], []
    dec_final, grad, ffn_grad_rows, ffn_sums = [], [], [], []
    for stream in range(streams):
        act, slope = gelu_both(project(second_rows[stream], ffn_up))
        dec_act.append(act)
        dec_slope.append(slope)
        resid, mine, other, saved = close_branch(
            second_resid[stream],
            project(act[:, :half], ffn_down),
            project(act[:, half:], ffn_down),
            ffn_gain,
            ffn_bias,
        )
        dec_final.append(natural_rows(mine, other))
        grad_out = half_rows(dec_cotan[stream][None], True).astype(WIDE)
        resid_grad, mine, other, sums = open_branch(grad_out, saved, ffn_gain)
        grad.append(resid_grad)
        ffn_grad_rows.append(jnp.concatenate([mine, other], 1))
        ffn_sums.append(sums)
    dec_final = jnp.concatenate(dec_final, 0)

    cross_sums, cross_grad_rows, hidden_grads = [], [], []
    for stream in range(streams):
        grad_act = jnp.einsum(
            "gsd,fd->gsf", ffn_grad_rows[stream], ffn_down, preferred_element_type=WIDE
        )
        hidden_grad = (grad_act * dec_slope[stream].astype(WIDE)).astype(LOW)
        hidden_grads.append(hidden_grad)
        grad[stream] = grad[stream] + summed_rows(
            back_project(hidden_grad[:, :half], ffn_up), back_project(hidden_grad[:, half:], ffn_up)
        )
        resid_grad, mine, other, sums = open_branch(grad[stream], second_saved[stream], cross_gain)
        grad[stream] = resid_grad
        cross_grad_rows.append((mine, other))
        cross_sums.append(sums)
    ffn_down_grad = weight_grad(jnp.concatenate(dec_act), jnp.concatenate(ffn_grad_rows))
    ffn_up_grad = weight_grad(jnp.concatenate(second_rows), jnp.concatenate(hidden_grads))
    ffn_sum = sum_seq([ffn_down_grad, ffn_up_grad], None)

    def att_grad(mine, other, weight):
        return natural_rows(
            jnp.einsum("gsd,fd->gsf", mine, weight, preferred_element_type=WIDE).astype(LOW),
            jnp.einsum("gsd,fd->gsf", other, weight, preferred_element_type=WIDE).astype(LOW),
        )

    def att_weight_grad(atts, grads):
        lefts, rights = [], []
        for att, (mine, other) in zip(atts, grads):
            lefts += [half_rows(att, True), half_rows(att, False)]
            rights += [mine, other]
        return weight_grad(jnp.concatenate(lefts, 1), jnp.concatenate(rights, 1))

    cross_query_grads, cross_parts = [], []
    for stream in range(streams):
        cross_att_grad = att_grad(*cross_grad_rows[stream], cross_wout)
        query_grad, *parts = full_backward(
            False,
            full_bounds,
            cross_query[stream],
            cross_att_grad,
            cross_wide[stream],
            cross_lse[stream],
            cross_before,
            cross_pair,
            cross_after,
            qdoc,
            cross_kdoc,
        )
        cross_query_grads.append(query_grad)
        cross_parts.append(parts)

    def fold_pair(parts, after):
        to_before = sum(part[0].astype(WIDE) for part in parts).astype(LOW)
        here = sum(part[1] for part in parts) + passed_along(to_before, -1).astype(WIDE)
        if after:
            to_after = sum(part[2].astype(WIDE) for part in parts).astype(LOW)
            here = here + passed_along(to_after, 1).astype(WIDE)
        return here.astype(LOW)

    cross_pair_grad = fold_pair(cross_parts, True)
    enc_extra = jnp.einsum("cfs,cdf->sd", cross_pair_grad, cross_wkv, preferred_element_type=WIDE)[None]
    enc_grad = half_rows(enc_cotan[None], True).astype(WIDE) + summed_rows(
        half_rows(enc_extra, True), half_rows(enc_extra, False)
    )
    enc_grad, mine, other, post_sums = open_branch(enc_grad, enc_saved_ffn, post_gain)
    enc_ffn_rows = jnp.concatenate([mine, other], 1)

    self_sums, self_grad_rows = [], []
    for stream in range(streams):
        query_grad = cross_query_grads[stream]
        grad[stream] = grad[stream] + summed_rows(
            back_project(half_rows(query_grad, True), cross_wq),
            back_project(half_rows(query_grad, False), cross_wq),
        )
        resid_grad, mine, other, sums = open_branch(grad[stream], first_saved[stream], self_gain)
        grad[stream] = resid_grad
        self_grad_rows.append((mine, other))
        self_sums.append(sums)
    cross_wout_grad = att_weight_grad(cross_att, cross_grad_rows)
    cross_wq_grad = att_weight_grad(cross_query_grads, first_rows).T
    cross_wkv_grad = jnp.einsum("sd,cfs->cdf", enc_final[0], cross_pair_grad, preferred_element_type=WIDE)
    cross_sum = sum_seq([cross_wout_grad, cross_wq_grad, cross_wkv_grad], ffn_sum)

    grad_act = jnp.einsum("gsd,fd->gsf", enc_ffn_rows, enc_down, preferred_element_type=WIDE)
    hidden_grad = (grad_act * enc_slope.astype(WIDE)).astype(LOW)
    enc_grad = enc_grad + summed_rows(
        back_project(hidden_grad[:, :half], enc_up), back_project(hidden_grad[:, half:], enc_up)
    )
    enc_sum = sum_seq(
        [weight_grad(enc_act, enc_ffn_rows), weight_grad(enc_middle, hidden_grad)], cross_sum
    )
    enc_grad, mine, other, enc_sums = open_branch(enc_grad, enc_saved_attn, enc_gain)
    enc_grad_rows = (mine, other)

    self_proj_grads, self_parts, table_grads = [], [], []
    for stream in range(streams):
        own = stream > 0
        self_att_grad = att_grad(*self_grad_rows[stream], self_wout)
        query_grad, table_grad, *parts = causal_backward(
            own,
            self_bounds,
            dec_proj[stream][:1],
            self_att_grad,
            self_wide[stream],
            self_lse[stream],
            main_before,
            main_pair,
            qdoc,
            self_kdoc,
            tables[stream : stream + 1],
            dec_proj[stream][1:][None] if own else None,
        )
        self_parts.append(parts[:2])
        table_grads.append(table_grad[:, :, :table_width])
        own_grad = parts[2][0] if own else None
        self_proj_grads.append([query_grad, own_grad])
    main_grad = fold_pair(self_parts, False)
    main_grad = jnp.swapaxes(main_grad, 1, 2)
    dec_grad = []
    full_proj_grads = []
    for stream in range(streams):
        query_grad, own_grad = self_proj_grads[stream]
        pair_grad = main_grad if stream == 0 else own_grad
        proj_grad = jnp.concatenate([query_grad, pair_grad], 0)
        full_proj_grads.append(proj_grad)
        partial_value = (
            jnp.einsum("csf,cdf->sd", proj_grad, self_qkv, preferred_element_type=WIDE)[None]
            + back_project(table_grads[stream], self_rel)
        )
        total = grad[stream] + summed_rows(
            half_rows(partial_value, True), half_rows(partial_value, False)
        )
        low = total.astype(LOW)
        dec_grad.append(natural_rows(low, swap_core(low)))
    dec_grad = jnp.concatenate(dec_grad, 0)
    self_qkv_grad = jnp.einsum(
        "gsd,gcsf->cdf", dec_input, jnp.stack(full_proj_grads), preferred_element_type=WIDE
    )
    self_rel_grad = weight_grad(dec_input, jnp.concatenate(table_grads, 0))
    self_wout_grad = att_weight_grad(self_att, self_grad_rows)

    enc_att_grad = att_grad(*enc_grad_rows, enc_wout)
    query_grad, *parts = full_backward(
        True,
        full_bounds,
        enc_query,
        enc_att_grad,
        enc_wide,
        enc_lse,
        enc_before,
        enc_pair,
        enc_after,
        qdoc,
        enc_kdoc,
    )
    pair_grad = jnp.swapaxes(fold_pair([parts], True), 1, 2)
    enc_proj_grad = jnp.concatenate([query_grad, pair_grad], 0)
    enc_qkv_grad = jnp.einsum("sd,csf->cdf", enc_input, enc_proj_grad, preferred_element_type=WIDE)
    partial_value = jnp.einsum(
        "csf,cdf->sd", enc_proj_grad, enc_qkv, preferred_element_type=WIDE
    )[None]
    enc_grad = enc_grad + summed_rows(
        half_rows(partial_value, True), half_rows(partial_value, False)
    )
    low = enc_grad.astype(LOW)
    enc_grad = natural_rows(low, swap_core(low))[0]
    enc_wout_grad = att_weight_grad([enc_att], [enc_grad_rows])

    sums = jnp.concatenate(
        [enc_sums, post_sums, sum(self_sums), sum(cross_sums), sum(ffn_sums)], 0
    )
    sums = sums + swap_core(sums)
    last_sum = sum_seq(
        [self_qkv_grad, self_rel_grad, self_wout_grad, enc_qkv_grad, enc_wout_grad, sums], enc_sum
    )
    ffn_down_grad, ffn_up_grad = [value.astype(WIDE) for value in ffn_sum]
    cross_wout_grad, cross_wq_grad, cross_wkv_grad = [value.astype(WIDE) for value in cross_sum]
    enc_down_grad, enc_up_grad = [value.astype(WIDE) for value in enc_sum]
    self_qkv_grad, self_rel_grad, self_wout_grad, enc_qkv_grad, enc_wout_grad, sums = [
        value.astype(WIDE) for value in last_sum
    ]
    return (
        enc_final[0],
        dec_final,
        enc_grad,
        dec_grad,
        enc_qkv_grad,
        enc_wout_grad,
        sums[0],
        sums[1],
        enc_up_grad,
        enc_down_grad,
        sums[2],
        sums[3],
        self_qkv_grad,
        self_rel_grad,
        self_wout_grad,
        sums[4],
        sums[5],
        cross_wq_grad,
        cross_wkv_grad,
        cross_wout_grad,
        sums[6],
        sums[7],
        ffn_up_grad,
        ffn_down_grad,
        sums[8],
        sums[9],
    )


def solution(mesh):
    in_specs = (
        P("seq", None),
        P(None, "seq", None),
        P("seq", None),
        P(None, "seq", None),
        P(),
        P(),
        P(None, None, "tp"),
        P("tp", None),
        P(),
        P(),
        P(None, "tp"),
        P("tp", None),
        P(),
        P(),
        P(None, None, "tp"),
        P(None, "tp"),
        P("tp", None),
        P(),
        P(),
        P(None, "tp"),
        P(None, None, "tp"),
        P("tp", None),
        P(),
        P(),
        P(None, "tp"),
        P("tp", None),
        P(),
        P(),
    )
    out_specs = (
        P("seq", None),
        P(None, "seq", None),
        P("seq", None),
        P(None, "seq", None),
        P(None, None, "tp"),
        P("tp", None),
        P(),
        P(),
        P(None, "tp"),
        P("tp", None),
        P(),
        P(),
        P(None, None, "tp"),
        P(None, "tp"),
        P("tp", None),
        P(),
        P(),
        P(None, "tp"),
        P(None, None, "tp"),
        P("tp", None),
        P(),
        P(),
        P(None, "tp"),
        P("tp", None),
        P(),
        P(),
    )
    return jax.shard_map(
        per_device, mesh=mesh, in_specs=in_specs, out_specs=out_specs, check_vma=False
    )
```

time: 2470 us -> 1000 us (0.40)
  waiting for transfers between devices: 1530 us -> 483 us
  matrix products: 546 us -> 117 us
  Pallas kernels: 0 us -> 125 us
  local copies, waits for them, and re-layouts: 174 us -> 60.3 us
  other arithmetic: 122 us -> 84.5 us
  starting transfers between devices: 36 us -> 73.3 us
    psum x1 -> x4, waiting for transfers between devices: 903 us -> 255 us  [sum_seq(): return lax.psum(low, 'seq')]
    dot_general x83 -> x89, matrix products: 543 us -> 116 us  [the longest x9 25.8 us: weight_grad(): return jnp.einsum('gsd,gsf->df', rows, grads, preferred_element_type=WIDE)]
    reduce_scatter x11 -> x0, waiting for transfers between devices: 408 us -> none  [reduce_rows(): lax.psum_scatter(partial_value, 'tp', scatter_dimension=1, tiled=True)]
    ppermute x10 -> x83, waiting for transfers between devices: 101 us -> 228 us  [the longest x23 165 us: sum_chips(): lax.ppermute(low, 'tp', [(place, place ^ hop) for place in range(count)])]
    pallas_call x0 -> x14, Pallas kernels: none -> 125 us  [the longest x4 36.3 us: full_forward(): local_call(functools.partial(full_forward_kernel, with_self), (streams, r...]
    all_gather x12 -> x0, waiting for transfers between devices: 117 us -> none  [spread_rows(): return lax.all_gather(rows_low, 'tp', axis=1, tiled=True)]
    another operation x22 -> x1, local copies, waits for them, and re-layouts: 43.2 us -> 0.08 us  [the longest x8 33.9 us: per_device(): jnp.stack([key_grad.reshape(rows + 2 * width, -1), value_grad.reshape(row...]
    ppermute x10 -> x83, starting transfers between devices: 34 us -> 72.3 us  [the longest x10 36.3 us: passed_along(): return lax.ppermute(value, 'seq', pairs)]
  transfers between devices with their start and end apart: 34 -> 87, of which waited for: 20 -> 32; matrix products, arithmetic and copies ran while one was open for 20% -> 22% of each run, Pallas kernels for 0% -> 12%
where the time goes in v1:
time: 1000 us; the launch traced here: 997 us
  waiting for transfers between devices  483 us (48%)
  Pallas kernels  125 us (12%)
  matrix products  117 us (12%)
  other arithmetic  84.5 us (8%)
  starting transfers between devices  73.3 us (7%)
  local copies, waits for them, and re-layouts  60.3 us (6%)
  blocking collectives  35.4 us (4%)
  between operations  18 us (2%)
    psum x4, waiting for transfers between devices, sum_seq(): return lax.psum(low, 'seq')  255 us
    ppermute x23, waiting for transfers between devices, sum_chips(): lax.ppermute(low, 'tp', [(place, place ^ hop) for place in range(count)])  165 us
    ppermute x10, waiting for transfers between devices, passed_along(): return lax.ppermute(value, 'seq', pairs)  56.2 us
    ppermute x10, starting transfers between devices, passed_along(): return lax.ppermute(value, 'seq', pairs)  36.3 us
    pallas_call x4, Pallas kernels, full_forward(): local_call(functools.partial(full_forward_kernel, with_self), (streams, r...  36.3 us
    pallas_call x4, Pallas kernels, full_backward(): local_call(functools.partial(full_backward_kernel, with_self), (streams,...  36 us
    psum x1, blocking collectives, sum_seq(): return lax.psum(low, 'seq')  35.4 us
    unnamed x463, local copies, waits for them, and re-layouts  34.1 us
  transfers between devices with their start and end apart: 87, of which 32 were waited for; matrix products, arithmetic and copies ran while one was open for 22% of the time, Pallas kernels for 12%

profile of v1, /device:TPU:0, one launch (start us, length us, event | category | flops | bytes accessed | tf_op | source)
XLA Modules:
  0.0 997.0 jit_solution(15275465997621425405)
XLA Ops:
  89.3 20.7 %collective-permute-done.10 = bf16[1,256,1024]{2,1,0:T(8,128)(2,1)S(1)} collective-permute-done((bf16[1,256,1024]{2,1,0:T(8,128)(2,1)S(1)}, bf16[1,256,1024]{2,1,0:T(8,128)(2,1)S(1)}, u32[]{:S(2)}, u32[]{:S(2)}) %collective-permute-start.10) | collective-permute-done | bytes 524320 | tf_op jit(solution)/shard_map/ppermute | solution.py:665
  111.5 9.8 collective-permute-done.21
  121.6 10.5 %collective-permute-done.3 = bf16[1,256,1024]{2,1,0:T(8,128)(2,1)S(1)} collective-permute-done((bf16[1,256,1024]{2,1,0:T(8,128)(2,1)S(1)}, bf16[1,256,1024]{2,1,0:T(8,128)(2,1)S(1)}, u32[]{:S(2)}, u32[]{:S(2)}) %collective-permute-start.3) | collective-permute-done | bytes 524320 | tf_op jit(solution)/shard_map/ppermute | solution.py:665
  143.5 11.7 %collective-permute-done.6 = bf16[1,256,1024]{2,1,0:T(8,128)(2,1)S(1)} collective-permute-done((bf16[1,256,1024]{2,1,0:T(8,128)(2,1)S(1)}, bf16[1,256,1024]{2,1,0:T(8,128)(2,1)S(1)}, u32[]{:S(2)}, u32[]{:S(2)}) %collective-permute-start.6) | collective-permute-done | bytes 524320 | tf_op jit(solution)/shard_map/ppermute | solution.py:665
  165.2 20.7 %collective-permute-done.12.before_ref = bf16[2,512,256]{2,1,0:T(8,128)(2,1)S(1)} collective-permute-done((bf16[2,512,256]{2,1,0:T(8,128)(2,1)S(1)}, bf16[2,512,256]{2,1,0:T(8,128)(2,1)S(1)}, u32[]{:S(2)}, u32[]{:S(2)}) %collective-permute-start.12) | collective-permute-done | bytes 524320 | tf_op jit(solution)/shard_map/ppermute | solution.py:743
  201.2 15.3 %shard_map.577 = (bf16[1,512,256]{2,1,0:T(8,128)(2,1)S(1)}, f32[1,512,256]{2,1,0:T(8,128)S(1)}, f32[1,512,128]{2,1,0:T(8,128)S(1)}) custom-call(s32[2,4]{1,0:T(2,128)S(1)} %pad_add_fusion.bounds_ref, bf16[1,512,256]{2,1,0:T(8,128)(2,1)S(1)} %pad_maximum_fusion.12.q_ref, bf16[2,512,256]{2,1,0:T(8,128)(2,1)S(1)} %collective-permute-done.12.before_ref, ...), custom_call_target="tpu_custom_call" | custom-call | flops 4000000000 | bytes 4194304 | tf_op jit(solution)/shard_map/pallas_call | solution.py:515
  221.6 10.4 %collective-permute-done.33 = bf16[1,256,1024]{2,1,0:T(8,128)(2,1)S(1)} collective-permute-done((bf16[1,256,1024]{2,1,0:T(8,128)(2,1)S(1)}, bf16[1,256,1024]{2,1,0:T(8,128)(2,1)S(1)}, u32[]{:S(2)}, u32[]{:S(2)}) %collective-permute-start.33) | collective-permute-done | bytes 524320 | tf_op jit(solution)/shard_map/ppermute | solution.py:665
  232.0 11.2 %collective-permute-done.24 = bf16[1,256,1024]{2,1,0:T(8,128)(2,1)S(1)} collective-permute-done((bf16[1,256,1024]{2,1,0:T(8,128)(2,1)S(1)}, bf16[1,256,1024]{2,1,0:T(8,128)(2,1)S(1)}, u32[]{:S(2)}, u32[]{:S(2)}) %collective-permute-start.24) | collective-permute-done | bytes 524320 | tf_op jit(solution)/shard_map/ppermute | solution.py:665
  243.2 10.8 %collective-permute-done.15 = bf16[1,256,1024]{2,1,0:T(8,128)(2,1)S(1)} collective-permute-done((bf16[1,256,1024]{2,1,0:T(8,128)(2,1)S(1)}, bf16[1,256,1024]{2,1,0:T(8,128)(2,1)S(1)}, u32[]{:S(2)}, u32[]{:S(2)}) %collective-permute-start.15) | collective-permute-done | bytes 524320 | tf_op jit(solution)/shard_map/ppermute | solution.py:665
  266.0 12.2 %collective-permute-done.18 = bf16[1,256,1024]{2,1,0:T(8,128)(2,1)S(1)} collective-permute-done((bf16[1,256,1024]{2,1,0:T(8,128)(2,1)S(1)}, bf16[1,256,1024]{2,1,0:T(8,128)(2,1)S(1)}, u32[]{:S(2)}, u32[]{:S(2)}) %collective-permute-start.18) | collective-permute-done | bytes 524320 | tf_op jit(solution)/shard_map/ppermute | solution.py:665
  291.3 11.7 %collective-permute-done.36 = bf16[1,256,1024]{2,1,0:T(8,128)(2,1)S(1)} collective-permute-done((bf16[1,256,1024]{2,1,0:T(8,128)(2,1)S(1)}, bf16[1,256,1024]{2,1,0:T(8,128)(2,1)S(1)}, u32[]{:S(2)}, u32[]{:S(2)}) %collective-permute-start.36) | collective-permute-done | bytes 524320 | tf_op jit(solution)/shard_map/ppermute | solution.py:665
  302.9 10.4 %collective-permute-done.27 = bf16[1,256,1024]{2,1,0:T(8,128)(2,1)S(1)} collective-permute-done((bf16[1,256,1024]{2,1,0:T(8,128)(2,1)S(1)}, bf16[1,256,1024]{2,1,0:T(8,128)(2,1)S(1)}, u32[]{:S(2)}, u32[]{:S(2)}) %collective-permute-start.27) | collective-permute-done | bytes 524320 | tf_op jit(solution)/shard_map/ppermute | solution.py:665
  363.4 9.0 collective-permute-done.44
  373.8 9.3 collective-permute-done.48
  441.7 20.1 %collective-permute-done.51 = bf16[2,256,512]{2,1,0:T(8,128)(2,1)S(1)} collective-permute-done((bf16[2,256,512]{2,1,0:T(8,128)(2,1)S(1)}, bf16[2,256,512]{2,1,0:T(8,128)(2,1)S(1)}, u32[]{:S(2)}, u32[]{:S(2)}) %collective-permute-start.51) | collective-permute-done | bytes 524320 | tf_op jit(solution)/shard_map/ppermute | solution.py:743
  492.2 39.3 %all-reduce.16.cloned.1.call-done = (bf16[1024,1024]{1,0:T(8,128)(2,1)}, bf16[1024,1024]{1,0:T(8,128)(2,1)}) async-done(((bf16[1024,1024]{1,0:T(8,128)(2,1)}, bf16[1024,1024]{1,0:T(8,128)(2,1)}), (bf16[1024,1024]{1,0:T(8,128)(2,1)}, bf16[1024,1024]{1,0:T(8,128)(2,1)})) %all-reduce.16.cloned.1.call-update) | async-done | bytes 4194320 | tf_op jit(solution)/shard_map/psum | solution.py:759
  549.8 10.4 %shard_map.587 = (bf16[1,512,256]{2,1,0:T(8,128)(2,1)S(1)}, bf16[1,512,128]{2,1,0:T(8,128)(2,1)S(1)}, bf16[2,256,512]{2,1,0:T(8,128)(2,1)S(1)}, f32[2,256,512]{2,1,0:T(8,128)S(1)}, bf16[1,2,512,256]{3,2,1,0:T(8,128)(2,1)S(1)}) custom-call(s32[4]{0:T(128)S(1)} %copy-done.51, bf16[1,512,256]{2,1,0:T(8,128)(2,1)S(1)} %copy-done.15, ...), custom_call_target="tpu_custom_call" | custom-call | flops 8000000000 | bytes 4194304 | tf_op jit(solution)/shard_map/pallas_call | solution.py:639
  579.0 10.4 %shard_map.588 = (bf16[1,512,256]{2,1,0:T(8,128)(2,1)S(1)}, bf16[1,512,128]{2,1,0:T(8,128)(2,1)S(1)}, bf16[2,256,512]{2,1,0:T(8,128)(2,1)S(1)}, f32[2,256,512]{2,1,0:T(8,128)S(1)}, bf16[1,2,512,256]{3,2,1,0:T(8,128)(2,1)S(1)}) custom-call(s32[4]{0:T(128)S(1)} %copy-done.51, bf16[1,512,256]{2,1,0:T(8,128)(2,1)S(1)} %copy-done.13, ...), custom_call_target="tpu_custom_call" | custom-call | flops 8000000000 | bytes 4194304 | tf_op jit(solution)/shard_map/pallas_call | solution.py:639
  625.1 17.0 %all-reduce.14.cloned.1.call-done = (bf16[256,1024]{1,0:T(8,128)(2,1)}, bf16[1024,256]{1,0:T(8,128)(2,1)}, bf16[2,1024,256]{1,2,0:T(8,128)(2,1)}) async-done(((bf16[256,1024]{1,0:T(8,128)(2,1)}, bf16[1024,256]{1,0:T(8,128)(2,1)}, bf16[2,1024,256]{1,2,0:T(8,128)(2,1)}), (bf16[256,1024]{1,0:T(8,128)(2,1)}, bf16[1024,256]{1,0:T(8,128)(2,1)}, bf16[2,1024,256]{1,2,0:T(8,128)(2,1)})) %all-reduce.14.cloned.1.call-update) | async-done | bytes 2097168 | tf_op jit(solution)/shard_map/psum | solution.py:759
  655.8 10.5 %shard_map.585 = (bf16[1,512,256]{2,1,0:T(8,128)(2,1)S(1)}, bf16[2,256,512]{2,1,0:T(8,128)(2,1)}, f32[2,256,512]{2,1,0:T(8,128)S(1)}, bf16[2,256,512]{2,1,0:T(8,128)(2,1)S(1)}) custom-call(s32[2,4]{1,0:T(2,128)S(1)} %pad_add_fusion.bounds_ref, bf16[1,512,256]{2,1,0:T(8,128)(2,1)S(1)} %slice.205.q_ref, bf16[1,512,256]{2,1,0:T(8,128)(2,1)S(1)} %pad_maximum_fusion.18.grad_ref, ...), custom_call_target="tpu_custom_call" | custom-call | flops 8000000000 | bytes 4194304 | tf_op jit(solution)/shard_map/pallas_call | solution.py:542
  693.3 119.4 %all-reduce.12.cloned.1.call-done = (bf16[1024,1024]{1,0:T(8,128)(2,1)}, bf16[1024,1024]{1,0:T(8,128)(2,1)}) async-done(((bf16[1024,1024]{1,0:T(8,128)(2,1)}, bf16[1024,1024]{1,0:T(8,128)(2,1)}), (bf16[1024,1024]{1,0:T(8,128)(2,1)}, bf16[1024,1024]{1,0:T(8,128)(2,1)})) %all-reduce.12.cloned.1.call-update) | async-done | bytes 4194320 | tf_op jit(solution)/shard_map/psum | solution.py:759
  823.5 10.5 %collective-permute-done.80 = bf16[1,256,1024]{2,1,0:T(8,128)(2,1)S(1)} collective-permute-done((bf16[1,256,1024]{2,1,0:T(8,128)(2,1)S(1)}, bf16[1,256,1024]{2,1,0:T(8,128)(2,1)S(1)}, u32[]{:S(2)}, u32[]{:S(2)}) %collective-permute-start.80) | collective-permute-done | bytes 524320 | tf_op jit(solution)/shard_map/ppermute | solution.py:665
  865.3 35.4 %psum.100 = bf16[10,1024]{1,0:T(8,128)(2,1)S(1)} all-reduce(bf16[10,1024]{1,0:T(8,128)(2,1)S(1)} %add_convert_fusion.26), channel_id=1, replica_groups=mesh['seq'=8,'tp'=4] {'seq'}, use_global_device_ids=true, to_apply=%region_80.81 | all-reduce | flops 10240 | bytes 40960 | tf_op jit(solution)/shard_map/psum | solution.py:759
  901.4 79.4 %all-reduce.10.cloned.1.call-done = (bf16[3,1024,256]{1,2,0:T(8,128)(2,1)}, bf16[3,1024,256]{1,2,0:T(8,128)(2,1)}, bf16[1024,128]{0,1:T(8,128)(2,1)}, bf16[256,1024]{1,0:T(8,128)(2,1)}, bf16[256,1024]{1,0:T(8,128)(2,1)}) async-done(((bf16[3,1024,256]{1,2,0:T(8,128)(2,1)}, bf16[3,1024,256]{1,2,0:T(8,128)(2,1)}, bf16[1024,128]{0,1:T(8,128)(2,1)}, bf16[256,1024]{1,0:T(8,128)(2,1)}, ...) | async-done | bytes 4456464 | tf_op jit(solution)/shard_map/psum | solution.py:759
  (919 shorter events, 452.9 us)
Async XLA Ops:
  7.2 524.3 %all-reduce.16.cloned.1.call-start = ((), (), s32[]{:S(2)}) async-start(), calls=%async_computation.3 | async-start | bytes 8388608 | tf_op jit(solution)/shard_map/psum | solution.py:759
  11.0 63.7 %collective-permute-start = (bf16[2,512,256]{2,1,0:T(8,128)(2,1)S(1)}, bf16[2,512,256]{2,1,0:T(8,128)(2,1)}, u32[]{:S(2)}, u32[]{:S(2)}) collective-permute-start(bf16[2,512,256]{2,1,0:T(8,128)(2,1)S(1)} %slice.206.here_ref), channel_id=1, source_target_pairs={{0,4},{4,8},{8,12},{12,16},{16,20},{20,24},{24,28},{1,5},{5,9},{9,... | collective-permute-start | bytes 1572872 | tf_op jit(solution)/shard_map/ppermute | solution.py:743
  16.8 58.4 %collective-permute-start.1 = (bf16[2,512,256]{2,1,0:T(8,128)(2,1)S(1)}, bf16[2,512,256]{2,1,0:T(8,128)(2,1)}, u32[]{:S(2)}, u32[]{:S(2)}) collective-permute-start(bf16[2,512,256]{2,1,0:T(8,128)(2,1)S(1)} %slice.206.here_ref), channel_id=1, source_target_pairs={{4,0},{8,4},{12,8},{16,12},{20,16},{24,20},{28,24},{5,1},{9,5},{13... | collective-permute-start | bytes 1572872 | tf_op jit(solution)/shard_map/ppermute | solution.py:743
  21.2 28.4 %collective-permute-start.8 = (bf16[2,512,256]{2,1,0:T(8,128)(2,1)S(1)}, bf16[2,512,256]{2,1,0:T(8,128)(2,1)}, u32[]{:S(2)}, u32[]{:S(2)}) collective-permute-start(bf16[2,512,256]{2,1,0:T(8,128)(2,1)S(1)} %slice.211.refs_3_.refs_6_), channel_id=1, source_target_pairs={{0,4},{4,8},{8,12},{12,16},{16,20},{20,24},{24,28},{1,5},{5,9},{9,... | collective-permute-start | bytes 1572872 | tf_op jit(solution)/shard_map/ppermute | solution.py:743
  86.9 34.4 %collective-permute-start.21 = (bf16[1,256,1024]{2,1,0:T(8,128)(2,1)S(1)}, bf16[1,256,1024]{2,1,0:T(8,128)(2,1)S(1)}, u32[]{:S(2)}, u32[]{:S(2)}) collective-permute-start(bf16[1,256,1024]{2,1,0:T(8,128)(2,1)S(1)} %fusion.98), channel_id=1, source_target_pairs={{0,2},{1,3},{2,0},{3,1},{4,6},{5,7},{6,4},{7,5},{8,10},{9,11},{10,... | collective-permute-start | bytes 1572872 | tf_op jit(solution)/shard_map/ppermute | solution.py:665
  88.8 43.3 %collective-permute-start.3 = (bf16[1,256,1024]{2,1,0:T(8,128)(2,1)S(1)}, bf16[1,256,1024]{2,1,0:T(8,128)(2,1)S(1)}, u32[]{:S(2)}, u32[]{:S(2)}) collective-permute-start(bf16[1,256,1024]{2,1,0:T(8,128)(2,1)S(1)} %fusion.101), channel_id=1, source_target_pairs={{0,2},{1,3},{2,0},{3,1},{4,6},{5,7},{6,4},{7,5},{8,10},{9,11},{10,... | collective-permute-start | bytes 1572872 | tf_op jit(solution)/shard_map/ppermute | solution.py:665
  220.0 34.0 %collective-permute-start.15 = (bf16[1,256,1024]{2,1,0:T(8,128)(2,1)S(1)}, bf16[1,256,1024]{2,1,0:T(8,128)(2,1)S(1)}, u32[]{:S(2)}, u32[]{:S(2)}) collective-permute-start(bf16[1,256,1024]{2,1,0:T(8,128)(2,1)S(1)} %fusion.99), channel_id=1, source_target_pairs={{0,2},{1,3},{2,0},{3,1},{4,6},{5,7},{6,4},{7,5},{8,10},{9,11},{10,... | collective-permute-start | bytes 1572872 | tf_op jit(solution)/shard_map/ppermute | solution.py:665
  342.8 299.2 %all-reduce.14.cloned.1.call-start = ((), (), s32[]{:S(2)}) async-start(), calls=%async_computation.2 | async-start | bytes 4194304 | tf_op jit(solution)/shard_map/psum | solution.py:759
  352.5 30.6 %collective-permute-start.48 = (bf16[1,256,1024]{2,1,0:T(8,128)(2,1)S(1)}, bf16[1,256,1024]{2,1,0:T(8,128)(2,1)S(1)}, u32[]{:S(2)}, u32[]{:S(2)}) collective-permute-start(bf16[1,256,1024]{2,1,0:T(8,128)(2,1)S(1)} %add_convert_fusion.15), channel_id=1, source_target_pairs={{0,2},{1,3},{2,0},{3,1},{4,6},{5,7},{6,4},{7,5},{8,10},{9,11},{10,... | collective-permute-start | bytes 1572872 | tf_op jit(solution)/shard_map/ppermute | solution.py:665
  362.9 33.9 %collective-permute-start.19 = (bf16[1,256,1024]{2,1,0:T(8,128)(2,1)S(1)}, bf16[1,256,1024]{2,1,0:T(8,128)(2,1)S(1)}, u32[]{:S(2)}, u32[]{:S(2)}) collective-permute-start(bf16[1,256,1024]{2,1,0:T(8,128)(2,1)S(1)} %get-tuple-element.353), channel_id=1, source_target_pairs={{0,1},{1,0},{2,3},{3,2},{4,5},{5,4},{6,7},{7,6},{8,9},{9,8},{10,11... | collective-permute-start | bytes 1572872 | tf_op jit(solution)/shard_map/ppermute | solution.py:657
  423.5 38.3 %collective-permute-start.51 = (bf16[2,256,512]{2,1,0:T(8,128)(2,1)S(1)}, bf16[2,256,512]{2,1,0:T(8,128)(2,1)S(1)}, u32[]{:S(2)}, u32[]{:S(2)}) collective-permute-start(bf16[2,256,512]{2,1,0:T(8,128)(2,1)S(1)} %add_convert_fusion.13), channel_id=1, source_target_pairs={{0,4},{4,8},{8,12},{12,16},{16,20},{20,24},{24,28},{1,5},{5,9},{9,... | collective-permute-start | bytes 1572872 | tf_op jit(solution)/shard_map/ppermute | solution.py:743
  433.6 53.0 %collective-permute-start.67 = (bf16[1,256,1024]{2,1,0:T(8,128)(2,1)}, bf16[1,256,1024]{2,1,0:T(8,128)(2,1)}, u32[]{:S(2)}, u32[]{:S(2)}) collective-permute-start(bf16[1,256,1024]{2,1,0:T(8,128)(2,1)} %fusion.93), channel_id=1, source_target_pairs={{0,2},{1,3},{2,0},{3,1},{4,6},{5,7},{6,4},{7,5},{8,10},{9,11},{10,... | collective-permute-start | bytes 1572872 | tf_op jit(solution)/shard_map/ppermute | solution.py:665
  434.4 30.4 %collective-permute-start.69 = (bf16[1,256,1024]{2,1,0:T(8,128)(2,1)S(1)}, bf16[1,256,1024]{2,1,0:T(8,128)(2,1)S(1)}, u32[]{:S(2)}, u32[]{:S(2)}) collective-permute-start(bf16[1,256,1024]{2,1,0:T(8,128)(2,1)S(1)} %fusion.129), channel_id=1, source_target_pairs={{0,1},{1,0},{2,3},{3,2},{4,5},{5,4},{6,7},{7,6},{8,9},{9,8},{10,11... | collective-permute-start | bytes 1572872 | tf_op jit(solution)/shard_map/ppermute | solution.py:657
  436.7 30.0 %collective-permute-start.65 = (bf16[1,256,1024]{2,1,0:T(8,128)(2,1)S(1)}, bf16[1,256,1024]{2,1,0:T(8,128)(2,1)S(1)}, u32[]{:S(2)}, u32[]{:S(2)}) collective-permute-start(bf16[1,256,1024]{2,1,0:T(8,128)(2,1)S(1)} %get-tuple-element.306), channel_id=1, source_target_pairs={{0,1},{1,0},{2,3},{3,2},{4,5},{5,4},{6,7},{7,6},{8,9},{9,8},{10,11... | collective-permute-start | bytes 1572872 | tf_op jit(solution)/shard_map/ppermute | solution.py:657
  485.3 53.4 %collective-permute-start.53 = (bf16[1,256,1024]{2,1,0:T(8,128)(2,1)S(1)}, bf16[1,256,1024]{2,1,0:T(8,128)(2,1)}, u32[]{:S(2)}, u32[]{:S(2)}) collective-permute-start(bf16[1,256,1024]{2,1,0:T(8,128)(2,1)S(1)} %fusion.168), channel_id=1, source_target_pairs={{0,2},{1,3},{2,0},{3,1},{4,6},{5,7},{6,4},{7,5},{8,10},{9,11},{10,... | collective-permute-start | bytes 1572872 | tf_op jit(solution)/shard_map/ppermute | solution.py:665
  492.2 50.5 %collective-permute-start.68 = (bf16[1,256,1024]{2,1,0:T(8,128)(2,1)}, bf16[1,256,1024]{2,1,0:T(8,128)(2,1)}, u32[]{:S(2)}, u32[]{:S(2)}) collective-permute-start(bf16[1,256,1024]{2,1,0:T(8,128)(2,1)} %get-tuple-element.303), channel_id=1, source_target_pairs={{0,1},{1,0},{2,3},{3,2},{4,5},{5,4},{6,7},{7,6},{8,9},{9,8},{10,11... | collective-permute-start | bytes 1572872 | tf_op jit(solution)/shard_map/ppermute | solution.py:657
  538.2 274.5 %all-reduce.12.cloned.1.call-start = ((), (), s32[]{:S(2)}) async-start(), calls=%async_computation.1 | async-start | bytes 8388608 | tf_op jit(solution)/shard_map/psum | solution.py:759
  542.7 27.3 %collective-permute-start.54 = (bf16[1,256,1024]{2,1,0:T(8,128)(2,1)}, bf16[1,256,1024]{2,1,0:T(8,128)(2,1)}, u32[]{:S(2)}, u32[]{:S(2)}) collective-permute-start(bf16[1,256,1024]{2,1,0:T(8,128)(2,1)} %get-tuple-element.314), channel_id=1, source_target_pairs={{0,1},{1,0},{2,3},{3,2},{4,5},{5,4},{6,7},{7,6},{8,9},{9,8},{10,11... | collective-permute-start | bytes 1572872 | tf_op jit(solution)/shard_map/ppermute | solution.py:657
  546.3 29.6 %collective-permute-start.71 = (bf16[1,256,1024]{2,1,0:T(8,128)(2,1)}, bf16[1,256,1024]{2,1,0:T(8,128)(2,1)}, u32[]{:S(2)}, u32[]{:S(2)}) collective-permute-start(bf16[1,256,1024]{2,1,0:T(8,128)(2,1)} %get-tuple-element.300), channel_id=1, source_target_pairs={{0,1},{1,0},{2,3},{3,2},{4,5},{5,4},{6,7},{7,6},{8,9},{9,8},{10,11... | collective-permute-start | bytes 1572872 | tf_op jit(solution)/shard_map/ppermute | solution.py:657
  569.0 28.0 %collective-permute-start.76 = (bf16[1,256,1024]{2,1,0:T(8,128)(2,1)}, bf16[1,256,1024]{2,1,0:T(8,128)(2,1)}, u32[]{:S(2)}, u32[]{:S(2)}) collective-permute-start(bf16[1,256,1024]{2,1,0:T(8,128)(2,1)} %fusion.192), channel_id=1, source_target_pairs={{0,1},{1,0},{2,3},{3,2},{4,5},{5,4},{6,7},{7,6},{8,9},{9,8},{10,11... | collective-permute-start | bytes 1572872 | tf_op jit(solution)/shard_map/ppermute | solution.py:657
  575.8 38.9 %collective-permute-start.55 = (bf16[1,256,1024]{2,1,0:T(8,128)(2,1)}, bf16[1,256,1024]{2,1,0:T(8,128)(2,1)}, u32[]{:S(2)}, u32[]{:S(2)}) collective-permute-start(bf16[1,256,1024]{2,1,0:T(8,128)(2,1)} %fusion.119), channel_id=1, source_target_pairs={{0,1},{1,0},{2,3},{3,2},{4,5},{5,4},{6,7},{7,6},{8,9},{9,8},{10,11... | collective-permute-start | bytes 1572872 | tf_op jit(solution)/shard_map/ppermute | solution.py:657
  599.3 216.6 %collective-permute-start.77 = (bf16[1,256,1024]{2,1,0:T(8,128)(2,1)}, bf16[1,256,1024]{2,1,0:T(8,128)(2,1)}, u32[]{:S(2)}, u32[]{:S(2)}) collective-permute-start(bf16[1,256,1024]{2,1,0:T(8,128)(2,1)} %fusion.165), channel_id=1, source_target_pairs={{0,2},{1,3},{2,0},{3,1},{4,6},{5,7},{6,4},{7,5},{8,10},{9,11},{10,... | collective-permute-start | bytes 1572872 | tf_op jit(solution)/shard_map/ppermute | solution.py:665
  604.7 213.3 %collective-permute-start.79 = (bf16[1,256,1024]{2,1,0:T(8,128)(2,1)}, bf16[1,256,1024]{2,1,0:T(8,128)(2,1)}, u32[]{:S(2)}, u32[]{:S(2)}) collective-permute-start(bf16[1,256,1024]{2,1,0:T(8,128)(2,1)} %fusion.193), channel_id=1, source_target_pairs={{0,1},{1,0},{2,3},{3,2},{4,5},{5,4},{6,7},{7,6},{8,9},{9,8},{10,11... | collective-permute-start | bytes 1572872 | tf_op jit(solution)/shard_map/ppermute | solution.py:657
  642.1 338.7 %all-reduce.10.cloned.1.call-start = ((), (), s32[]{:S(2)}) async-start(), calls=%async_computation | async-start | bytes 8912896 | tf_op jit(solution)/shard_map/psum | solution.py:759
  (282 other events, 3495.0 us)
Sparse Core Ops, SparseCore 0:
  343.0 188.4 all-reduce.15
  538.4 103.6 all-reduce.13
  646.4 166.2 all-reduce.11
  816.8 163.9 all-reduce.9

commit v2 on v1

--- a/solution.py
+++ b/solution.py
@@ -225,9 +225,10 @@
 
     @pl.when((stream == pl.num_programs(0) - 1) & (step == pl.num_programs(1) - 1))
     def _():
-        gbefore_ref[...] = wgrad[:, :, :rows].astype(LOW)
-        ghere_ref[...] = wgrad[:, :, rows : 2 * rows]
-        gafter_ref[...] = wgrad[:, :, 2 * rows :].astype(LOW)
+        for side in range(2):
+            gbefore_ref[side] = wgrad[side, :, :rows].T.astype(LOW)
+            ghere_ref[side] = wgrad[side, :, rows : 2 * rows].T
+            gafter_ref[side] = wgrad[side, :, 2 * rows :].T.astype(LOW)
 
 
 def causal_parts(own, table, gidx, pair):
@@ -464,8 +465,9 @@
 
     @pl.when((stream == pl.num_programs(0) - 1) & (step == pl.num_programs(1) - 1))
     def _():
-        gbefore_ref[...] = wgrad[:, :, :rows].astype(LOW)
-        ghere_ref[...] = wgrad[:, :, rows:]
+        for side in range(2):
+            gbefore_ref[side] = wgrad[side, :, :rows].T.astype(LOW)
+            ghere_ref[side] = wgrad[side, :, rows:].T
 
 
 def whole_spec(shape):
@@ -502,7 +504,7 @@
             vmem_limit_bytes=VMEM_BYTES, dimension_semantics=("arbitrary", "arbitrary")
         ),
         cost_estimate=pl.CostEstimate(
-            flops=int(cost), bytes_accessed=4 * 1024 * 1024, transcendentals=0
+            flops=int(cost), bytes_accessed=int(cost), transcendentals=0
         ),
     )
 
@@ -529,7 +531,7 @@
             pltpu.VMEM((pairs, 2 * BQ, 128), WIDE),
             pltpu.VMEM((pairs, 2 * BQ, 128), WIDE),
         ],
-        streams * 4e9,
+        1000,
     )(bounds, queries, before, here, after, qdoc, kdoc)
 
 
@@ -538,7 +540,7 @@
     pairs = width // PAIR
     blocks = 3 * rows // BK
     kv_spec = whole_spec((2, rows, width))
-    grad_spec = whole_spec((2, width, rows))
+    grad_spec = whole_spec((2, rows, width))
     return local_call(
         functools.partial(full_backward_kernel, with_self),
         (streams, rows // BQ),
@@ -547,16 +549,16 @@
         [rows_spec(width), grad_spec, grad_spec, grad_spec],
         [
             shaped((streams, rows, width), LOW),
-            shaped((2, width, rows), LOW),
-            shaped((2, width, rows), WIDE),
-            shaped((2, width, rows), LOW),
+            shaped((2, rows, width), LOW),
+            shaped((2, rows, width), WIDE),
+            shaped((2, rows, width), LOW),
         ],
         [
             pltpu.VMEM((2, 3 * rows, width), LOW),
             pltpu.VMEM((2, width, 3 * rows), WIDE),
             pltpu.VMEM((pairs, 2 * BQ, 128), WIDE),
         ],
-        streams * 8e9,
+        1000,
     )(bounds, queries, grads, att, lse, before, here, after, qdoc, kdoc)
 
 
@@ -606,7 +608,7 @@
             pltpu.VMEM((pairs, 2 * BQ, 128), WIDE),
             pltpu.VMEM((pairs, 2 * BQ, 128), WIDE),
         ],
-        streams * 4e9,
+        1000,
     )(*operands)
 
 
@@ -617,7 +619,7 @@
     pairs = width // PAIR
     blocks = 2 * rows // 128
     kv_spec = whole_spec((2, rows, width))
-    grad_spec = whole_spec((2, width, rows))
+    grad_spec = whole_spec((2, rows, width))
     specs = [rows_spec(width)] * 3 + [rows_spec(128), kv_spec, kv_spec, QDOC_SPEC]
     specs += [whole_spec((blocks, 1, 128)), rows_spec(128), whole_spec((BQ, 128))]
     specs += [whole_spec((BQ, 128)), whole_spec((2 * pairs, 128, 128))]
@@ -628,8 +630,8 @@
     out_shape = [
         shaped((streams, rows, width), LOW),
         shaped((streams, rows, 128), LOW),
-        shaped((2, width, rows), LOW),
-        shaped((2, width, rows), WIDE),
+        shaped((2, rows, width), LOW),
+        shaped((2, rows, width), WIDE),
     ]
     if own:
         specs.append(pair_rows_spec(width))
@@ -648,8 +650,242 @@
             pltpu.VMEM((pairs, 2 * BQ, 128), WIDE),
             pltpu.VMEM((pairs, 2 * BQ, 128), WIDE),
         ],
-        streams * 8e9,
+        1000,
     )(*operands)
+
+
+SUM_ROWS = 64
+SUM_WIDTH = 1024
+SUM_DELAY = 3
+MESH = pl.DeviceIdType.MESH
+
+
+def tree_kernel(count, *refs):
+    out_ref, x_ref, total, part, landed, sent_up, came_up, sent_down, came_down, filled = refs[-10:]
+    chunks = x_ref.shape[0]
+    fills, at = [], 0
+    for place, piece in enumerate(refs[:-10]):
+        size = piece.shape[0]
+        fills.append(
+            pltpu.make_async_copy(piece, x_ref.at[pl.ds(at, size)], filled.at[place])
+        )
+        at += size
+    for fill in fills:
+        fill.start()
+    ring = part.shape[0]
+    tall = count // 2
+    place = lax.axis_index("seq")
+    column = lax.rem(place, 2)
+    row = place // 2
+    beside = place + 1 - 2 * column
+
+    def everyone(act):
+        act(beside, None)
+        act(place - 2, row > 0)
+        act(place + 2, row < tall - 1)
+
+    barrier = pltpu.get_barrier_semaphore()
+
+    def greet(device, there):
+        def signal():
+            pl.semaphore_signal(barrier, inc=1, device_id={"seq": device}, device_id_type=MESH)
+
+        if there is None:
+            signal()
+        else:
+            pl.when(there)(signal)
+
+    everyone(greet)
+    friends = 1 + (row > 0).astype(jnp.int32) + (row < tall - 1).astype(jnp.int32)
+    pl.semaphore_wait(barrier, friends)
+
+    def role(chunk):
+        kind = lax.rem(chunk, 6 + tall)
+        spine = kind < 6
+        top = jnp.where(spine, tall // 2 - 1 + lax.rem(kind // 2, 2), kind - 6)
+        main = column == lax.rem(kind, 2)
+        walks = main | jnp.logical_not(spine)
+        here = row == top
+        children = (
+            main & (spine | here),
+            walks & (row > 0) & (row <= top),
+            walks & (row < tall - 1) & (row >= top),
+        )
+        reach = jnp.where(row < top, row, tall - 1 - row)
+        reach = jnp.where(here, jnp.maximum(top, tall - 1 - top), reach)
+        level = jnp.where(
+            spine, jnp.where(main, 1 + reach, 0), reach + (here & main).astype(jnp.int32)
+        )
+        depth = jnp.abs(row - top) + jnp.logical_not(main).astype(jnp.int32)
+        sideways = jnp.logical_not(main) & (spine | here)
+        return children, level, depth, main & here, sideways, row < top
+
+    devices = (beside, place - 2, place + 2)
+
+    def up_copy(chunk, slot, device):
+        at = lax.rem(chunk, ring)
+        return pltpu.make_async_remote_copy(
+            src_ref=part.at[at],
+            dst_ref=landed.at[at, slot],
+            send_sem=sent_up.at[at],
+            recv_sem=came_up.at[at, slot],
+            device_id={"seq": device},
+            device_id_type=MESH,
+        )
+
+    def down_copy(chunk, slot, device):
+        at = lax.rem(chunk, ring)
+        return pltpu.make_async_remote_copy(
+            src_ref=out_ref.at[chunk],
+            dst_ref=out_ref.at[chunk],
+            send_sem=sent_down.at[at, slot],
+            recv_sem=came_down.at[at],
+            device_id={"seq": device},
+            device_id_type=MESH,
+        )
+
+    def spread(chunk, children):
+        for slot, child in enumerate(children):
+
+            @pl.when(child)
+            def _():
+                down_copy(chunk, slot, devices[slot]).start()
+
+    def climb(chunk, children, root, sideways, rising):
+        at = lax.rem(chunk, ring)
+        total[...] = x_ref[chunk].astype(WIDE)
+        for slot, child in enumerate(children):
+
+            @pl.when(child)
+            def _():
+                up_copy(chunk, slot, devices[slot]).wait_recv()
+                total[...] += landed[at, slot].astype(WIDE)
+
+        @pl.when(root)
+        def _():
+            out_ref[chunk] = total[...].astype(LOW)
+            spread(chunk, children)
+
+        @pl.when(jnp.logical_not(root))
+        def _():
+            part[at] = total[...].astype(LOW)
+
+            @pl.when(sideways)
+            def _():
+                up_copy(chunk, 0, beside).start()
+
+            @pl.when(jnp.logical_not(sideways) & rising)
+            def _():
+                up_copy(chunk, 1, place + 2).start()
+
+            @pl.when(jnp.logical_not(sideways) & jnp.logical_not(rising))
+            def _():
+                up_copy(chunk, 2, place - 2).start()
+
+    def fall(chunk, children):
+        down_copy(chunk, 0, beside).wait_recv()
+        up_copy(chunk, 0, beside).wait_send()
+        spread(chunk, children)
+
+    def finish(chunk, children):
+        for slot, child in enumerate(children):
+
+            @pl.when(child)
+            def _():
+                down_copy(chunk, slot, devices[slot]).wait_send()
+
+    levels = tall + 1
+    for fill in fills:
+        fill.wait()
+
+    def period(time, carry):
+        def at_level(place_in_line, act):
+            chunk = time - SUM_DELAY * place_in_line
+
+            @pl.when((chunk >= 0) & (chunk < chunks))
+            def _():
+                act(chunk)
+
+        def finish_step(chunk):
+            finish(chunk, role(chunk)[0])
+
+        at_level(2 * levels + 1, finish_step)
+        for depth_now in range(levels, 0, -1):
+
+            def fall_step(chunk, depth_now=depth_now):
+                children, _, depth, root, _, _ = role(chunk)
+
+                @pl.when((depth == depth_now) & jnp.logical_not(root))
+                def _():
+                    fall(chunk, children)
+
+            at_level(levels + depth_now, fall_step)
+        for level_now in range(levels - 1, -1, -1):
+
+            def climb_step(chunk, level_now=level_now):
+                children, level, _, root, sideways, rising = role(chunk)
+
+                @pl.when(level == level_now)
+                def _():
+                    climb(chunk, children, root, sideways, rising)
+
+            at_level(level_now, climb_step)
+        return carry
+
+    lax.fori_loop(0, chunks + SUM_DELAY * (2 * levels + 1), period, 0)
+
+
+def link_sum(pieces, count):
+    levels = count // 2 + 1
+    chunks = sum(piece.shape[0] for piece in pieces)
+    ring = min(chunks, SUM_DELAY * (2 * levels + 1) + 1)
+    block = (SUM_ROWS, SUM_WIDTH)
+    return pl.pallas_call(
+        functools.partial(tree_kernel, count),
+        in_specs=[pl.BlockSpec(memory_space=pl.ANY)] * len(pieces),
+        out_specs=pl.BlockSpec(memory_space=pltpu.VMEM),
+        out_shape=shaped((chunks,) + block, LOW),
+        scratch_shapes=[
+            pltpu.VMEM((chunks,) + block, LOW),
+            pltpu.VMEM(block, WIDE),
+            pltpu.VMEM((ring,) + block, LOW),
+            pltpu.VMEM((ring, 3) + block, LOW),
+            pltpu.SemaphoreType.DMA((ring,)),
+            pltpu.SemaphoreType.DMA((ring, 3)),
+            pltpu.SemaphoreType.DMA((ring, 3)),
+            pltpu.SemaphoreType.DMA((ring,)),
+            pltpu.SemaphoreType.DMA((len(pieces),)),
+        ],
+        compiler_params=pltpu.CompilerParams(
+            collective_id=0, has_side_effects=True, vmem_limit_bytes=56 * 1024 * 1024
+        ),
+        cost_estimate=pl.CostEstimate(flops=1000, bytes_accessed=1000, transcendentals=0),
+    )(*pieces)
+
+
+PLAN = (
+    "e012ee0eee10ee20102010112122020101212020",
+    "101212F020011212e200Ce1e11Ce2eGe202ee100",
+    "S122D00eeWWee",
+)
+
+
+class Kept:
+    pass
+
+
+class Order:
+    def __init__(self):
+        self.token = None
+
+    def enter(self, *values):
+        if self.token is None:
+            return values
+        values, _ = lax.optimization_barrier((values, self.token))
+        return values
+
+    def leave(self, value):
+        self.token = value
 
 
 def swap_core(value):
@@ -657,16 +893,15 @@
     return lax.ppermute(value, "tp", [(place, place ^ 1) for place in range(count)])
 
 
-def sum_chips(value):
+def swap_chip(low):
     count = lax.axis_size("tp")
     hop = 2
-    while hop < count:
-        low = value.astype(LOW)
-        value = low.astype(WIDE) + lax.ppermute(
-            low, "tp", [(place, place ^ hop) for place in range(count)]
-        ).astype(WIDE)
+    got = lax.ppermute(low, "tp", [(place, place ^ hop) for place in range(count)])
+    while 2 * hop < count:
         hop *= 2
-    return value
+        low = (low.astype(WIDE) + got.astype(WIDE)).astype(LOW)
+        got = lax.ppermute(low, "tp", [(place, place ^ hop) for place in range(count)])
+    return low, got
 
 
 def core_index():
@@ -696,8 +931,16 @@
     return jnp.einsum("gsd,gsf->df", rows, grads, preferred_element_type=WIDE)
 
 
-def summed_rows(mine, other):
-    return sum_chips(mine + swap_core(other.astype(LOW)).astype(WIDE))
+def split_rows(cells):
+    if isinstance(cells, tuple):
+        return list(cells)
+    return [half_rows(cells, True), half_rows(cells, False)]
+
+
+def rows_weight_grad(lefts, rights):
+    lefts = [part for cells in lefts for part in split_rows(cells)]
+    rights = [part for cells in rights for part in split_rows(cells)]
+    return weight_grad(jnp.concatenate(lefts, 1), jnp.concatenate(rights, 1))
 
 
 def norm_forward(resid, gain, shift):
@@ -708,13 +951,7 @@
     return (normed * gain + shift, normed, inverse)
 
 
-def close_branch(resid, mine, other, gain, shift):
-    output, normed, inverse = norm_forward(resid + summed_rows(mine, other), gain, shift)
-    low = output.astype(LOW)
-    return (output, low, swap_core(low), (normed, inverse))
-
-
-def open_branch(grad_out, saved, gain):
+def norm_backward(grad_out, saved, gain):
     normed, inverse = saved
     grad_normed = grad_out * gain
     grad_resid = inverse * (
@@ -722,9 +959,8 @@
         - jnp.mean(grad_normed, -1, keepdims=True)
         - normed * jnp.mean(grad_normed * normed, -1, keepdims=True)
     )
-    low = grad_resid.astype(LOW)
     sums = jnp.stack([jnp.sum(grad_out * normed, (0, 1)), jnp.sum(grad_out, (0, 1))])
-    return (grad_resid, low, swap_core(low), sums)
+    return (grad_resid, sums)
 
 
 def gelu_both(hidden):
@@ -752,16 +988,14 @@
     return jnp.sum(jnp.where(match, values[None, :], 0), 1)
 
 
-def sum_seq(values, earlier):
-    low = tuple(value.astype(LOW) for value in values)
-    if earlier is not None:
-        low, earlier = lax.optimization_barrier((low, earlier))
-    return lax.psum(low, "seq")
-
-
 def pad_tables(tables):
     missing = 128 - tables.shape[-1]
     return jnp.pad(tables, ((0, 0), (0, 0), (0, missing))) if missing else tables
+
+
+def sum_seq(values, turn):
+    places = list(range(lax.axis_size("seq")))
+    return lax.psum(tuple(values), "seq", axis_index_groups=[places[turn:] + places[:turn]])
 
 
 def per_device(
@@ -820,141 +1054,154 @@
     full_bounds = jnp.stack([block_first // BK, (block_end + BK - 1) // BK])
     self_bounds = block_first // 128
 
-    enc_rows = enc_input[None]
-    enc_proj = jnp.einsum("sd,cdf->csf", enc_input, enc_qkv, preferred_element_type=WIDE).astype(LOW)
-    enc_pair = enc_proj[1:]
-    enc_query = enc_proj[:1]
-    enc_before = passed_along(enc_pair, 1)
-    enc_after = passed_along(enc_pair, -1)
-    dec_proj = [
-        jnp.einsum("sd,cdf->csf", dec_input[stream], self_qkv, preferred_element_type=WIDE).astype(LOW)
-        for stream in range(streams)
-    ]
-    main_pair = dec_proj[0][1:]
-    main_before = passed_along(main_pair, 1)
-    tables = pad_tables(project(dec_input, self_rel))
-
-    enc_att, enc_wide, enc_lse = full_forward(
-        True, full_bounds, enc_query, enc_before, enc_pair, enc_after, qdoc, enc_kdoc
-    )
-    enc_resid, enc_mine, enc_other, enc_saved_attn = close_branch(
-        half_rows(enc_rows, True).astype(WIDE),
-        project(half_rows(enc_att, True), enc_wout),
-        project(half_rows(enc_att, False), enc_wout),
-        enc_gain,
-        enc_bias,
-    )
-    enc_middle = jnp.concatenate([enc_mine, enc_other], 1)
-    enc_act, enc_slope = gelu_both(project(enc_middle, enc_up))
-
-    self_att, self_wide, self_lse = [], [], []
-    for stream in range(streams):
-        own = stream > 0
-        att, wide, lse = causal_forward(
-            own,
-            self_bounds,
-            dec_proj[stream][:1],
-            main_before,
-            main_pair,
+    order = Order()
+    enter, leave = order.enter, order.leave
+    enc, cross = Kept(), Kept()
+    dec = [Kept() for _ in range(streams)]
+    straight_rows = enc_input[None]
+
+    def halves(att, weight):
+        other = project(half_rows(att, False), weight).astype(LOW)
+        mine = project(half_rows(att, True), weight)
+        return mine, other
+
+    def back_halves(grads, weight):
+        other = back_project(half_rows(grads, False), weight).astype(LOW)
+        mine = back_project(half_rows(grads, True), weight)
+        return mine, other
+
+    def exchange(mine, other):
+        got = swap_core(other)
+        yield
+        mine, got = enter(mine, got)
+        low = (mine + got.astype(WIDE)).astype(LOW)
+        leave(low)
+        low, got = swap_chip(low)
+        yield
+        low, got = enter(low, got)
+        return low.astype(WIDE) + got.astype(WIDE)
+
+    def close_branch(resid, mine, other, gain, shift):
+        total = yield from exchange(mine, other)
+        output, normed, inverse = norm_forward(resid + total, gain, shift)
+        low = output.astype(LOW)
+        leave(low)
+        return output, low, swap_core(low), (normed, inverse)
+
+    def open_branch(grad, saved, gain):
+        grad, sums = norm_backward(grad, saved, gain)
+        low = grad.astype(LOW)
+        leave(low)
+        return grad, low, swap_core(low), sums
+
+    def encoder():
+        (enc_rows,) = enter(enc_input)
+        pair = jnp.einsum("sd,cdf->csf", enc_rows, enc_qkv[1:], preferred_element_type=WIDE).astype(LOW)
+        enc.pair = pair
+        enc.before = passed_along(pair, 1)
+        enc.after = passed_along(pair, -1)
+        enc.query = project(enc_rows[None], enc_qkv[0]).astype(LOW)
+        leave(enc.query)
+        yield
+        query, before, after = enter(enc.query, enc.before, enc.after)
+        enc.query, enc.before, enc.after = query, before, after
+        att, wide, lse = full_forward(
+            True, full_bounds, query, before, enc.pair, after, qdoc, enc_kdoc
+        )
+        enc.att, enc.wide, enc.lse = att, wide, lse
+        mine, other = halves(att, enc_wout)
+        leave(mine)
+        resid = half_rows(straight_rows, True).astype(WIDE)
+        resid, mine, got, enc.saved_att = yield from close_branch(
+            resid, mine, other, enc_gain, enc_bias
+        )
+        yield
+        mine, got = enter(mine, got)
+        middle = jnp.concatenate([mine, got], 1)
+        act, slope = gelu_both(project(middle, enc_up))
+        enc.middle, enc.act, enc.slope = middle, act, slope
+        other = project(act[:, half:], enc_down).astype(LOW)
+        mine = project(act[:, :half], enc_down)
+        leave(mine)
+        resid, mine, got, enc.saved_ffn = yield from close_branch(
+            resid, mine, other, post_gain, post_bias
+        )
+        yield
+        mine, got = enter(mine, got)
+        enc.final = natural_rows(mine, got)
+        pair = jnp.einsum(
+            "sd,cdf->csf", enc.final[0], cross_wkv, preferred_element_type=WIDE
+        ).astype(LOW)
+        leave(pair)
+        cross.pair = pair
+        cross.before = passed_along(pair, 1)
+        cross.after = passed_along(pair, -1)
+        yield
+        parts = enter(*[dec[stream].cross_parts for stream in range(streams)])
+        to_before = sum(part[0].astype(WIDE) for part in parts).astype(LOW)
+        to_after = sum(part[2].astype(WIDE) for part in parts).astype(LOW)
+        here = sum(part[1] for part in parts)
+        leave(to_after)
+        from_next = passed_along(to_before, -1)
+        from_last = passed_along(to_after, 1)
+        yield
+        here, from_next, from_last = enter(here, from_next, from_last)
+        pair_grad = (here + from_next.astype(WIDE) + from_last.astype(WIDE)).astype(LOW)
+        cross.pair_grad = pair_grad
+        extra = jnp.einsum("csf,cdf->sd", pair_grad, cross_wkv, preferred_element_type=WIDE)[None]
+        mine, other = half_rows(extra, True), half_rows(extra, False).astype(LOW)
+        leave(other)
+        total = yield from exchange(mine, other)
+        grad = half_rows(enc_cotan[None], True).astype(WIDE) + total
+        grad, mine, got, enc.post_sums = open_branch(grad, enc.saved_ffn, post_gain)
+        yield
+        mine, got = enter(mine, got)
+        ffn_rows = jnp.concatenate([mine, got], 1)
+        grad_act = jnp.einsum("gsd,fd->gsf", ffn_rows, enc_down, preferred_element_type=WIDE)
+        hidden_grad = (grad_act * enc.slope.astype(WIDE)).astype(LOW)
+        enc.ffn_rows, enc.hidden_grad = ffn_rows, hidden_grad
+        other = back_project(hidden_grad[:, half:], enc_up).astype(LOW)
+        mine = back_project(hidden_grad[:, :half], enc_up)
+        leave(mine)
+        total = yield from exchange(mine, other)
+        grad, mine, got, enc.att_sums = open_branch(grad + total, enc.saved_att, enc_gain)
+        yield
+        mine, got = enter(mine, got)
+        enc.att_rows = (mine, got)
+        query_grad, to_before, here, to_after = full_backward(
+            True,
+            full_bounds,
+            enc.query,
+            att_grad(mine, got, enc_wout),
+            enc.wide,
+            enc.lse,
+            enc.before,
+            enc.pair,
+            enc.after,
             qdoc,
-            self_kdoc,
-            tables[stream : stream + 1],
-            dec_proj[stream][1:][None] if own else None,
-        )
-        self_att.append(att)
-        self_wide.append(wide)
-        self_lse.append(lse)
-
-    enc_resid, enc_mine, enc_other, enc_saved_ffn = close_branch(
-        enc_resid,
-        project(enc_act[:, :half], enc_down),
-        project(enc_act[:, half:], enc_down),
-        post_gain,
-        post_bias,
-    )
-    enc_final = natural_rows(enc_mine, enc_other)
-    cross_pair = jnp.einsum(
-        "sd,cdf->csf", enc_final[0], cross_wkv, preferred_element_type=WIDE
-    ).astype(LOW)
-    cross_before = passed_along(cross_pair, 1)
-    cross_after = passed_along(cross_pair, -1)
-
-    groups = [(stream, stream + 1) for stream in range(streams)]
-    first_saved, first_rows, first_resid = [], [], []
-    for stream in range(streams):
-        resid, mine, other, saved = close_branch(
-            half_rows(dec_input[stream][None], True).astype(WIDE),
-            project(half_rows(self_att[stream], True), self_wout),
-            project(half_rows(self_att[stream], False), self_wout),
-            self_gain,
-            self_bias,
-        )
-        first_resid.append(resid)
-        first_saved.append(saved)
-        first_rows.append((mine, other))
-    cross_query, cross_att, cross_wide, cross_lse = [], [], [], []
-    for stream in range(streams):
-        mine, other = first_rows[stream]
-        query = natural_rows(
-            project(mine, cross_wq).astype(LOW), project(other, cross_wq).astype(LOW)
-        )
-        att, wide, lse = full_forward(
-            False, full_bounds, query, cross_before, cross_pair, cross_after, qdoc, cross_kdoc
-        )
-        cross_query.append(query)
-        cross_att.append(att)
-        cross_wide.append(wide)
-        cross_lse.append(lse)
-    second_saved, second_rows, second_resid = [], [], []
-    for stream in range(streams):
-        resid, mine, other, saved = close_branch(
-            first_resid[stream],
-            project(half_rows(cross_att[stream], True), cross_wout),
-            project(half_rows(cross_att[stream], False), cross_wout),
-            cross_gain,
-            cross_bias,
-        )
-        second_resid.append(resid)
-        second_saved.append(saved)
-        second_rows.append(jnp.concatenate([mine, other], 1))
-    dec_act, dec_slope = [], []
-    dec_final, grad, ffn_grad_rows, ffn_sums = [], [], [], []
-    for stream in range(streams):
-        act, slope = gelu_both(project(second_rows[stream], ffn_up))
-        dec_act.append(act)
-        dec_slope.append(slope)
-        resid, mine, other, saved = close_branch(
-            second_resid[stream],
-            project(act[:, :half], ffn_down),
-            project(act[:, half:], ffn_down),
-            ffn_gain,
-            ffn_bias,
-        )
-        dec_final.append(natural_rows(mine, other))
-        grad_out = half_rows(dec_cotan[stream][None], True).astype(WIDE)
-        resid_grad, mine, other, sums = open_branch(grad_out, saved, ffn_gain)
-        grad.append(resid_grad)
-        ffn_grad_rows.append(jnp.concatenate([mine, other], 1))
-        ffn_sums.append(sums)
-    dec_final = jnp.concatenate(dec_final, 0)
-
-    cross_sums, cross_grad_rows, hidden_grads = [], [], []
-    for stream in range(streams):
-        grad_act = jnp.einsum(
-            "gsd,fd->gsf", ffn_grad_rows[stream], ffn_down, preferred_element_type=WIDE
-        )
-        hidden_grad = (grad_act * dec_slope[stream].astype(WIDE)).astype(LOW)
-        hidden_grads.append(hidden_grad)
-        grad[stream] = grad[stream] + summed_rows(
-            back_project(hidden_grad[:, :half], ffn_up), back_project(hidden_grad[:, half:], ffn_up)
-        )
-        resid_grad, mine, other, sums = open_branch(grad[stream], second_saved[stream], cross_gain)
-        grad[stream] = resid_grad
-        cross_grad_rows.append((mine, other))
-        cross_sums.append(sums)
-    ffn_down_grad = weight_grad(jnp.concatenate(dec_act), jnp.concatenate(ffn_grad_rows))
-    ffn_up_grad = weight_grad(jnp.concatenate(second_rows), jnp.concatenate(hidden_grads))
-    ffn_sum = sum_seq([ffn_down_grad, ffn_up_grad], None)
+            enc_kdoc,
+        )
+        leave(query_grad)
+        from_next = passed_along(to_before, -1)
+        from_last = passed_along(to_after, 1)
+        yield
+        here, from_next, from_last = enter(here, from_next, from_last)
+        pair_grad = (here + from_next.astype(WIDE) + from_last.astype(WIDE)).astype(LOW)
+        enc.query_grad, enc.pair_grad = query_grad, pair_grad
+        partial_value = back_project(query_grad, enc_qkv[0]) + jnp.einsum(
+            "csf,cdf->sd", pair_grad, enc_qkv[1:], preferred_element_type=WIDE
+        )
+        mine, other = half_rows(partial_value, True), half_rows(partial_value, False).astype(LOW)
+        leave(other)
+        total = yield from exchange(mine, other)
+        low = (grad + total).astype(LOW)
+        leave(low)
+        got = swap_core(low)
+        yield
+        low, got = enter(low, got)
+        enc.grad = natural_rows(low, got)[0]
+        leave(enc.grad)
+        yield
 
     def att_grad(mine, other, weight):
         return natural_rows(
@@ -962,167 +1209,270 @@
             jnp.einsum("gsd,fd->gsf", other, weight, preferred_element_type=WIDE).astype(LOW),
         )
 
-    def att_weight_grad(atts, grads):
-        lefts, rights = [], []
-        for att, (mine, other) in zip(atts, grads):
-            lefts += [half_rows(att, True), half_rows(att, False)]
-            rights += [mine, other]
-        return weight_grad(jnp.concatenate(lefts, 1), jnp.concatenate(rights, 1))
-
-    cross_query_grads, cross_parts = [], []
-    for stream in range(streams):
-        cross_att_grad = att_grad(*cross_grad_rows[stream], cross_wout)
-        query_grad, *parts = full_backward(
+    def decoder(stream):
+        own = stream > 0
+        kept = dec[stream]
+        (dec_rows,) = enter(dec_input[stream : stream + 1])
+        pair = jnp.einsum(
+            "gsd,cdf->gcsf", dec_rows, self_qkv[1:], preferred_element_type=WIDE
+        ).astype(LOW)
+        query = project(dec_rows, self_qkv[0]).astype(LOW)
+        table = pad_tables(project(dec_rows, self_rel))
+        leave((pair, query, table))
+        if stream == 0:
+            cross.main = pair[0]
+            cross.main_before = passed_along(pair[0], 1)
+        yield
+        main = cross.main
+        query, main_before = enter(query, cross.main_before)
+        cross.main_before = main_before
+        own_pair = pair if own else None
+        att, wide, lse = causal_forward(
+            own, self_bounds, query, main_before, main, qdoc, self_kdoc, table, own_pair
+        )
+        kept.self_att = att
+        mine, other = halves(att, self_wout)
+        leave(mine)
+        resid, mine, got, saved_self = yield from close_branch(
+            half_rows(dec_rows, True).astype(WIDE), mine, other, self_gain, self_bias
+        )
+        yield
+        mine, got = enter(mine, got)
+        kept.first = (mine, got)
+        cross_query = natural_rows(
+            project(mine, cross_wq).astype(LOW), project(got, cross_wq).astype(LOW)
+        )
+        leave(cross_query)
+        yield
+        cross_query, before, after = enter(cross_query, cross.before, cross.after)
+        cross.before, cross.after = before, after
+        cross_att, cross_wide, cross_lse = full_forward(
+            False, full_bounds, cross_query, before, cross.pair, after, qdoc, cross_kdoc
+        )
+        kept.cross_att = cross_att
+        mine, other = halves(cross_att, cross_wout)
+        leave(mine)
+        resid, mine, got, saved_cross = yield from close_branch(
+            resid, mine, other, cross_gain, cross_bias
+        )
+        yield
+        mine, got = enter(mine, got)
+        second = jnp.concatenate([mine, got], 1)
+        act, slope = gelu_both(project(second, ffn_up))
+        kept.second, kept.act = second, act
+        other = project(act[:, half:], ffn_down).astype(LOW)
+        mine = project(act[:, :half], ffn_down)
+        leave(mine)
+        total = yield from exchange(mine, other)
+        output, normed, inverse = norm_forward(resid + total, ffn_gain, ffn_bias)
+        final_mine = output.astype(LOW)
+        final_got = swap_core(final_mine)
+        grad = half_rows(dec_cotan[stream : stream + 1], True).astype(WIDE)
+        grad, mine, got, kept.ffn_sums = open_branch(grad, (normed, inverse), ffn_gain)
+        yield
+        mine, got = enter(mine, got)
+        ffn_rows = jnp.concatenate([mine, got], 1)
+        grad_act = jnp.einsum("gsd,fd->gsf", ffn_rows, ffn_down, preferred_element_type=WIDE)
+        hidden_grad = (grad_act * slope.astype(WIDE)).astype(LOW)
+        kept.ffn_rows, kept.hidden_grad = ffn_rows, hidden_grad
+        other = back_project(hidden_grad[:, half:], ffn_up).astype(LOW)
+        mine = back_project(hidden_grad[:, :half], ffn_up)
+        leave(mine)
+        total = yield from exchange(mine, other)
+        grad, mine, got, kept.cross_sums = open_branch(grad + total, saved_cross, cross_gain)
+        kept.final = natural_rows(final_mine, final_got)
+        yield
+        mine, got = enter(mine, got)
+        kept.cross_rows = (mine, got)
+        query_grad, *kept.cross_parts = full_backward(
             False,
             full_bounds,
-            cross_query[stream],
-            cross_att_grad,
-            cross_wide[stream],
-            cross_lse[stream],
-            cross_before,
-            cross_pair,
-            cross_after,
+            cross_query,
+            att_grad(mine, got, cross_wout),
+            cross_wide,
+            cross_lse,
+            cross.before,
+            cross.pair,
+            cross.after,
             qdoc,
             cross_kdoc,
         )
-        cross_query_grads.append(query_grad)
-        cross_parts.append(parts)
-
-    def fold_pair(parts, after):
-        to_before = sum(part[0].astype(WIDE) for part in parts).astype(LOW)
-        here = sum(part[1] for part in parts) + passed_along(to_before, -1).astype(WIDE)
-        if after:
-            to_after = sum(part[2].astype(WIDE) for part in parts).astype(LOW)
-            here = here + passed_along(to_after, 1).astype(WIDE)
-        return here.astype(LOW)
-
-    cross_pair_grad = fold_pair(cross_parts, True)
-    enc_extra = jnp.einsum("cfs,cdf->sd", cross_pair_grad, cross_wkv, preferred_element_type=WIDE)[None]
-    enc_grad = half_rows(enc_cotan[None], True).astype(WIDE) + summed_rows(
-        half_rows(enc_extra, True), half_rows(enc_extra, False)
-    )
-    enc_grad, mine, other, post_sums = open_branch(enc_grad, enc_saved_ffn, post_gain)
-    enc_ffn_rows = jnp.concatenate([mine, other], 1)
-
-    self_sums, self_grad_rows = [], []
-    for stream in range(streams):
-        query_grad = cross_query_grads[stream]
-        grad[stream] = grad[stream] + summed_rows(
-            back_project(half_rows(query_grad, True), cross_wq),
-            back_project(half_rows(query_grad, False), cross_wq),
-        )
-        resid_grad, mine, other, sums = open_branch(grad[stream], first_saved[stream], self_gain)
-        grad[stream] = resid_grad
-        self_grad_rows.append((mine, other))
-        self_sums.append(sums)
-    cross_wout_grad = att_weight_grad(cross_att, cross_grad_rows)
-    cross_wq_grad = att_weight_grad(cross_query_grads, first_rows).T
-    cross_wkv_grad = jnp.einsum("sd,cfs->cdf", enc_final[0], cross_pair_grad, preferred_element_type=WIDE)
-    cross_sum = sum_seq([cross_wout_grad, cross_wq_grad, cross_wkv_grad], ffn_sum)
-
-    grad_act = jnp.einsum("gsd,fd->gsf", enc_ffn_rows, enc_down, preferred_element_type=WIDE)
-    hidden_grad = (grad_act * enc_slope.astype(WIDE)).astype(LOW)
-    enc_grad = enc_grad + summed_rows(
-        back_project(hidden_grad[:, :half], enc_up), back_project(hidden_grad[:, half:], enc_up)
-    )
-    enc_sum = sum_seq(
-        [weight_grad(enc_act, enc_ffn_rows), weight_grad(enc_middle, hidden_grad)], cross_sum
-    )
-    enc_grad, mine, other, enc_sums = open_branch(enc_grad, enc_saved_attn, enc_gain)
-    enc_grad_rows = (mine, other)
-
-    self_proj_grads, self_parts, table_grads = [], [], []
-    for stream in range(streams):
-        own = stream > 0
-        self_att_grad = att_grad(*self_grad_rows[stream], self_wout)
-        query_grad, table_grad, *parts = causal_backward(
+        kept.cross_query_grad = query_grad
+        mine, other = back_halves(query_grad, cross_wq)
+        leave(mine)
+        total = yield from exchange(mine, other)
+        grad, mine, got, kept.self_sums = open_branch(grad + total, saved_self, self_gain)
+        yield
+        mine, got = enter(mine, got)
+        kept.self_rows = (mine, got)
+        query_grad, table_grad, to_before, here, *own_grad = causal_backward(
             own,
             self_bounds,
-            dec_proj[stream][:1],
-            self_att_grad,
-            self_wide[stream],
-            self_lse[stream],
+            query,
+            att_grad(mine, got, self_wout),
+            wide,
+            lse,
             main_before,
-            main_pair,
+            main,
             qdoc,
             self_kdoc,
-            tables[stream : stream + 1],
-            dec_proj[stream][1:][None] if own else None,
-        )
-        self_parts.append(parts[:2])
-        table_grads.append(table_grad[:, :, :table_width])
-        own_grad = parts[2][0] if own else None
-        self_proj_grads.append([query_grad, own_grad])
-    main_grad = fold_pair(self_parts, False)
-    main_grad = jnp.swapaxes(main_grad, 1, 2)
-    dec_grad = []
-    full_proj_grads = []
-    for stream in range(streams):
-        query_grad, own_grad = self_proj_grads[stream]
-        pair_grad = main_grad if stream == 0 else own_grad
-        proj_grad = jnp.concatenate([query_grad, pair_grad], 0)
-        full_proj_grads.append(proj_grad)
+            table,
+            own_pair,
+        )
+        table_grad = table_grad[:, :, :table_width]
+        kept.table_grad = table_grad
+        kept.self_parts = (to_before, here)
+        leave(query_grad)
+        if own:
+            pair_grad = own_grad[0][0]
+        else:
+            yield
+            parts = enter(*[dec[item].self_parts for item in range(streams)])
+            to_before = sum(part[0].astype(WIDE) for part in parts).astype(LOW)
+            here = sum(part[1] for part in parts)
+            leave(to_before)
+            from_next = passed_along(to_before, -1)
+            yield
+            here, from_next = enter(here, from_next)
+            pair_grad = (here + from_next.astype(WIDE)).astype(LOW)
+        kept.query_grad, kept.pair_grad = query_grad, pair_grad
         partial_value = (
-            jnp.einsum("csf,cdf->sd", proj_grad, self_qkv, preferred_element_type=WIDE)[None]
-            + back_project(table_grads[stream], self_rel)
-        )
-        total = grad[stream] + summed_rows(
-            half_rows(partial_value, True), half_rows(partial_value, False)
-        )
-        low = total.astype(LOW)
-        dec_grad.append(natural_rows(low, swap_core(low)))
-    dec_grad = jnp.concatenate(dec_grad, 0)
-    self_qkv_grad = jnp.einsum(
-        "gsd,gcsf->cdf", dec_input, jnp.stack(full_proj_grads), preferred_element_type=WIDE
-    )
-    self_rel_grad = weight_grad(dec_input, jnp.concatenate(table_grads, 0))
-    self_wout_grad = att_weight_grad(self_att, self_grad_rows)
-
-    enc_att_grad = att_grad(*enc_grad_rows, enc_wout)
-    query_grad, *parts = full_backward(
-        True,
-        full_bounds,
-        enc_query,
-        enc_att_grad,
-        enc_wide,
-        enc_lse,
-        enc_before,
-        enc_pair,
-        enc_after,
-        qdoc,
-        enc_kdoc,
-    )
-    pair_grad = jnp.swapaxes(fold_pair([parts], True), 1, 2)
-    enc_proj_grad = jnp.concatenate([query_grad, pair_grad], 0)
-    enc_qkv_grad = jnp.einsum("sd,csf->cdf", enc_input, enc_proj_grad, preferred_element_type=WIDE)
-    partial_value = jnp.einsum(
-        "csf,cdf->sd", enc_proj_grad, enc_qkv, preferred_element_type=WIDE
-    )[None]
-    enc_grad = enc_grad + summed_rows(
-        half_rows(partial_value, True), half_rows(partial_value, False)
-    )
-    low = enc_grad.astype(LOW)
-    enc_grad = natural_rows(low, swap_core(low))[0]
-    enc_wout_grad = att_weight_grad([enc_att], [enc_grad_rows])
-
-    sums = jnp.concatenate(
-        [enc_sums, post_sums, sum(self_sums), sum(cross_sums), sum(ffn_sums)], 0
-    )
-    sums = sums + swap_core(sums)
-    last_sum = sum_seq(
-        [self_qkv_grad, self_rel_grad, self_wout_grad, enc_qkv_grad, enc_wout_grad, sums], enc_sum
-    )
-    ffn_down_grad, ffn_up_grad = [value.astype(WIDE) for value in ffn_sum]
-    cross_wout_grad, cross_wq_grad, cross_wkv_grad = [value.astype(WIDE) for value in cross_sum]
-    enc_down_grad, enc_up_grad = [value.astype(WIDE) for value in enc_sum]
-    self_qkv_grad, self_rel_grad, self_wout_grad, enc_qkv_grad, enc_wout_grad, sums = [
-        value.astype(WIDE) for value in last_sum
+            back_project(query_grad, self_qkv[0])
+            + jnp.einsum("csf,cdf->sd", pair_grad, self_qkv[1:], preferred_element_type=WIDE)
+            + back_project(table_grad, self_rel)
+        )
+        mine, other = half_rows(partial_value, True), half_rows(partial_value, False).astype(LOW)
+        leave(other)
+        total = yield from exchange(mine, other)
+        low = (grad + total).astype(LOW)
+        leave(low)
+        got = swap_core(low)
+        yield
+        low, got = enter(low, got)
+        kept.grad = natural_rows(low, got)
+        leave(kept.grad)
+        yield
+
+    weights = Kept()
+
+    def ffn_weights():
+        acts, grads = enter([kept.act for kept in dec], [kept.ffn_rows for kept in dec])
+        down = weight_grad(jnp.concatenate(acts), jnp.concatenate(grads)).astype(LOW)
+        seconds, grads = [kept.second for kept in dec], [kept.hidden_grad for kept in dec]
+        up = weight_grad(jnp.concatenate(seconds), jnp.concatenate(grads)).astype(LOW)
+        leave((down, up))
+        weights.ffn = sum_seq((down, up), 0)
+        yield
+
+    def cross_weights():
+        atts, grads = enter([kept.cross_att for kept in dec], [kept.cross_rows for kept in dec])
+        wout = rows_weight_grad(atts, grads).astype(LOW)
+        firsts = [kept.first for kept in dec]
+        wq = rows_weight_grad(firsts, [kept.cross_query_grad for kept in dec]).astype(LOW)
+        leave((wout, wq))
+        weights.cross = (wout, wq)
+        yield
+        (final,) = enter(enc.final)
+        wkv = jnp.einsum(
+            "sd,csf->cdf", final[0], cross.pair_grad, preferred_element_type=WIDE
+        ).astype(LOW)
+        leave(wkv)
+        weights.cross = sum_seq(weights.cross + (wkv,), 1)
+        yield
+
+    def enc_ffn_weights():
+        act, grads = enter(enc.act, enc.ffn_rows)
+        down = weight_grad(act, grads).astype(LOW)
+        up = weight_grad(enc.middle, enc.hidden_grad).astype(LOW)
+        leave((down, up))
+        weights.enc = [down, up]
+        yield
+
+    def turned(cells):
+        return jnp.swapaxes(cells, -1, -2)
+
+    def self_weights():
+        atts, grads = enter([kept.self_att for kept in dec], [kept.self_rows for kept in dec])
+        wout = rows_weight_grad(atts, grads).astype(LOW)
+        tables = jnp.concatenate([kept.table_grad for kept in dec], 0)
+        rel = weight_grad(tables, dec_input).astype(LOW)
+        queries = jnp.concatenate([kept.query_grad for kept in dec])
+        query = weight_grad(queries, dec_input).astype(LOW)
+        pairs = jnp.stack([kept.pair_grad for kept in dec])
+        pair = jnp.einsum(
+            "gsd,gcsf->cfd", dec_input, pairs, preferred_element_type=WIDE
+        ).astype(LOW)
+        leave((wout, rel, query, pair))
+        weights.self = [wout, rel, query, pair]
+        yield
+
+    def finished():
+        (finals,) = enter([kept.final for kept in dec])
+        weights.final = jnp.concatenate(finals, 0)
+        leave(weights.final)
+        yield
+
+    def enc_weights():
+        query_grad, pair_grad, grads = enter(enc.query_grad, enc.pair_grad, enc.att_rows)
+        query = weight_grad(query_grad, straight_rows).astype(LOW)
+        pair = jnp.einsum(
+            "sd,csf->cfd", enc_input, pair_grad, preferred_element_type=WIDE
+        ).astype(LOW)
+        wout = rows_weight_grad([enc.att], [grads]).astype(LOW)
+        sums = jnp.concatenate(
+            [
+                enc.att_sums,
+                enc.post_sums,
+                sum(kept.self_sums for kept in dec),
+                sum(kept.cross_sums for kept in dec),
+                sum(kept.ffn_sums for kept in dec),
+            ],
+            0,
+        )
+        sums = (sums + swap_core(sums)).astype(LOW).reshape(-1, SUM_WIDTH)
+        padded = jnp.pad(sums, ((0, -sums.shape[0] % SUM_ROWS), (0, 0)))
+        parts = weights.enc + weights.self + [wout, query, pair]
+        pieces = [part.reshape(-1, SUM_ROWS, SUM_WIDTH) for part in parts + [padded]]
+        parts.append(sums)
+        leave((wout, query, pair, padded))
+        yield
+        pieces = enter(*pieces)
+        summed = link_sum(pieces, lax.axis_size("seq"))
+        leave(summed)
+        weights.ffn, weights.cross = enter(weights.ffn, weights.cross)
+        summed = summed.reshape(-1, SUM_WIDTH)
+        found, at = [], 0
+        for part in parts:
+            size = part.size // SUM_WIDTH
+            found.append(summed[at : at + size].astype(WIDE).reshape(part.shape))
+            at += size
+        weights.last = found
+        yield
+
+    tasks = {"e": encoder(), "F": ffn_weights(), "C": cross_weights()}
+    tasks.update({"D": finished(), "G": enc_ffn_weights(), "S": self_weights(), "W": enc_weights()})
+    tasks.update({str(stream): decoder(stream) for stream in range(streams)})
+    for item in "".join(PLAN):
+        next(tasks[item], None)
+    for task in tasks.values():
+        for _ in task:
+            pass
+
+    ffn_down_grad, ffn_up_grad = [value.astype(WIDE) for value in weights.ffn]
+    cross_wout_grad, cross_wq_grad, cross_wkv_grad = [
+        value.astype(WIDE) for value in weights.cross
     ]
+    enc_down_grad, enc_up_grad, *found = weights.last
+    self_wout_grad, self_rel_grad, query, pair, *found = found
+    self_qkv_grad = jnp.concatenate([turned(query)[None], turned(pair)], 0)
+    enc_wout_grad, query, pair, sums = found
+    enc_qkv_grad = jnp.concatenate([turned(query)[None], turned(pair)], 0)
+    sums = sums.reshape(-1, enc_input.shape[1])
     return (
-        enc_final[0],
-        dec_final,
-        enc_grad,
-        dec_grad,
+        enc.final[0],
+        weights.final,
+        enc.grad,
+        jnp.concatenate([kept.grad for kept in dec], 0),
         enc_qkv_grad,
         enc_wout_grad,
         sums[0],
@@ -1132,7 +1482,7 @@
         sums[2],
         sums[3],
         self_qkv_grad,
-        self_rel_grad,
+        self_rel_grad.T,
         self_wout_grad,
         sums[4],
         sums[5],

time: 1000 us -> 837 us (0.84); the launches traced: 997 us -> 823 us
  waiting for transfers between devices: 483 us -> 135 us
  Pallas kernels: 125 us -> 309 us
  blocking collectives: 35.4 us -> 0 us
  starting transfers between devices: 73.3 us -> 91.2 us
  other arithmetic: 84.5 us -> 101 us
    psum x4 -> x2, waiting for transfers between devices: 255 us -> 0.01 us  [sum_seq(): lax.psum(tuple(values), 'seq', axis_index_groups=[places[turn:] + places[...]
    pallas_call x0 -> x1, Pallas kernels: none -> 210 us  [link_sum(): pl.pallas_call(functools.partial(tree_kernel, count), in_specs=[pl.BlockS...]
    ppermute x23, waiting for transfers between devices: 165 us -> 79.7 us  [swap_chip(): lax.ppermute(low, 'tp', [(place, place ^ hop) for place in range(count)])]
    psum x1 -> x0, blocking collectives: 35.4 us -> none  [sum_seq(): return lax.psum(low, 'seq')]
    ppermute x10, starting transfers between devices: 36.3 us -> 56.9 us  [passed_along(): return lax.ppermute(value, 'seq', pairs)]
    convert_element_type x21 -> x51, other arithmetic: 28.6 us -> 47.5 us  [the longest x23 15.2 us: exchange(): low = (mine + got.astype(WIDE)).astype(LOW)]
    dot_general x33 -> x39, matrix products: 21.2 us -> 38.3 us  [project(): return jnp.einsum('gsd,df->gsf', rows, weight, preferred_element_type=WIDE)]
    dot_general x17, matrix products: 38.6 us -> 27.5 us  [the longest x3 6.22 us: decoder(): jnp.einsum('gsd,fd->gsf', ffn_rows, ffn_down, preferred_element_type=WIDE)]
  transfers between devices with their start and end apart: 87 -> 85, of which waited for: 32 -> 31; matrix products, arithmetic and copies ran while one was open for 22% -> 27% of each run, Pallas kernels for 12% -> 36%
where the time goes in v2:
time: 837 us; the launch traced here: 823 us
  Pallas kernels  309 us (37%)
  waiting for transfers between devices  135 us (16%)
  matrix products  115 us (14%)
  other arithmetic  101 us (12%)
  starting transfers between devices  91.2 us (11%)
  local copies, waits for them, and re-layouts  52.3 us (6%)
  between operations  19.6 us (2%)
    pallas_call x1, Pallas kernels, link_sum(): pl.pallas_call(functools.partial(tree_kernel, count), in_specs=[pl.BlockS...  210 us
    ppermute x23, waiting for transfers between devices, swap_chip(): lax.ppermute(low, 'tp', [(place, place ^ hop) for place in range(count)])  79.7 us
    ppermute x10, starting transfers between devices, passed_along(): return lax.ppermute(value, 'seq', pairs)  56.9 us
    ppermute x10, waiting for transfers between devices, passed_along(): return lax.ppermute(value, 'seq', pairs)  48.4 us
    dot_general x39, matrix products, project(): return jnp.einsum('gsd,df->gsf', rows, weight, preferred_element_type=WIDE)  38.3 us
    pallas_call x4, Pallas kernels, full_backward(): local_call(functools.partial(full_backward_kernel, with_self), (streams,...  34.6 us
    unnamed x648, local copies, waits for them, and re-layouts  32.2 us
    dot_general x11, matrix products, weight_grad(): return jnp.einsum('gsd,gsf->df', rows, grads, preferred_element_type=WIDE)  26.1 us
  transfers between devices with their start and end apart: 85, of which 31 were waited for; matrix products, arithmetic and copies ran while one was open for 27% of the time, Pallas kernels for 36%

profile of v2, /device:TPU:0, one launch (start us, length us, event | category | flops | bytes accessed | tf_op | source)
XLA Modules:
  0.0 823.4 jit_solution(3522975135828754916)
XLA Ops:
  37.0 7.1 shard_map.575
  46.8 7.5 collective-permute-start.4
  58.7 6.9 collective-permute-done.4.refs_2_.refs_5_
  114.2 6.8 collective-permute-start.13
  129.1 14.6 %collective-permute-done.13.before_ref = bf16[2,512,256]{2,1,0:T(8,128)(2,1)S(1)} collective-permute-done((bf16[2,512,256]{2,1,0:T(8,128)(2,1)S(1)}, bf16[2,512,256]{2,1,0:T(8,128)(2,1)S(1)}, u32[]{:S(2)}, u32[]{:S(2)}) %collective-permute-start.13) | collective-permute-done | bytes 524320 | tf_op jit(solution)/shard_map/ppermute | solution.py:979
  187.7 9.1 %collective-permute-done.26 = bf16[1,256,1024]{2,1,0:T(8,128)(2,1)S(1)} collective-permute-done((bf16[1,256,1024]{2,1,0:T(8,128)(2,1)S(1)}, bf16[1,256,1024]{2,1,0:T(8,128)(2,1)S(1)}, u32[]{:S(2)}, u32[]{:S(2)}) %collective-permute-start.26) | collective-permute-done | bytes 524320 | tf_op jit(solution)/shard_map/ppermute | solution.py:899
  203.3 9.1 %collective-permute-done.28 = bf16[1,256,1024]{2,1,0:T(8,128)(2,1)S(1)} collective-permute-done((bf16[1,256,1024]{2,1,0:T(8,128)(2,1)S(1)}, bf16[1,256,1024]{2,1,0:T(8,128)(2,1)S(1)}, u32[]{:S(2)}, u32[]{:S(2)}) %collective-permute-start.28) | collective-permute-done | bytes 524320 | tf_op jit(solution)/shard_map/ppermute | solution.py:899
  219.2 9.2 %collective-permute-done.27 = bf16[1,256,1024]{2,1,0:T(8,128)(2,1)S(1)} collective-permute-done((bf16[1,256,1024]{2,1,0:T(8,128)(2,1)S(1)}, bf16[1,256,1024]{2,1,0:T(8,128)(2,1)S(1)}, u32[]{:S(2)}, u32[]{:S(2)}) %collective-permute-start.27) | collective-permute-done | bytes 524320 | tf_op jit(solution)/shard_map/ppermute | solution.py:899
  236.8 8.6 %collective-permute-done.33 = bf16[1,256,1024]{2,1,0:T(8,128)(2,1)S(1)} collective-permute-done((bf16[1,256,1024]{2,1,0:T(8,128)(2,1)S(1)}, bf16[1,256,1024]{2,1,0:T(8,128)(2,1)S(1)}, u32[]{:S(2)}, u32[]{:S(2)}) %collective-permute-start.33) | collective-permute-done | bytes 524320 | tf_op jit(solution)/shard_map/ppermute | solution.py:899
  255.1 8.7 %collective-permute-done.37 = bf16[1,256,1024]{2,1,0:T(8,128)(2,1)S(1)} collective-permute-done((bf16[1,256,1024]{2,1,0:T(8,128)(2,1)S(1)}, bf16[1,256,1024]{2,1,0:T(8,128)(2,1)S(1)}, u32[]{:S(2)}, u32[]{:S(2)}) %collective-permute-start.37) | collective-permute-done | bytes 524320 | tf_op jit(solution)/shard_map/ppermute | solution.py:899
  296.9 8.5 %shard_map.582 = (bf16[1,512,256]{2,1,0:T(8,128)(2,1)S(1)}, bf16[2,512,256]{2,1,0:T(8,128)(2,1)S(1)}, f32[2,512,256]{2,1,0:T(8,128)S(1)}, bf16[2,512,256]{2,1,0:T(8,128)(2,1)S(1)}) custom-call(s32[2,4]{1,0:T(2,128)S(1)} %pad_add_fusion.bounds_ref, bf16[1,512,256]{2,1,0:T(8,128)(2,1)S(1)} %copy-done.15, bf16[1,512,256]{2,1,0:T(8,128)(2,1)S(1)} %pad_maximum_fusion.7.grad_ref, ...), custom_call_target="tpu_custom_call" | custom-call | flops 1000 | bytes 1000 | tf_op jit(solution)/shard_map/pallas_call | solution.py:544
  314.2 9.9 %collective-permute-done.46 = bf16[1,256,1024]{2,1,0:T(8,128)(2,1)} collective-permute-done((bf16[1,256,1024]{2,1,0:T(8,128)(2,1)}, bf16[1,256,1024]{2,1,0:T(8,128)(2,1)}, u32[]{:S(2)}, u32[]{:S(2)}) %collective-permute-start.46) | collective-permute-done | bytes 524320 | tf_op jit(solution)/shard_map/ppermute | solution.py:899
  330.0 8.3 %shard_map.583 = (bf16[1,512,256]{2,1,0:T(8,128)(2,1)S(1)}, bf16[2,512,256]{2,1,0:T(8,128)(2,1)S(1)}, f32[2,512,256]{2,1,0:T(8,128)S(1)}, bf16[2,512,256]{2,1,0:T(8,128)(2,1)S(1)}) custom-call(s32[2,4]{1,0:T(2,128)S(1)} %pad_add_fusion.bounds_ref, bf16[1,512,256]{2,1,0:T(8,128)(2,1)S(1)} %copy-done.13, bf16[1,512,256]{2,1,0:T(8,128)(2,1)S(1)} %pad_maximum_fusion.8.grad_ref, ...), custom_call_target="tpu_custom_call" | custom-call | flops 1000 | bytes 1000 | tf_op jit(solution)/shard_map/pallas_call | solution.py:544
  345.7 8.3 %shard_map.584 = (bf16[1,512,256]{2,1,0:T(8,128)(2,1)S(1)}, bf16[2,512,256]{2,1,0:T(8,128)(2,1)S(1)}, f32[2,512,256]{2,1,0:T(8,128)S(1)}, bf16[2,512,256]{2,1,0:T(8,128)(2,1)S(1)}) custom-call(s32[2,4]{1,0:T(2,128)S(1)} %pad_add_fusion.bounds_ref, bf16[1,512,256]{2,1,0:T(8,128)(2,1)S(1)} %copy-done.11, bf16[1,512,256]{2,1,0:T(8,128)(2,1)S(1)} %pad_maximum_fusion.9.grad_ref, ...), custom_call_target="tpu_custom_call" | custom-call | flops 1000 | bytes 1000 | tf_op jit(solution)/shard_map/pallas_call | solution.py:544
  355.8 17.2 %collective-permute-start.55 = (bf16[2,512,256]{2,1,0:T(8,128)(2,1)S(1)}, bf16[2,512,256]{2,1,0:T(8,128)(2,1)S(1)}, u32[]{:S(2)}, u32[]{:S(2)}) collective-permute-start(bf16[2,512,256]{2,1,0:T(8,128)(2,1)S(1)} %add_convert_fusion.20), channel_id=1, source_target_pairs={{0,4},{4,8},{8,12},{12,16},{16,20},{20,24},{24,28},{1,5},{5,9},{9,... | collective-permute-start | bytes 1572872 | tf_op jit(solution)/shard_map/ppermute | solution.py:979
  384.9 6.5 shard_map.585
  394.5 7.9 collective-permute-done.55
  409.8 8.2 shard_map.586
  430.3 10.3 %collective-permute-done.60 = bf16[1,256,1024]{2,1,0:T(8,128)(2,1)} collective-permute-done((bf16[1,256,1024]{2,1,0:T(8,128)(2,1)}, bf16[1,256,1024]{2,1,0:T(8,128)(2,1)}, u32[]{:S(2)}, u32[]{:S(2)}) %collective-permute-start.60) | collective-permute-done | bytes 524320 | tf_op jit(solution)/shard_map/ppermute | solution.py:899
  460.7 8.2 shard_map.587
  485.6 9.6 %shard_map.588 = (bf16[1,512,256]{2,1,0:T(8,128)(2,1)S(1)}, bf16[2,512,256]{2,1,0:T(8,128)(2,1)S(1)}, f32[2,512,256]{2,1,0:T(8,128)S(1)}, bf16[2,512,256]{2,1,0:T(8,128)(2,1)S(1)}) custom-call(s32[2,4]{1,0:T(2,128)S(1)} %pad_add_fusion.bounds_ref, bf16[1,512,256]{2,1,0:T(8,128)(2,1)S(1)} %copy-done.32, bf16[1,512,256]{2,1,0:T(8,128)(2,1)S(1)} %pad_maximum_fusion.13.grad_ref, ...), custom_call_target="tpu_custom_call" | custom-call | flops 1000 | bytes 1000 | tf_op jit(solution)/shard_map/pallas_call | solution.py:544
  496.6 13.5 %collective-permute-start.76 = (bf16[2,512,256]{2,1,0:T(8,128)(2,1)S(1)}, bf16[2,512,256]{2,1,0:T(8,128)(2,1)S(1)}, u32[]{:S(2)}, u32[]{:S(2)}) collective-permute-start(bf16[2,512,256]{2,1,0:T(8,128)(2,1)S(1)} %get-tuple-element.557), channel_id=1, source_target_pairs={{0,4},{4,8},{8,12},{12,16},{16,20},{20,24},{24,28},{1,5},{5,9},{9,... | collective-permute-start | bytes 1572872 | tf_op jit(solution)/shard_map/ppermute | solution.py:979
  527.8 12.3 %collective-permute-done.76 = bf16[2,512,256]{2,1,0:T(8,128)(2,1)S(1)} collective-permute-done((bf16[2,512,256]{2,1,0:T(8,128)(2,1)S(1)}, bf16[2,512,256]{2,1,0:T(8,128)(2,1)S(1)}, u32[]{:S(2)}, u32[]{:S(2)}) %collective-permute-start.76) | collective-permute-done | bytes 524320 | tf_op jit(solution)/shard_map/ppermute | solution.py:979
  552.9 210.0 %shard_map.589 = bf16[67,64,1024]{2,1,0:T(8,128)(2,1)} custom-call(bf16[16,64,1024]{2,1,0:T(8,128)(2,1)} %bitcast.748, bf16[16,64,1024]{2,1,0:T(8,128)(2,1)} %bitcast.749, bf16[4,64,1024]{2,1,0:T(8,128)(2,1)} %bitcast.759, bf16[2,64,1024]{2,1,0:T(8,128)(2,1)} %bitcast.755, bf16[4,64,1024]{2,1,0:T(8,128)(2,1)} %bitcast.758, bf16[8,64,1024]{2,1,0:T(8,128)(2,1)} %bitcast.756, ...), custom_call_target="tpu_custom_call" | custom-call | flops 1000 | bytes 1000 | tf_op jit(solution)/shard_map/pallas_call | solution.py:843
  (1151 shorter events, 377.6 us)
Async XLA Ops:
  7.2 762.4 %all-reduce.7.cloned.1.call-start = ((), (), s32[]{:S(2)}) async-start(), calls=%async_computation | async-start | bytes 8388608 | tf_op jit(solution)/shard_map/psum | solution.py:998
  9.7 27.3 %collective-permute-start = (bf16[2,512,256]{2,1,0:T(8,128)(2,1)S(1)}, bf16[2,512,256]{2,1,0:T(8,128)(2,1)S(1)}, u32[]{:S(2)}, u32[]{:S(2)}) collective-permute-start(bf16[2,512,256]{2,1,0:T(8,128)(2,1)S(1)} %fusion.83.here_ref), channel_id=1, source_target_pairs={{0,4},{4,8},{8,12},{12,16},{16,20},{20,24},{24,28},{1,5},{5,9},{9,... | collective-permute-start | bytes 1572872 | tf_op jit(solution)/shard_map/ppermute | solution.py:979
  14.6 22.4 %collective-permute-start.1 = (bf16[2,512,256]{2,1,0:T(8,128)(2,1)S(1)}, bf16[2,512,256]{2,1,0:T(8,128)(2,1)}, u32[]{:S(2)}, u32[]{:S(2)}) collective-permute-start(bf16[2,512,256]{2,1,0:T(8,128)(2,1)S(1)} %fusion.83.here_ref), channel_id=1, source_target_pairs={{4,0},{8,4},{12,8},{16,12},{20,16},{24,20},{28,24},{5,1},{9,5},{13... | collective-permute-start | bytes 1572872 | tf_op jit(solution)/shard_map/ppermute | solution.py:979
  100.8 21.5 %collective-permute-start.12 = (bf16[1,256,1024]{2,1,0:T(8,128)(2,1)}, bf16[1,256,1024]{2,1,0:T(8,128)(2,1)}, u32[]{:S(2)}, u32[]{:S(2)}) collective-permute-start(bf16[1,256,1024]{2,1,0:T(8,128)(2,1)} %fusion.86), channel_id=1, source_target_pairs={{0,1},{1,0},{2,3},{3,2},{4,5},{5,4},{6,7},{7,6},{8,9},{9,8},{10,11... | collective-permute-start | bytes 1572872 | tf_op jit(solution)/shard_map/ppermute | solution.py:893
  114.2 29.4 %collective-permute-start.13 = (bf16[2,512,256]{2,1,0:T(8,128)(2,1)S(1)}, bf16[2,512,256]{2,1,0:T(8,128)(2,1)S(1)}, u32[]{:S(2)}, u32[]{:S(2)}) collective-permute-start(bf16[2,512,256]{2,1,0:T(8,128)(2,1)S(1)} %fusion.74.here_ref), channel_id=1, source_target_pairs={{0,4},{4,8},{8,12},{12,16},{16,20},{20,24},{24,28},{1,5},{5,9},{9,... | collective-permute-start | bytes 1572872 | tf_op jit(solution)/shard_map/ppermute | solution.py:979
  121.0 22.6 %collective-permute-start.14 = (bf16[2,512,256]{2,1,0:T(8,128)(2,1)S(1)}, bf16[2,512,256]{2,1,0:T(8,128)(2,1)S(1)}, u32[]{:S(2)}, u32[]{:S(2)}) collective-permute-start(bf16[2,512,256]{2,1,0:T(8,128)(2,1)S(1)} %fusion.74.here_ref), channel_id=1, source_target_pairs={{4,0},{8,4},{12,8},{16,12},{20,16},{24,20},{28,24},{5,1},{9,5},{13... | collective-permute-start | bytes 1572872 | tf_op jit(solution)/shard_map/ppermute | solution.py:979
  125.4 25.0 %collective-permute-start.17 = (bf16[1,256,1024]{2,1,0:T(8,128)(2,1)S(1)}, bf16[1,256,1024]{2,1,0:T(8,128)(2,1)S(1)}, u32[]{:S(2)}, u32[]{:S(2)}) collective-permute-start(bf16[1,256,1024]{2,1,0:T(8,128)(2,1)S(1)} %add_convert_fusion.36), channel_id=1, source_target_pairs={{0,2},{1,3},{2,0},{3,1},{4,6},{5,7},{6,4},{7,5},{8,10},{9,11},{10,... | collective-permute-start | bytes 1572872 | tf_op jit(solution)/shard_map/ppermute | solution.py:899
  310.4 459.3 %all-reduce.9.cloned.1.call-start = ((), (), s32[]{:S(2)}) async-start(), calls=%async_computation.1 | async-start | bytes 4194304 | tf_op jit(solution)/shard_map/psum | solution.py:998
  310.8 28.2 %collective-permute-start.45 = (bf16[1,256,1024]{2,1,0:T(8,128)(2,1)}, bf16[1,256,1024]{2,1,0:T(8,128)(2,1)S(1)}, u32[]{:S(2)}, u32[]{:S(2)}) collective-permute-start(bf16[1,256,1024]{2,1,0:T(8,128)(2,1)} %add_convert_fusion.23), channel_id=1, source_target_pairs={{0,2},{1,3},{2,0},{3,1},{4,6},{5,7},{6,4},{7,5},{8,10},{9,11},{10,... | collective-permute-start | bytes 1572872 | tf_op jit(solution)/shard_map/ppermute | solution.py:899
  327.8 49.7 %collective-permute-start.56 = (bf16[1,256,1024]{2,1,0:T(8,128)(2,1)S(1)}, bf16[1,256,1024]{2,1,0:T(8,128)(2,1)S(1)}, u32[]{:S(2)}, u32[]{:S(2)}) collective-permute-start(bf16[1,256,1024]{2,1,0:T(8,128)(2,1)S(1)} %add_convert_fusion.22), channel_id=1, source_target_pairs={{0,2},{1,3},{2,0},{3,1},{4,6},{5,7},{6,4},{7,5},{8,10},{9,11},{10,... | collective-permute-start | bytes 1572872 | tf_op jit(solution)/shard_map/ppermute | solution.py:899
  343.1 30.2 %collective-permute-start.40 = (bf16[1,256,1024]{2,1,0:T(8,128)(2,1)S(1)}, bf16[1,256,1024]{2,1,0:T(8,128)(2,1)S(1)}, u32[]{:S(2)}, u32[]{:S(2)}) collective-permute-start(bf16[1,256,1024]{2,1,0:T(8,128)(2,1)S(1)} %get-tuple-element.780), channel_id=1, source_target_pairs={{0,1},{1,0},{2,3},{3,2},{4,5},{5,4},{6,7},{7,6},{8,9},{9,8},{10,11... | collective-permute-start | bytes 1572872 | tf_op jit(solution)/shard_map/ppermute | solution.py:893
  354.7 48.9 %collective-permute-start.59 = (bf16[1,256,1024]{2,1,0:T(8,128)(2,1)S(1)}, bf16[1,256,1024]{2,1,0:T(8,128)(2,1)S(1)}, u32[]{:S(2)}, u32[]{:S(2)}) collective-permute-start(bf16[1,256,1024]{2,1,0:T(8,128)(2,1)S(1)} %add_convert_fusion.21), channel_id=1, source_target_pairs={{0,2},{1,3},{2,0},{3,1},{4,6},{5,7},{6,4},{7,5},{8,10},{9,11},{10,... | collective-permute-start | bytes 1572872 | tf_op jit(solution)/shard_map/ppermute | solution.py:899
  355.8 46.7 %collective-permute-start.55 = (bf16[2,512,256]{2,1,0:T(8,128)(2,1)S(1)}, bf16[2,512,256]{2,1,0:T(8,128)(2,1)S(1)}, u32[]{:S(2)}, u32[]{:S(2)}) collective-permute-start(bf16[2,512,256]{2,1,0:T(8,128)(2,1)S(1)} %add_convert_fusion.20), channel_id=1, source_target_pairs={{0,4},{4,8},{8,12},{12,16},{16,20},{20,24},{24,28},{1,5},{5,9},{9,... | collective-permute-start | bytes 1572872 | tf_op jit(solution)/shard_map/ppermute | solution.py:979
  373.3 29.2 %collective-permute-start.54 = (bf16[2,512,256]{2,1,0:T(8,128)(2,1)S(1)}, bf16[2,512,256]{2,1,0:T(8,128)(2,1)S(1)}, u32[]{:S(2)}, u32[]{:S(2)}) collective-permute-start(bf16[2,512,256]{2,1,0:T(8,128)(2,1)S(1)} %add_convert_fusion.18), channel_id=1, source_target_pairs={{4,0},{8,4},{12,8},{16,12},{20,16},{24,20},{28,24},{5,1},{9,5},{13... | collective-permute-start | bytes 1572872 | tf_op jit(solution)/shard_map/ppermute | solution.py:979
  406.2 37.3 %collective-permute-start.53 = (bf16[1,256,1024]{2,1,0:T(8,128)(2,1)}, bf16[1,256,1024]{2,1,0:T(8,128)(2,1)}, u32[]{:S(2)}, u32[]{:S(2)}) collective-permute-start(bf16[1,256,1024]{2,1,0:T(8,128)(2,1)} %add_convert_fusion.19), channel_id=1, source_target_pairs={{0,2},{1,3},{2,0},{3,1},{4,6},{5,7},{6,4},{7,5},{8,10},{9,11},{10,... | collective-permute-start | bytes 1572872 | tf_op jit(solution)/shard_map/ppermute | solution.py:899
  427.6 82.6 %collective-permute-start.68 = (bf16[1,256,1024]{2,1,0:T(8,128)(2,1)}, bf16[1,256,1024]{2,1,0:T(8,128)(2,1)}, u32[]{:S(2)}, u32[]{:S(2)}) collective-permute-start(bf16[1,256,1024]{2,1,0:T(8,128)(2,1)} %add_convert_fusion.15), channel_id=1, source_target_pairs={{0,2},{1,3},{2,0},{3,1},{4,6},{5,7},{6,4},{7,5},{8,10},{9,11},{10,... | collective-permute-start | bytes 1572872 | tf_op jit(solution)/shard_map/ppermute | solution.py:899
  474.7 37.3 %collective-permute-start.72 = (bf16[2,512,256]{2,1,0:T(8,128)(2,1)}, bf16[2,512,256]{2,1,0:T(8,128)(2,1)}, u32[]{:S(2)}, u32[]{:S(2)}) collective-permute-start(bf16[2,512,256]{2,1,0:T(8,128)(2,1)} %add_convert_fusion.13), channel_id=1, source_target_pairs={{4,0},{8,4},{12,8},{16,12},{20,16},{24,20},{28,24},{5,1},{9,5},{13... | collective-permute-start | bytes 1572872 | tf_op jit(solution)/shard_map/ppermute | solution.py:979
  483.1 35.6 %collective-permute-start.67 = (bf16[1,256,1024]{2,1,0:T(8,128)(2,1)S(1)}, bf16[1,256,1024]{2,1,0:T(8,128)(2,1)S(1)}, u32[]{:S(2)}, u32[]{:S(2)}) collective-permute-start(bf16[1,256,1024]{2,1,0:T(8,128)(2,1)S(1)} %copy-done.231), channel_id=1, source_target_pairs={{0,2},{1,3},{2,0},{3,1},{4,6},{5,7},{6,4},{7,5},{8,10},{9,11},{10,... | collective-permute-start | bytes 1572872 | tf_op jit(solution)/shard_map/ppermute | solution.py:899
  495.2 32.6 %collective-permute-start.75 = (bf16[2,512,256]{2,1,0:T(8,128)(2,1)S(1)}, bf16[2,512,256]{2,1,0:T(8,128)(2,1)S(1)}, u32[]{:S(2)}, u32[]{:S(2)}) collective-permute-start(bf16[2,512,256]{2,1,0:T(8,128)(2,1)S(1)} %get-tuple-element.556), channel_id=1, source_target_pairs={{4,0},{8,4},{12,8},{16,12},{20,16},{24,20},{28,24},{5,1},{9,5},{13... | collective-permute-start | bytes 1572872 | tf_op jit(solution)/shard_map/ppermute | solution.py:979
  496.6 43.5 %collective-permute-start.76 = (bf16[2,512,256]{2,1,0:T(8,128)(2,1)S(1)}, bf16[2,512,256]{2,1,0:T(8,128)(2,1)S(1)}, u32[]{:S(2)}, u32[]{:S(2)}) collective-permute-start(bf16[2,512,256]{2,1,0:T(8,128)(2,1)S(1)} %get-tuple-element.557), channel_id=1, source_target_pairs={{0,4},{4,8},{8,12},{12,16},{16,20},{20,24},{24,28},{1,5},{5,9},{9,... | collective-permute-start | bytes 1572872 | tf_op jit(solution)/shard_map/ppermute | solution.py:979
  511.9 33.5 %collective-permute-start.71 = (bf16[1,256,1024]{2,1,0:T(8,128)(2,1)S(1)}, bf16[1,256,1024]{2,1,0:T(8,128)(2,1)S(1)}, u32[]{:S(2)}, u32[]{:S(2)}) collective-permute-start(bf16[1,256,1024]{2,1,0:T(8,128)(2,1)S(1)} %add_convert_fusion.11), channel_id=1, source_target_pairs={{0,1},{1,0},{2,3},{3,2},{4,5},{5,4},{6,7},{7,6},{8,9},{9,8},{10,11... | collective-permute-start | bytes 1572872 | tf_op jit(solution)/shard_map/ppermute | solution.py:893
  519.0 26.5 %collective-permute-start.74 = (bf16[1,256,1024]{2,1,0:T(8,128)(2,1)S(1)}, bf16[1,256,1024]{2,1,0:T(8,128)(2,1)S(1)}, u32[]{:S(2)}, u32[]{:S(2)}) collective-permute-start(bf16[1,256,1024]{2,1,0:T(8,128)(2,1)S(1)} %add_convert_fusion.8), channel_id=1, source_target_pairs={{0,1},{1,0},{2,3},{3,2},{4,5},{5,4},{6,7},{7,6},{8,9},{9,8},{10,11... | collective-permute-start | bytes 1572872 | tf_op jit(solution)/shard_map/ppermute | solution.py:893
  521.5 269.1 %collective-permute-start.77 = (bf16[1,256,1024]{2,1,0:T(8,128)(2,1)}, bf16[1,256,1024]{2,1,0:T(8,128)(2,1)}, u32[]{:S(2)}, u32[]{:S(2)}) collective-permute-start(bf16[1,256,1024]{2,1,0:T(8,128)(2,1)} %add_convert_fusion.9), channel_id=1, source_target_pairs={{0,2},{1,3},{2,0},{3,1},{4,6},{5,7},{6,4},{7,5},{8,10},{9,11},{10,... | collective-permute-start | bytes 1572872 | tf_op jit(solution)/shard_map/ppermute | solution.py:899
  767.4 42.2 %collective-permute-start.80 = (bf16[1,256,1024]{2,1,0:T(8,128)(2,1)}, bf16[1,256,1024]{2,1,0:T(8,128)(2,1)}, u32[]{:S(2)}, u32[]{:S(2)}) collective-permute-start(bf16[1,256,1024]{2,1,0:T(8,128)(2,1)} %add_convert_fusion.5), channel_id=1, source_target_pairs={{0,2},{1,3},{2,0},{3,1},{4,6},{5,7},{6,4},{7,5},{8,10},{9,11},{10,... | collective-permute-start | bytes 1572872 | tf_op jit(solution)/shard_map/ppermute | solution.py:899
  (366 other events, 2596.6 us)
Sparse Core Ops, SparseCore 0:
  310.5 178.9 all-reduce.6
  494.0 150.5 all-reduce.8

commit v3 on v2

--- a/solution.py
+++ b/solution.py
@@ -654,25 +654,33 @@
     )(*operands)
 
 
-SUM_ROWS = 64
-SUM_WIDTH = 1024
+SUM_ROWS = 256
+SUM_WIDTH = 256
 SUM_DELAY = 3
 MESH = pl.DeviceIdType.MESH
 
 
-def tree_kernel(count, *refs):
-    out_ref, x_ref, total, part, landed, sent_up, came_up, sent_down, came_down, filled = refs[-10:]
-    chunks = x_ref.shape[0]
-    fills, at = [], 0
-    for place, piece in enumerate(refs[:-10]):
-        size = piece.shape[0]
-        fills.append(
-            pltpu.make_async_copy(piece, x_ref.at[pl.ds(at, size)], filled.at[place])
-        )
-        at += size
+def blocks_of(shape):
+    return [(shape[0], column) for column in range(0, shape[1], SUM_WIDTH)]
+
+
+def tree_kernel(count, pieces, *refs):
+    sources, targets, refs = refs[:pieces], refs[pieces : 2 * pieces], refs[2 * pieces :]
+    x_ref, out_ref, total, part, landed, sent_up, came_up, sent_down, came_down, filled = refs
+    chunks = x_ref.shape[0] // SUM_ROWS
+    ring = part.shape[0]
+    fills, drains, at = [], [], 0
+    for place, (source, target) in enumerate(zip(sources, targets)):
+        for rows, column in blocks_of(source.shape):
+            columns = pl.ds(column, SUM_WIDTH)
+            inside, outside = pl.ds(at, rows), filled.at[len(fills)]
+            fills.append(pltpu.make_async_copy(source.at[:, columns], x_ref.at[inside], outside))
+            drains.append(pltpu.make_async_copy(out_ref.at[inside], target.at[:, columns], outside))
+            at += rows
+    if at < x_ref.shape[0]:
+        x_ref[at:, :] = jnp.zeros((x_ref.shape[0] - at, SUM_WIDTH), LOW)
     for fill in fills:
         fill.start()
-    ring = part.shape[0]
     tall = count // 2
     place = lax.axis_index("seq")
     column = lax.rem(place, 2)
@@ -722,6 +730,9 @@
 
     devices = (beside, place - 2, place + 2)
 
+    def rows_at(chunk):
+        return pl.ds(pl.multiple_of(chunk * SUM_ROWS, SUM_ROWS), SUM_ROWS)
+
     def up_copy(chunk, slot, device):
         at = lax.rem(chunk, ring)
         return pltpu.make_async_remote_copy(
@@ -736,8 +747,8 @@
     def down_copy(chunk, slot, device):
         at = lax.rem(chunk, ring)
         return pltpu.make_async_remote_copy(
-            src_ref=out_ref.at[chunk],
-            dst_ref=out_ref.at[chunk],
+            src_ref=out_ref.at[rows_at(chunk)],
+            dst_ref=out_ref.at[rows_at(chunk)],
             send_sem=sent_down.at[at, slot],
             recv_sem=came_down.at[at],
             device_id={"seq": device},
@@ -753,7 +764,7 @@
 
     def climb(chunk, children, root, sideways, rising):
         at = lax.rem(chunk, ring)
-        total[...] = x_ref[chunk].astype(WIDE)
+        total[...] = x_ref[rows_at(chunk), :].astype(WIDE)
         for slot, child in enumerate(children):
 
             @pl.when(child)
@@ -763,7 +774,7 @@
 
         @pl.when(root)
         def _():
-            out_ref[chunk] = total[...].astype(LOW)
+            out_ref[rows_at(chunk), :] = total[...].astype(LOW)
             spread(chunk, children)
 
         @pl.when(jnp.logical_not(root))
@@ -833,20 +844,27 @@
         return carry
 
     lax.fori_loop(0, chunks + SUM_DELAY * (2 * levels + 1), period, 0)
+    for drain in drains:
+        drain.start()
+    for drain in drains:
+        drain.wait()
 
 
 def link_sum(pieces, count):
     levels = count // 2 + 1
-    chunks = sum(piece.shape[0] for piece in pieces)
+    blocks = [block for piece in pieces for block in blocks_of(piece.shape)]
+    chunks = -(-sum(rows for rows, _ in blocks) // SUM_ROWS)
     ring = min(chunks, SUM_DELAY * (2 * levels + 1) + 1)
     block = (SUM_ROWS, SUM_WIDTH)
+    anywhere = [pl.BlockSpec(memory_space=pl.ANY)] * len(pieces)
     return pl.pallas_call(
-        functools.partial(tree_kernel, count),
-        in_specs=[pl.BlockSpec(memory_space=pl.ANY)] * len(pieces),
-        out_specs=pl.BlockSpec(memory_space=pltpu.VMEM),
-        out_shape=shaped((chunks,) + block, LOW),
+        functools.partial(tree_kernel, count, len(pieces)),
+        in_specs=anywhere,
+        out_specs=anywhere,
+        out_shape=[shaped(piece.shape, LOW) for piece in pieces],
         scratch_shapes=[
-            pltpu.VMEM((chunks,) + block, LOW),
+            pltpu.VMEM((chunks * SUM_ROWS, SUM_WIDTH), LOW),
+            pltpu.VMEM((chunks * SUM_ROWS, SUM_WIDTH), LOW),
             pltpu.VMEM(block, WIDE),
             pltpu.VMEM((ring,) + block, LOW),
             pltpu.VMEM((ring, 3) + block, LOW),
@@ -854,7 +872,7 @@
             pltpu.SemaphoreType.DMA((ring, 3)),
             pltpu.SemaphoreType.DMA((ring, 3)),
             pltpu.SemaphoreType.DMA((ring,)),
-            pltpu.SemaphoreType.DMA((len(pieces),)),
+            pltpu.SemaphoreType.DMA((len(blocks),)),
         ],
         compiler_params=pltpu.CompilerParams(
             collective_id=0, has_side_effects=True, vmem_limit_bytes=56 * 1024 * 1024
@@ -1388,22 +1406,27 @@
         weights.enc = [down, up]
         yield
 
-    def turned(cells):
-        return jnp.swapaxes(cells, -1, -2)
+    def flat(cells):
+        if cells.shape[-1] % SUM_WIDTH:
+            cells = jnp.swapaxes(cells, -1, -2)
+        return cells.reshape(-1, cells.shape[-1])
+
+    def unflat(cells, shape):
+        if shape[-1] % SUM_WIDTH:
+            return jnp.swapaxes(cells.reshape(shape[:-2] + (shape[-1], shape[-2])), -1, -2)
+        return cells.reshape(shape)
 
     def self_weights():
         atts, grads = enter([kept.self_att for kept in dec], [kept.self_rows for kept in dec])
         wout = rows_weight_grad(atts, grads).astype(LOW)
         tables = jnp.concatenate([kept.table_grad for kept in dec], 0)
-        rel = weight_grad(tables, dec_input).astype(LOW)
+        rel = weight_grad(dec_input, tables).astype(LOW)
         queries = jnp.concatenate([kept.query_grad for kept in dec])
-        query = weight_grad(queries, dec_input).astype(LOW)
-        pairs = jnp.stack([kept.pair_grad for kept in dec])
-        pair = jnp.einsum(
-            "gsd,gcsf->cfd", dec_input, pairs, preferred_element_type=WIDE
-        ).astype(LOW)
-        leave((wout, rel, query, pair))
-        weights.self = [wout, rel, query, pair]
+        query = weight_grad(dec_input, queries).astype(LOW)
+        sides = [jnp.stack([kept.pair_grad[side] for kept in dec]) for side in range(2)]
+        key, value = [weight_grad(dec_input, side).astype(LOW) for side in sides]
+        leave((wout, rel, query, key, value))
+        weights.self = [wout, rel, query, key, value]
         yield
 
     def finished():
@@ -1414,10 +1437,9 @@
 
     def enc_weights():
         query_grad, pair_grad, grads = enter(enc.query_grad, enc.pair_grad, enc.att_rows)
-        query = weight_grad(query_grad, straight_rows).astype(LOW)
-        pair = jnp.einsum(
-            "sd,csf->cfd", enc_input, pair_grad, preferred_element_type=WIDE
-        ).astype(LOW)
+        query = weight_grad(straight_rows, query_grad).astype(LOW)
+        key = weight_grad(straight_rows, pair_grad[:1]).astype(LOW)
+        value = weight_grad(straight_rows, pair_grad[1:]).astype(LOW)
         wout = rows_weight_grad([enc.att], [grads]).astype(LOW)
         sums = jnp.concatenate(
             [
@@ -1429,24 +1451,19 @@
             ],
             0,
         )
-        sums = (sums + swap_core(sums)).astype(LOW).reshape(-1, SUM_WIDTH)
-        padded = jnp.pad(sums, ((0, -sums.shape[0] % SUM_ROWS), (0, 0)))
-        parts = weights.enc + weights.self + [wout, query, pair]
-        pieces = [part.reshape(-1, SUM_ROWS, SUM_WIDTH) for part in parts + [padded]]
-        parts.append(sums)
-        leave((wout, query, pair, padded))
+        sums = sums + swap_core(sums)
+        sums = jnp.pad(sums, ((0, -sums.shape[0] % 16), (0, 0))).astype(LOW)
+        parts = weights.enc + weights.self + [wout, query, key, value, sums]
+        pieces = [flat(part) for part in parts]
+        leave((wout, query, key, value, sums))
         yield
         pieces = enter(*pieces)
         summed = link_sum(pieces, lax.axis_size("seq"))
-        leave(summed)
+        leave(summed[0])
         weights.ffn, weights.cross = enter(weights.ffn, weights.cross)
-        summed = summed.reshape(-1, SUM_WIDTH)
-        found, at = [], 0
-        for part in parts:
-            size = part.size // SUM_WIDTH
-            found.append(summed[at : at + size].astype(WIDE).reshape(part.shape))
-            at += size
-        weights.last = found
+        weights.last = [
+            unflat(cells.astype(WIDE), part.shape) for cells, part in zip(summed, parts)
+        ]
         yield
 
     tasks = {"e": encoder(), "F": ffn_weights(), "C": cross_weights()}
@@ -1463,11 +1480,10 @@
         value.astype(WIDE) for value in weights.cross
     ]
     enc_down_grad, enc_up_grad, *found = weights.last
-    self_wout_grad, self_rel_grad, query, pair, *found = found
-    self_qkv_grad = jnp.concatenate([turned(query)[None], turned(pair)], 0)
-    enc_wout_grad, query, pair, sums = found
-    enc_qkv_grad = jnp.concatenate([turned(query)[None], turned(pair)], 0)
-    sums = sums.reshape(-1, enc_input.shape[1])
+    self_wout_grad, self_rel_grad, *found = found
+    self_qkv_grad = jnp.stack(found[:3])
+    enc_wout_grad, sums = found[3], found[7]
+    enc_qkv_grad = jnp.stack(found[4:7])
     return (
         enc.final[0],
         weights.final,
@@ -1482,7 +1498,7 @@
         sums[2],
         sums[3],
         self_qkv_grad,
-        self_rel_grad.T,
+        self_rel_grad,
         self_wout_grad,
         sums[4],
         sums[5],

time: 837 us -> 816 us (0.975)
  Pallas kernels: 309 us -> 329 us
  waiting for transfers between devices: 135 us -> 119 us
  local copies, waits for them, and re-layouts: 52.3 us -> 38.7 us
    ppermute x10, waiting for transfers between devices: 48.4 us -> 35.4 us  [passed_along(): return lax.ppermute(value, 'seq', pairs)]
    ppermute x10, starting transfers between devices: 56.9 us -> 48.3 us  [passed_along(): return lax.ppermute(value, 'seq', pairs)]
    dot_general x11 -> x15, matrix products: 26.1 us -> 34.5 us  [weight_grad(): return jnp.einsum('gsd,gsf->df', rows, grads, preferred_element_type=WIDE)]
    unnamed x648 -> x647, local copies, waits for them, and re-layouts: 32.2 us -> 31.6 us
  transfers between devices with their start and end apart: 85 -> 85, of which waited for: 31 -> 30; matrix products, arithmetic and copies ran while one was open for 27% -> 26% of each run, Pallas kernels for 36% -> 39%
where the time goes in v3:
time: 816 us; the launch traced here: 806 us
  Pallas kernels  329 us (40%)
  waiting for transfers between devices  119 us (15%)
  matrix products  118 us (14%)
  other arithmetic  97.1 us (12%)
  starting transfers between devices  83.4 us (10%)
  local copies, waits for them, and re-layouts  38.7 us (5%)
  between operations  19.7 us (2%)
    pallas_call x1, Pallas kernels, link_sum(): pl.pallas_call(functools.partial(tree_kernel, count, len(pieces)), in_spe...  218 us
    ppermute x23, waiting for transfers between devices, swap_chip(): lax.ppermute(low, 'tp', [(place, place ^ hop) for place in range(count)])  76.6 us
    ppermute x10, starting transfers between devices, passed_along(): return lax.ppermute(value, 'seq', pairs)  48.3 us
    pallas_call x4, Pallas kernels, full_backward(): local_call(functools.partial(full_backward_kernel, with_self), (streams,...  39.8 us
    dot_general x39, matrix products, project(): return jnp.einsum('gsd,df->gsf', rows, weight, preferred_element_type=WIDE)  38.1 us
    ppermute x10, waiting for transfers between devices, passed_along(): return lax.ppermute(value, 'seq', pairs)  35.4 us
    dot_general x15, matrix products, weight_grad(): return jnp.einsum('gsd,gsf->df', rows, grads, preferred_element_type=WIDE)  34.5 us
    unnamed x647, local copies, waits for them, and re-layouts  31.6 us
  transfers between devices with their start and end apart: 85, of which 30 were waited for; matrix products, arithmetic and copies ran while one was open for 26% of the time, Pallas kernels for 39%

profile of v3, /device:TPU:0, one launch (start us, length us, event | category | flops | bytes accessed | tf_op | source)
XLA Modules:
  0.0 805.8 jit_solution(276686126892090212)
XLA Ops:
  37.0 8.1 %shard_map.575 = (bf16[1,512,256]{2,1,0:T(8,128)(2,1)S(1)}, f32[1,512,256]{2,1,0:T(8,128)S(1)}, f32[1,512,128]{2,1,0:T(8,128)S(1)}) custom-call(s32[2,4]{1,0:T(2,128)S(1)} %pad_add_fusion.bounds_ref, bf16[1,512,256]{2,1,0:T(8,128)(2,1)S(1)} %copy-done.31, bf16[2,512,256]{2,1,0:T(8,128)(2,1)S(1)} %collective-permute-done.before_ref, ...), custom_call_target="tpu_custom_call" | custom-call | flops 1000 | bytes 1000 | tf_op jit(solution)/shard_map/pallas_call | solution.py:517
  114.7 7.9 collective-permute-start.13
  130.6 14.6 %collective-permute-done.13.before_ref = bf16[2,512,256]{2,1,0:T(8,128)(2,1)S(1)} collective-permute-done((bf16[2,512,256]{2,1,0:T(8,128)(2,1)S(1)}, bf16[2,512,256]{2,1,0:T(8,128)(2,1)S(1)}, u32[]{:S(2)}, u32[]{:S(2)}) %collective-permute-start.13) | collective-permute-done | bytes 524320 | tf_op jit(solution)/shard_map/ppermute | solution.py:997
  145.2 7.0 shard_map.579
  156.6 7.0 shard_map.580
  172.2 7.2 shard_map.581
  190.2 9.1 %collective-permute-done.26 = bf16[1,256,1024]{2,1,0:T(8,128)(2,1)S(1)} collective-permute-done((bf16[1,256,1024]{2,1,0:T(8,128)(2,1)S(1)}, bf16[1,256,1024]{2,1,0:T(8,128)(2,1)S(1)}, u32[]{:S(2)}, u32[]{:S(2)}) %collective-permute-start.26) | collective-permute-done | bytes 524320 | tf_op jit(solution)/shard_map/ppermute | solution.py:917
  205.7 9.1 %collective-permute-done.28 = bf16[1,256,1024]{2,1,0:T(8,128)(2,1)S(1)} collective-permute-done((bf16[1,256,1024]{2,1,0:T(8,128)(2,1)S(1)}, bf16[1,256,1024]{2,1,0:T(8,128)(2,1)S(1)}, u32[]{:S(2)}, u32[]{:S(2)}) %collective-permute-start.28) | collective-permute-done | bytes 524320 | tf_op jit(solution)/shard_map/ppermute | solution.py:917
  221.6 9.2 %collective-permute-done.27 = bf16[1,256,1024]{2,1,0:T(8,128)(2,1)S(1)} collective-permute-done((bf16[1,256,1024]{2,1,0:T(8,128)(2,1)S(1)}, bf16[1,256,1024]{2,1,0:T(8,128)(2,1)S(1)}, u32[]{:S(2)}, u32[]{:S(2)}) %collective-permute-start.27) | collective-permute-done | bytes 524320 | tf_op jit(solution)/shard_map/ppermute | solution.py:917
  239.2 8.7 %collective-permute-done.33 = bf16[1,256,1024]{2,1,0:T(8,128)(2,1)S(1)} collective-permute-done((bf16[1,256,1024]{2,1,0:T(8,128)(2,1)S(1)}, bf16[1,256,1024]{2,1,0:T(8,128)(2,1)S(1)}, u32[]{:S(2)}, u32[]{:S(2)}) %collective-permute-start.33) | collective-permute-done | bytes 524320 | tf_op jit(solution)/shard_map/ppermute | solution.py:917
  257.5 8.8 %collective-permute-done.37 = bf16[1,256,1024]{2,1,0:T(8,128)(2,1)S(1)} collective-permute-done((bf16[1,256,1024]{2,1,0:T(8,128)(2,1)S(1)}, bf16[1,256,1024]{2,1,0:T(8,128)(2,1)S(1)}, u32[]{:S(2)}, u32[]{:S(2)}) %collective-permute-start.37) | collective-permute-done | bytes 524320 | tf_op jit(solution)/shard_map/ppermute | solution.py:917
  299.2 9.8 %shard_map.582 = (bf16[1,512,256]{2,1,0:T(8,128)(2,1)S(1)}, bf16[2,512,256]{2,1,0:T(8,128)(2,1)S(1)}, f32[2,512,256]{2,1,0:T(8,128)S(1)}, bf16[2,512,256]{2,1,0:T(8,128)(2,1)S(1)}) custom-call(s32[2,4]{1,0:T(2,128)S(1)} %pad_add_fusion.bounds_ref, bf16[1,512,256]{2,1,0:T(8,128)(2,1)S(1)} %copy-done.15, bf16[1,512,256]{2,1,0:T(8,128)(2,1)S(1)} %pad_maximum_fusion.7.grad_ref, ...), custom_call_target="tpu_custom_call" | custom-call | flops 1000 | bytes 1000 | tf_op jit(solution)/shard_map/pallas_call | solution.py:544
  317.7 10.0 %collective-permute-done.46 = bf16[1,256,1024]{2,1,0:T(8,128)(2,1)} collective-permute-done((bf16[1,256,1024]{2,1,0:T(8,128)(2,1)}, bf16[1,256,1024]{2,1,0:T(8,128)(2,1)}, u32[]{:S(2)}, u32[]{:S(2)}) %collective-permute-start.46) | collective-permute-done | bytes 524320 | tf_op jit(solution)/shard_map/ppermute | solution.py:917
  333.4 9.6 %shard_map.583 = (bf16[1,512,256]{2,1,0:T(8,128)(2,1)S(1)}, bf16[2,512,256]{2,1,0:T(8,128)(2,1)S(1)}, f32[2,512,256]{2,1,0:T(8,128)S(1)}, bf16[2,512,256]{2,1,0:T(8,128)(2,1)S(1)}) custom-call(s32[2,4]{1,0:T(2,128)S(1)} %pad_add_fusion.bounds_ref, bf16[1,512,256]{2,1,0:T(8,128)(2,1)S(1)} %copy-done.13, bf16[1,512,256]{2,1,0:T(8,128)(2,1)S(1)} %pad_maximum_fusion.8.grad_ref, ...), custom_call_target="tpu_custom_call" | custom-call | flops 1000 | bytes 1000 | tf_op jit(solution)/shard_map/pallas_call | solution.py:544
  350.4 9.6 %shard_map.584 = (bf16[1,512,256]{2,1,0:T(8,128)(2,1)S(1)}, bf16[2,512,256]{2,1,0:T(8,128)(2,1)S(1)}, f32[2,512,256]{2,1,0:T(8,128)S(1)}, bf16[2,512,256]{2,1,0:T(8,128)(2,1)S(1)}) custom-call(s32[2,4]{1,0:T(2,128)S(1)} %pad_add_fusion.bounds_ref, bf16[1,512,256]{2,1,0:T(8,128)(2,1)S(1)} %copy-done.11, bf16[1,512,256]{2,1,0:T(8,128)(2,1)S(1)} %pad_maximum_fusion.9.grad_ref, ...), custom_call_target="tpu_custom_call" | custom-call | flops 1000 | bytes 1000 | tf_op jit(solution)/shard_map/pallas_call | solution.py:544
  361.7 9.6 %collective-permute-start.55 = (bf16[2,512,256]{2,1,0:T(8,128)(2,1)S(1)}, bf16[2,512,256]{2,1,0:T(8,128)(2,1)S(1)}, u32[]{:S(2)}, u32[]{:S(2)}) collective-permute-start(bf16[2,512,256]{2,1,0:T(8,128)(2,1)S(1)} %add_convert_fusion.20), channel_id=1, source_target_pairs={{0,4},{4,8},{8,12},{12,16},{16,20},{20,24},{24,28},{1,5},{5,9},{9,... | collective-permute-start | bytes 1572872 | tf_op jit(solution)/shard_map/ppermute | solution.py:997
  383.5 7.1 shard_map.585
  393.4 8.4 %collective-permute-done.55 = bf16[2,512,256]{2,1,0:T(8,128)(2,1)S(1)} collective-permute-done((bf16[2,512,256]{2,1,0:T(8,128)(2,1)S(1)}, bf16[2,512,256]{2,1,0:T(8,128)(2,1)S(1)}, u32[]{:S(2)}, u32[]{:S(2)}) %collective-permute-start.55) | collective-permute-done | bytes 524320 | tf_op jit(solution)/shard_map/ppermute | solution.py:997
  409.8 8.7 %shard_map.586 = (bf16[1,512,256]{2,1,0:T(8,128)(2,1)S(1)}, bf16[1,512,128]{2,1,0:T(8,128)(2,1)S(1)}, bf16[2,512,256]{2,1,0:T(8,128)(2,1)S(1)}, f32[2,512,256]{2,1,0:T(8,128)S(1)}, bf16[1,2,512,256]{3,2,1,0:T(8,128)(2,1)S(1)}) custom-call(s32[4]{0:T(128)S(1)} %and_select_fusion.1.refs_0_, bf16[1,512,256]{2,1,0:T(8,128)(2,1)S(1)} %copy-done.55, ...), custom_call_target="tpu_custom_call" | custom-call | flops 1000 | bytes 1000 | tf_op jit(solution)/shard_map/pallas_call | solution.py:641
  428.4 9.4 %collective-permute-done.60 = bf16[1,256,1024]{2,1,0:T(8,128)(2,1)} collective-permute-done((bf16[1,256,1024]{2,1,0:T(8,128)(2,1)}, bf16[1,256,1024]{2,1,0:T(8,128)(2,1)}, u32[]{:S(2)}, u32[]{:S(2)}) %collective-permute-start.60) | collective-permute-done | bytes 524320 | tf_op jit(solution)/shard_map/ppermute | solution.py:917
  458.2 8.8 %shard_map.587 = (bf16[1,512,256]{2,1,0:T(8,128)(2,1)S(1)}, bf16[1,512,128]{2,1,0:T(8,128)(2,1)S(1)}, bf16[2,512,256]{2,1,0:T(8,128)(2,1)S(1)}, f32[2,512,256]{2,1,0:T(8,128)S(1)}, bf16[1,2,512,256]{3,2,1,0:T(8,128)(2,1)S(1)}) custom-call(s32[4]{0:T(128)S(1)} %and_select_fusion.1.refs_0_, bf16[1,512,256]{2,1,0:T(8,128)(2,1)S(1)} %copy-done.53, ...), custom_call_target="tpu_custom_call" | custom-call | flops 1000 | bytes 1000 | tf_op jit(solution)/shard_map/pallas_call | solution.py:641
  484.5 10.9 %shard_map.588 = (bf16[1,512,256]{2,1,0:T(8,128)(2,1)S(1)}, bf16[2,512,256]{2,1,0:T(8,128)(2,1)S(1)}, f32[2,512,256]{2,1,0:T(8,128)S(1)}, bf16[2,512,256]{2,1,0:T(8,128)(2,1)S(1)}) custom-call(s32[2,4]{1,0:T(2,128)S(1)} %pad_add_fusion.bounds_ref, bf16[1,512,256]{2,1,0:T(8,128)(2,1)S(1)} %copy-done.32, bf16[1,512,256]{2,1,0:T(8,128)(2,1)S(1)} %pad_maximum_fusion.13.grad_ref, ...), custom_call_target="tpu_custom_call" | custom-call | flops 1000 | bytes 1000 | tf_op jit(solution)/shard_map/pallas_call | solution.py:544
  496.9 12.9 %collective-permute-start.76 = (bf16[2,512,256]{2,1,0:T(8,128)(2,1)S(1)}, bf16[2,512,256]{2,1,0:T(8,128)(2,1)S(1)}, u32[]{:S(2)}, u32[]{:S(2)}) collective-permute-start(bf16[2,512,256]{2,1,0:T(8,128)(2,1)S(1)} %get-tuple-element.571), channel_id=1, source_target_pairs={{0,4},{4,8},{8,12},{12,16},{16,20},{20,24},{24,28},{1,5},{5,9},{9,... | collective-permute-start | bytes 1572872 | tf_op jit(solution)/shard_map/ppermute | solution.py:997
  545.4 218.3 %shard_map.589 = (bf16[1024,1024]{1,0:T(8,128)(2,1)}, bf16[1024,1024]{1,0:T(8,128)(2,1)}, bf16[256,1024]{1,0:T(8,128)(2,1)}, bf16[128,1024]{1,0:T(8,128)(2,1)}, ...) custom-call(bf16[1024,1024]{1,0:T(8,128)(2,1)} %convolution_convert_, ...), custom_call_target="tpu_custom_call" | custom-call | flops 1000 | bytes 1000 | tf_op jit(solution)/shard_map/pallas_call | solution.py:860
  (1144 shorter events, 356.4 us)
Async XLA Ops:
  7.2 760.5 %all-reduce.7.cloned.1.call-start = ((), (), s32[]{:S(2)}) async-start(), calls=%async_computation | async-start | bytes 8388608 | tf_op jit(solution)/shard_map/psum | solution.py:1016
  9.7 27.3 %collective-permute-start = (bf16[2,512,256]{2,1,0:T(8,128)(2,1)S(1)}, bf16[2,512,256]{2,1,0:T(8,128)(2,1)S(1)}, u32[]{:S(2)}, u32[]{:S(2)}) collective-permute-start(bf16[2,512,256]{2,1,0:T(8,128)(2,1)S(1)} %fusion.76.here_ref), channel_id=1, source_target_pairs={{0,4},{4,8},{8,12},{12,16},{16,20},{20,24},{24,28},{1,5},{5,9},{9,... | collective-permute-start | bytes 1572872 | tf_op jit(solution)/shard_map/ppermute | solution.py:997
  14.6 22.4 %collective-permute-start.1 = (bf16[2,512,256]{2,1,0:T(8,128)(2,1)S(1)}, bf16[2,512,256]{2,1,0:T(8,128)(2,1)}, u32[]{:S(2)}, u32[]{:S(2)}) collective-permute-start(bf16[2,512,256]{2,1,0:T(8,128)(2,1)S(1)} %fusion.76.here_ref), channel_id=1, source_target_pairs={{4,0},{8,4},{12,8},{16,12},{20,16},{24,20},{28,24},{5,1},{9,5},{13... | collective-permute-start | bytes 1572872 | tf_op jit(solution)/shard_map/ppermute | solution.py:997
  101.0 22.9 %collective-permute-start.12 = (bf16[1,256,1024]{2,1,0:T(8,128)(2,1)}, bf16[1,256,1024]{2,1,0:T(8,128)(2,1)}, u32[]{:S(2)}, u32[]{:S(2)}) collective-permute-start(bf16[1,256,1024]{2,1,0:T(8,128)(2,1)} %fusion.79), channel_id=1, source_target_pairs={{0,1},{1,0},{2,3},{3,2},{4,5},{5,4},{6,7},{7,6},{8,9},{9,8},{10,11... | collective-permute-start | bytes 1572872 | tf_op jit(solution)/shard_map/ppermute | solution.py:911
  114.7 30.4 %collective-permute-start.13 = (bf16[2,512,256]{2,1,0:T(8,128)(2,1)S(1)}, bf16[2,512,256]{2,1,0:T(8,128)(2,1)S(1)}, u32[]{:S(2)}, u32[]{:S(2)}) collective-permute-start(bf16[2,512,256]{2,1,0:T(8,128)(2,1)S(1)} %fusion.67.here_ref), channel_id=1, source_target_pairs={{0,4},{4,8},{8,12},{12,16},{16,20},{20,24},{24,28},{1,5},{5,9},{9,... | collective-permute-start | bytes 1572872 | tf_op jit(solution)/shard_map/ppermute | solution.py:997
  122.6 22.6 %collective-permute-start.14 = (bf16[2,512,256]{2,1,0:T(8,128)(2,1)S(1)}, bf16[2,512,256]{2,1,0:T(8,128)(2,1)S(1)}, u32[]{:S(2)}, u32[]{:S(2)}) collective-permute-start(bf16[2,512,256]{2,1,0:T(8,128)(2,1)S(1)} %fusion.67.here_ref), channel_id=1, source_target_pairs={{4,0},{8,4},{12,8},{16,12},{20,16},{24,20},{28,24},{5,1},{9,5},{13... | collective-permute-start | bytes 1572872 | tf_op jit(solution)/shard_map/ppermute | solution.py:997
  126.9 25.9 %collective-permute-start.17 = (bf16[1,256,1024]{2,1,0:T(8,128)(2,1)S(1)}, bf16[1,256,1024]{2,1,0:T(8,128)(2,1)S(1)}, u32[]{:S(2)}, u32[]{:S(2)}) collective-permute-start(bf16[1,256,1024]{2,1,0:T(8,128)(2,1)S(1)} %add_convert_fusion.36), channel_id=1, source_target_pairs={{0,2},{1,3},{2,0},{3,1},{4,6},{5,7},{6,4},{7,5},{8,10},{9,11},{10,... | collective-permute-start | bytes 1572872 | tf_op jit(solution)/shard_map/ppermute | solution.py:917
  314.0 453.8 %all-reduce.9.cloned.1.call-start = ((), (), s32[]{:S(2)}) async-start(), calls=%async_computation.1 | async-start | bytes 4194304 | tf_op jit(solution)/shard_map/psum | solution.py:1016
  314.3 29.4 %collective-permute-start.45 = (bf16[1,256,1024]{2,1,0:T(8,128)(2,1)}, bf16[1,256,1024]{2,1,0:T(8,128)(2,1)S(1)}, u32[]{:S(2)}, u32[]{:S(2)}) collective-permute-start(bf16[1,256,1024]{2,1,0:T(8,128)(2,1)} %add_convert_fusion.23), channel_id=1, source_target_pairs={{0,2},{1,3},{2,0},{3,1},{4,6},{5,7},{6,4},{7,5},{8,10},{9,11},{10,... | collective-permute-start | bytes 1572872 | tf_op jit(solution)/shard_map/ppermute | solution.py:917
  331.3 44.5 %collective-permute-start.56 = (bf16[1,256,1024]{2,1,0:T(8,128)(2,1)S(1)}, bf16[1,256,1024]{2,1,0:T(8,128)(2,1)S(1)}, u32[]{:S(2)}, u32[]{:S(2)}) collective-permute-start(bf16[1,256,1024]{2,1,0:T(8,128)(2,1)S(1)} %add_convert_fusion.22), channel_id=1, source_target_pairs={{0,2},{1,3},{2,0},{3,1},{4,6},{5,7},{6,4},{7,5},{8,10},{9,11},{10,... | collective-permute-start | bytes 1572872 | tf_op jit(solution)/shard_map/ppermute | solution.py:917
  347.7 23.8 %collective-permute-start.40 = (bf16[1,256,1024]{2,1,0:T(8,128)(2,1)S(1)}, bf16[1,256,1024]{2,1,0:T(8,128)(2,1)S(1)}, u32[]{:S(2)}, u32[]{:S(2)}) collective-permute-start(bf16[1,256,1024]{2,1,0:T(8,128)(2,1)S(1)} %get-tuple-element.800), channel_id=1, source_target_pairs={{0,1},{1,0},{2,3},{3,2},{4,5},{5,4},{6,7},{7,6},{8,9},{9,8},{10,11... | collective-permute-start | bytes 1572872 | tf_op jit(solution)/shard_map/ppermute | solution.py:911
  360.7 42.2 %collective-permute-start.59 = (bf16[1,256,1024]{2,1,0:T(8,128)(2,1)S(1)}, bf16[1,256,1024]{2,1,0:T(8,128)(2,1)S(1)}, u32[]{:S(2)}, u32[]{:S(2)}) collective-permute-start(bf16[1,256,1024]{2,1,0:T(8,128)(2,1)S(1)} %add_convert_fusion.21), channel_id=1, source_target_pairs={{0,2},{1,3},{2,0},{3,1},{4,6},{5,7},{6,4},{7,5},{8,10},{9,11},{10,... | collective-permute-start | bytes 1572872 | tf_op jit(solution)/shard_map/ppermute | solution.py:917
  361.7 40.1 %collective-permute-start.55 = (bf16[2,512,256]{2,1,0:T(8,128)(2,1)S(1)}, bf16[2,512,256]{2,1,0:T(8,128)(2,1)S(1)}, u32[]{:S(2)}, u32[]{:S(2)}) collective-permute-start(bf16[2,512,256]{2,1,0:T(8,128)(2,1)S(1)} %add_convert_fusion.20), channel_id=1, source_target_pairs={{0,4},{4,8},{8,12},{12,16},{16,20},{20,24},{24,28},{1,5},{5,9},{9,... | collective-permute-start | bytes 1572872 | tf_op jit(solution)/shard_map/ppermute | solution.py:997
  371.6 30.2 %collective-permute-start.54 = (bf16[2,512,256]{2,1,0:T(8,128)(2,1)S(1)}, bf16[2,512,256]{2,1,0:T(8,128)(2,1)S(1)}, u32[]{:S(2)}, u32[]{:S(2)}) collective-permute-start(bf16[2,512,256]{2,1,0:T(8,128)(2,1)S(1)} %add_convert_fusion.18), channel_id=1, source_target_pairs={{4,0},{8,4},{12,8},{16,12},{20,16},{24,20},{28,24},{5,1},{9,5},{13... | collective-permute-start | bytes 1572872 | tf_op jit(solution)/shard_map/ppermute | solution.py:997
  381.4 59.4 %collective-permute-start.53 = (bf16[1,256,1024]{2,1,0:T(8,128)(2,1)}, bf16[1,256,1024]{2,1,0:T(8,128)(2,1)}, u32[]{:S(2)}, u32[]{:S(2)}) collective-permute-start(bf16[1,256,1024]{2,1,0:T(8,128)(2,1)} %add_convert_fusion.19), channel_id=1, source_target_pairs={{0,2},{1,3},{2,0},{3,1},{4,6},{5,7},{6,4},{7,5},{8,10},{9,11},{10,... | collective-permute-start | bytes 1572872 | tf_op jit(solution)/shard_map/ppermute | solution.py:917
  425.7 84.1 %collective-permute-start.68 = (bf16[1,256,1024]{2,1,0:T(8,128)(2,1)}, bf16[1,256,1024]{2,1,0:T(8,128)(2,1)}, u32[]{:S(2)}, u32[]{:S(2)}) collective-permute-start(bf16[1,256,1024]{2,1,0:T(8,128)(2,1)} %add_convert_fusion.15), channel_id=1, source_target_pairs={{0,2},{1,3},{2,0},{3,1},{4,6},{5,7},{6,4},{7,5},{8,10},{9,11},{10,... | collective-permute-start | bytes 1572872 | tf_op jit(solution)/shard_map/ppermute | solution.py:917
  456.3 20.0 %collective-permute-start.69 = (bf16[1,256,1024]{2,1,0:T(8,128)(2,1)S(1)}, bf16[1,256,1024]{2,1,0:T(8,128)(2,1)S(1)}, u32[]{:S(2)}, u32[]{:S(2)}) collective-permute-start(bf16[1,256,1024]{2,1,0:T(8,128)(2,1)S(1)} %add_convert_fusion.14), channel_id=1, source_target_pairs={{0,2},{1,3},{2,0},{3,1},{4,6},{5,7},{6,4},{7,5},{8,10},{9,11},{10,... | collective-permute-start | bytes 1572872 | tf_op jit(solution)/shard_map/ppermute | solution.py:917
  472.8 38.8 %collective-permute-start.72 = (bf16[2,512,256]{2,1,0:T(8,128)(2,1)}, bf16[2,512,256]{2,1,0:T(8,128)(2,1)}, u32[]{:S(2)}, u32[]{:S(2)}) collective-permute-start(bf16[2,512,256]{2,1,0:T(8,128)(2,1)} %add_convert_fusion.13), channel_id=1, source_target_pairs={{4,0},{8,4},{12,8},{16,12},{20,16},{24,20},{28,24},{5,1},{9,5},{13... | collective-permute-start | bytes 1572872 | tf_op jit(solution)/shard_map/ppermute | solution.py:997
  481.0 33.3 %collective-permute-start.67 = (bf16[1,256,1024]{2,1,0:T(8,128)(2,1)}, bf16[1,256,1024]{2,1,0:T(8,128)(2,1)S(1)}, u32[]{:S(2)}, u32[]{:S(2)}) collective-permute-start(bf16[1,256,1024]{2,1,0:T(8,128)(2,1)} %add_convert_fusion.12), channel_id=1, source_target_pairs={{0,2},{1,3},{2,0},{3,1},{4,6},{5,7},{6,4},{7,5},{8,10},{9,11},{10,... | collective-permute-start | bytes 1572872 | tf_op jit(solution)/shard_map/ppermute | solution.py:917
  495.4 29.7 %collective-permute-start.75 = (bf16[2,512,256]{2,1,0:T(8,128)(2,1)S(1)}, bf16[2,512,256]{2,1,0:T(8,128)(2,1)S(1)}, u32[]{:S(2)}, u32[]{:S(2)}) collective-permute-start(bf16[2,512,256]{2,1,0:T(8,128)(2,1)S(1)} %get-tuple-element.570), channel_id=1, source_target_pairs={{4,0},{8,4},{12,8},{16,12},{20,16},{24,20},{28,24},{5,1},{9,5},{13... | collective-permute-start | bytes 1572872 | tf_op jit(solution)/shard_map/ppermute | solution.py:997
  496.9 32.0 %collective-permute-start.76 = (bf16[2,512,256]{2,1,0:T(8,128)(2,1)S(1)}, bf16[2,512,256]{2,1,0:T(8,128)(2,1)S(1)}, u32[]{:S(2)}, u32[]{:S(2)}) collective-permute-start(bf16[2,512,256]{2,1,0:T(8,128)(2,1)S(1)} %get-tuple-element.571), channel_id=1, source_target_pairs={{0,4},{4,8},{8,12},{12,16},{16,20},{20,24},{24,28},{1,5},{5,9},{9,... | collective-permute-start | bytes 1572872 | tf_op jit(solution)/shard_map/ppermute | solution.py:997
  511.5 22.7 %collective-permute-start.71 = (bf16[1,256,1024]{2,1,0:T(8,128)(2,1)S(1)}, bf16[1,256,1024]{2,1,0:T(8,128)(2,1)S(1)}, u32[]{:S(2)}, u32[]{:S(2)}) collective-permute-start(bf16[1,256,1024]{2,1,0:T(8,128)(2,1)S(1)} %add_convert_fusion.11), channel_id=1, source_target_pairs={{0,1},{1,0},{2,3},{3,2},{4,5},{5,4},{6,7},{7,6},{8,9},{9,8},{10,11... | collective-permute-start | bytes 1572872 | tf_op jit(solution)/shard_map/ppermute | solution.py:911
  524.0 255.3 %collective-permute-start.77 = (bf16[1,256,1024]{2,1,0:T(8,128)(2,1)}, bf16[1,256,1024]{2,1,0:T(8,128)(2,1)}, u32[]{:S(2)}, u32[]{:S(2)}) collective-permute-start(bf16[1,256,1024]{2,1,0:T(8,128)(2,1)} %add_convert_fusion.9), channel_id=1, source_target_pairs={{0,2},{1,3},{2,0},{3,1},{4,6},{5,7},{6,4},{7,5},{8,10},{9,11},{10,... | collective-permute-start | bytes 1572872 | tf_op jit(solution)/shard_map/ppermute | solution.py:917
  536.4 255.8 %collective-permute-start.80 = (bf16[1,256,1024]{2,1,0:T(8,128)(2,1)}, bf16[1,256,1024]{2,1,0:T(8,128)(2,1)}, u32[]{:S(2)}, u32[]{:S(2)}) collective-permute-start(bf16[1,256,1024]{2,1,0:T(8,128)(2,1)} %add_convert_fusion.5), channel_id=1, source_target_pairs={{0,2},{1,3},{2,0},{3,1},{4,6},{5,7},{6,4},{7,5},{8,10},{9,11},{10,... | collective-permute-start | bytes 1572872 | tf_op jit(solution)/shard_map/ppermute | solution.py:917
  (364 other events, 2578.4 us)
Sparse Core Ops, SparseCore 0:
  314.0 181.6 all-reduce.6
  500.2 132.9 all-reduce.8

commit v4 on v3

--- a/solution.py
+++ b/solution.py
@@ -884,7 +884,7 @@
 PLAN = (
     "e012ee0eee10ee20102010112122020101212020",
     "101212F020011212e200Ce1e11Ce2eGe202ee100",
-    "S122D00eeWWee",
+    "S122D00WeeWWee",
 )
 
 
@@ -1200,12 +1200,13 @@
             enc_kdoc,
         )
         leave(query_grad)
+        enc.query_grad = query_grad
         from_next = passed_along(to_before, -1)
         from_last = passed_along(to_after, 1)
         yield
         here, from_next, from_last = enter(here, from_next, from_last)
         pair_grad = (here + from_next.astype(WIDE) + from_last.astype(WIDE)).astype(LOW)
-        enc.query_grad, enc.pair_grad = query_grad, pair_grad
+        enc.pair_grad = pair_grad
         partial_value = back_project(query_grad, enc_qkv[0]) + jnp.einsum(
             "csf,cdf->sd", pair_grad, enc_qkv[1:], preferred_element_type=WIDE
         )
@@ -1395,7 +1396,7 @@
             "sd,csf->cdf", final[0], cross.pair_grad, preferred_element_type=WIDE
         ).astype(LOW)
         leave(wkv)
-        weights.cross = sum_seq(weights.cross + (wkv,), 1)
+        weights.cross = list(weights.cross) + [wkv]
         yield
 
     def enc_ffn_weights():
@@ -1436,11 +1437,14 @@
         yield
 
     def enc_weights():
-        query_grad, pair_grad, grads = enter(enc.query_grad, enc.pair_grad, enc.att_rows)
+        query_grad, grads = enter(enc.query_grad, enc.att_rows)
         query = weight_grad(straight_rows, query_grad).astype(LOW)
+        wout = rows_weight_grad([enc.att], [grads]).astype(LOW)
+        leave((query, wout))
+        yield
+        (pair_grad,) = enter(enc.pair_grad)
         key = weight_grad(straight_rows, pair_grad[:1]).astype(LOW)
         value = weight_grad(straight_rows, pair_grad[1:]).astype(LOW)
-        wout = rows_weight_grad([enc.att], [grads]).astype(LOW)
         sums = jnp.concatenate(
             [
                 enc.att_sums,
@@ -1453,14 +1457,14 @@
         )
         sums = sums + swap_core(sums)
         sums = jnp.pad(sums, ((0, -sums.shape[0] % 16), (0, 0))).astype(LOW)
-        parts = weights.enc + weights.self + [wout, query, key, value, sums]
+        parts = weights.cross + weights.enc + weights.self + [wout, query, key, value, sums]
         pieces = [flat(part) for part in parts]
         leave((wout, query, key, value, sums))
         yield
         pieces = enter(*pieces)
         summed = link_sum(pieces, lax.axis_size("seq"))
         leave(summed[0])
-        weights.ffn, weights.cross = enter(weights.ffn, weights.cross)
+        (weights.ffn,) = enter(weights.ffn)
         weights.last = [
             unflat(cells.astype(WIDE), part.shape) for cells, part in zip(summed, parts)
         ]
@@ -1476,10 +1480,8 @@
             pass
 
     ffn_down_grad, ffn_up_grad = [value.astype(WIDE) for value in weights.ffn]
-    cross_wout_grad, cross_wq_grad, cross_wkv_grad = [
-        value.astype(WIDE) for value in weights.cross
-    ]
-    enc_down_grad, enc_up_grad, *found = weights.last
+    cross_wout_grad, cross_wq_grad, cross_wkv_grad, *found = weights.last
+    enc_down_grad, enc_up_grad, *found = found
     self_wout_grad, self_rel_grad, *found = found
     self_qkv_grad = jnp.stack(found[:3])
     enc_wout_grad, sums = found[3], found[7]

time: 816 us -> 822 us (level)
  Pallas kernels: 329 us -> 341 us
    pallas_call x1, Pallas kernels: 218 us -> 234 us  [link_sum(): pl.pallas_call(functools.partial(tree_kernel, count, len(pieces)), in_spe...]
    unnamed x647 -> x652, local copies, waits for them, and re-layouts: 31.6 us -> 29.3 us
  transfers between devices with their start and end apart: 85 -> 84, of which waited for: 30 -> 30; matrix products, arithmetic and copies ran while one was open for 26% -> 26% of each run, Pallas kernels for 39% -> 40%
where the time goes in v4:
time: 822 us; the launch traced here: 815 us
  Pallas kernels  341 us (41%)
  matrix products  119 us (14%)
  waiting for transfers between devices  112 us (14%)
  other arithmetic  98 us (12%)
  starting transfers between devices  85.9 us (10%)
  local copies, waits for them, and re-layouts  39.7 us (5%)
  between operations  19.7 us (2%)
    pallas_call x1, Pallas kernels, link_sum(): pl.pallas_call(functools.partial(tree_kernel, count, len(pieces)), in_spe...  234 us
    ppermute x23, waiting for transfers between devices, swap_chip(): lax.ppermute(low, 'tp', [(place, place ^ hop) for place in range(count)])  77 us
    ppermute x10, starting transfers between devices, passed_along(): return lax.ppermute(value, 'seq', pairs)  52 us
    dot_general x39, matrix products, project(): return jnp.einsum('gsd,df->gsf', rows, weight, preferred_element_type=WIDE)  38.3 us
    pallas_call x4, Pallas kernels, full_backward(): local_call(functools.partial(full_backward_kernel, with_self), (streams,...  37.3 us
    dot_general x15, matrix products, weight_grad(): return jnp.einsum('gsd,gsf->df', rows, grads, preferred_element_type=WIDE)  34.7 us
    unnamed x652, local copies, waits for them, and re-layouts  29.3 us
    pallas_call x4, Pallas kernels, full_forward(): local_call(functools.partial(full_forward_kernel, with_self), (streams, r...  27.3 us
  transfers between devices with their start and end apart: 84, of which 30 were waited for; matrix products, arithmetic and copies ran while one was open for 26% of the time, Pallas kernels for 40%

profile of v4, /device:TPU:0, one launch (start us, length us, event | category | flops | bytes accessed | tf_op | source)
XLA Modules:
  0.0 814.6 jit_solution(1489524887093975219)
XLA Ops:
  37.0 7.6 shard_map.575
  47.2 6.5 collective-permute-start.4
  58.2 6.9 collective-permute-done.4.refs_2_.refs_5_
  82.4 6.5 shard_map.577
  104.9 6.5 shard_map.578
  128.5 14.5 %collective-permute-done.13.before_ref = bf16[2,512,256]{2,1,0:T(8,128)(2,1)S(1)} collective-permute-done((bf16[2,512,256]{2,1,0:T(8,128)(2,1)S(1)}, bf16[2,512,256]{2,1,0:T(8,128)(2,1)S(1)}, u32[]{:S(2)}, u32[]{:S(2)}) %collective-permute-start.13) | collective-permute-done | bytes 524320 | tf_op jit(solution)/shard_map/ppermute | solution.py:997
  169.6 6.7 shard_map.581
  187.6 9.1 %collective-permute-done.26 = bf16[1,256,1024]{2,1,0:T(8,128)(2,1)S(1)} collective-permute-done((bf16[1,256,1024]{2,1,0:T(8,128)(2,1)S(1)}, bf16[1,256,1024]{2,1,0:T(8,128)(2,1)S(1)}, u32[]{:S(2)}, u32[]{:S(2)}) %collective-permute-start.26) | collective-permute-done | bytes 524320 | tf_op jit(solution)/shard_map/ppermute | solution.py:917
  203.2 9.1 %collective-permute-done.28 = bf16[1,256,1024]{2,1,0:T(8,128)(2,1)S(1)} collective-permute-done((bf16[1,256,1024]{2,1,0:T(8,128)(2,1)S(1)}, bf16[1,256,1024]{2,1,0:T(8,128)(2,1)S(1)}, u32[]{:S(2)}, u32[]{:S(2)}) %collective-permute-start.28) | collective-permute-done | bytes 524320 | tf_op jit(solution)/shard_map/ppermute | solution.py:917
  219.0 9.2 %collective-permute-done.27 = bf16[1,256,1024]{2,1,0:T(8,128)(2,1)S(1)} collective-permute-done((bf16[1,256,1024]{2,1,0:T(8,128)(2,1)S(1)}, bf16[1,256,1024]{2,1,0:T(8,128)(2,1)S(1)}, u32[]{:S(2)}, u32[]{:S(2)}) %collective-permute-start.27) | collective-permute-done | bytes 524320 | tf_op jit(solution)/shard_map/ppermute | solution.py:917
  236.6 8.7 %collective-permute-done.33 = bf16[1,256,1024]{2,1,0:T(8,128)(2,1)S(1)} collective-permute-done((bf16[1,256,1024]{2,1,0:T(8,128)(2,1)S(1)}, bf16[1,256,1024]{2,1,0:T(8,128)(2,1)S(1)}, u32[]{:S(2)}, u32[]{:S(2)}) %collective-permute-start.33) | collective-permute-done | bytes 524320 | tf_op jit(solution)/shard_map/ppermute | solution.py:917
  254.9 8.8 %collective-permute-done.37 = bf16[1,256,1024]{2,1,0:T(8,128)(2,1)S(1)} collective-permute-done((bf16[1,256,1024]{2,1,0:T(8,128)(2,1)S(1)}, bf16[1,256,1024]{2,1,0:T(8,128)(2,1)S(1)}, u32[]{:S(2)}, u32[]{:S(2)}) %collective-permute-start.37) | collective-permute-done | bytes 524320 | tf_op jit(solution)/shard_map/ppermute | solution.py:917
  296.7 9.1 %shard_map.582 = (bf16[1,512,256]{2,1,0:T(8,128)(2,1)S(1)}, bf16[2,512,256]{2,1,0:T(8,128)(2,1)S(1)}, f32[2,512,256]{2,1,0:T(8,128)S(1)}, bf16[2,512,256]{2,1,0:T(8,128)(2,1)S(1)}) custom-call(s32[2,4]{1,0:T(2,128)S(1)} %pad_add_fusion.bounds_ref, bf16[1,512,256]{2,1,0:T(8,128)(2,1)S(1)} %copy-done.15, bf16[1,512,256]{2,1,0:T(8,128)(2,1)S(1)} %pad_maximum_fusion.7.grad_ref, ...), custom_call_target="tpu_custom_call" | custom-call | flops 1000 | bytes 1000 | tf_op jit(solution)/shard_map/pallas_call | solution.py:544
  314.5 10.0 %collective-permute-done.46 = bf16[1,256,1024]{2,1,0:T(8,128)(2,1)} collective-permute-done((bf16[1,256,1024]{2,1,0:T(8,128)(2,1)}, bf16[1,256,1024]{2,1,0:T(8,128)(2,1)}, u32[]{:S(2)}, u32[]{:S(2)}) %collective-permute-start.46) | collective-permute-done | bytes 524320 | tf_op jit(solution)/shard_map/ppermute | solution.py:917
  330.4 8.9 %shard_map.583 = (bf16[1,512,256]{2,1,0:T(8,128)(2,1)S(1)}, bf16[2,512,256]{2,1,0:T(8,128)(2,1)S(1)}, f32[2,512,256]{2,1,0:T(8,128)S(1)}, bf16[2,512,256]{2,1,0:T(8,128)(2,1)S(1)}) custom-call(s32[2,4]{1,0:T(2,128)S(1)} %pad_add_fusion.bounds_ref, bf16[1,512,256]{2,1,0:T(8,128)(2,1)S(1)} %copy-done.13, bf16[1,512,256]{2,1,0:T(8,128)(2,1)S(1)} %pad_maximum_fusion.8.grad_ref, ...), custom_call_target="tpu_custom_call" | custom-call | flops 1000 | bytes 1000 | tf_op jit(solution)/shard_map/pallas_call | solution.py:544
  345.9 8.9 %shard_map.584 = (bf16[1,512,256]{2,1,0:T(8,128)(2,1)S(1)}, bf16[2,512,256]{2,1,0:T(8,128)(2,1)S(1)}, f32[2,512,256]{2,1,0:T(8,128)S(1)}, bf16[2,512,256]{2,1,0:T(8,128)(2,1)S(1)}) custom-call(s32[2,4]{1,0:T(2,128)S(1)} %pad_add_fusion.bounds_ref, bf16[1,512,256]{2,1,0:T(8,128)(2,1)S(1)} %copy-done.11, bf16[1,512,256]{2,1,0:T(8,128)(2,1)S(1)} %pad_maximum_fusion.9.grad_ref, ...), custom_call_target="tpu_custom_call" | custom-call | flops 1000 | bytes 1000 | tf_op jit(solution)/shard_map/pallas_call | solution.py:544
  356.7 12.1 %collective-permute-start.55 = (bf16[2,512,256]{2,1,0:T(8,128)(2,1)S(1)}, bf16[2,512,256]{2,1,0:T(8,128)(2,1)S(1)}, u32[]{:S(2)}, u32[]{:S(2)}) collective-permute-start(bf16[2,512,256]{2,1,0:T(8,128)(2,1)S(1)} %add_convert_fusion.20), channel_id=1, source_target_pairs={{0,4},{4,8},{8,12},{12,16},{16,20},{20,24},{24,28},{1,5},{5,9},{9,... | collective-permute-start | bytes 1572872 | tf_op jit(solution)/shard_map/ppermute | solution.py:997
  381.4 7.1 shard_map.585
  399.6 8.8 %shard_map.586 = (bf16[1,512,256]{2,1,0:T(8,128)(2,1)S(1)}, bf16[1,512,128]{2,1,0:T(8,128)(2,1)S(1)}, bf16[2,512,256]{2,1,0:T(8,128)(2,1)S(1)}, f32[2,512,256]{2,1,0:T(8,128)S(1)}, bf16[1,2,512,256]{3,2,1,0:T(8,128)(2,1)S(1)}) custom-call(s32[4]{0:T(128)S(1)} %and_select_fusion.1.refs_0_, bf16[1,512,256]{2,1,0:T(8,128)(2,1)S(1)} %copy-done.55, ...), custom_call_target="tpu_custom_call" | custom-call | flops 1000 | bytes 1000 | tf_op jit(solution)/shard_map/pallas_call | solution.py:641
  418.7 9.1 %collective-permute-done.60 = bf16[1,256,1024]{2,1,0:T(8,128)(2,1)S(1)} collective-permute-done((bf16[1,256,1024]{2,1,0:T(8,128)(2,1)S(1)}, bf16[1,256,1024]{2,1,0:T(8,128)(2,1)S(1)}, u32[]{:S(2)}, u32[]{:S(2)}) %collective-permute-start.60) | collective-permute-done | bytes 524320 | tf_op jit(solution)/shard_map/ppermute | solution.py:917
  450.7 8.8 %shard_map.587 = (bf16[1,512,256]{2,1,0:T(8,128)(2,1)S(1)}, bf16[1,512,128]{2,1,0:T(8,128)(2,1)S(1)}, bf16[2,512,256]{2,1,0:T(8,128)(2,1)S(1)}, f32[2,512,256]{2,1,0:T(8,128)S(1)}, bf16[1,2,512,256]{3,2,1,0:T(8,128)(2,1)S(1)}) custom-call(s32[4]{0:T(128)S(1)} %and_select_fusion.1.refs_0_, bf16[1,512,256]{2,1,0:T(8,128)(2,1)S(1)} %copy-done.53, ...), custom_call_target="tpu_custom_call" | custom-call | flops 1000 | bytes 1000 | tf_op jit(solution)/shard_map/pallas_call | solution.py:641
  477.7 10.3 %shard_map.588 = (bf16[1,512,256]{2,1,0:T(8,128)(2,1)S(1)}, bf16[2,512,256]{2,1,0:T(8,128)(2,1)S(1)}, f32[2,512,256]{2,1,0:T(8,128)S(1)}, bf16[2,512,256]{2,1,0:T(8,128)(2,1)S(1)}) custom-call(s32[2,4]{1,0:T(2,128)S(1)} %pad_add_fusion.bounds_ref, bf16[1,512,256]{2,1,0:T(8,128)(2,1)S(1)} %copy-done.32, bf16[1,512,256]{2,1,0:T(8,128)(2,1)S(1)} %pad_maximum_fusion.13.grad_ref, ...), custom_call_target="tpu_custom_call" | custom-call | flops 1000 | bytes 1000 | tf_op jit(solution)/shard_map/pallas_call | solution.py:544
  489.4 15.8 %collective-permute-start.76 = (bf16[2,512,256]{2,1,0:T(8,128)(2,1)S(1)}, bf16[2,512,256]{2,1,0:T(8,128)(2,1)S(1)}, u32[]{:S(2)}, u32[]{:S(2)}) collective-permute-start(bf16[2,512,256]{2,1,0:T(8,128)(2,1)S(1)} %get-tuple-element.574), channel_id=1, source_target_pairs={{0,4},{4,8},{8,12},{12,16},{16,20},{20,24},{24,28},{1,5},{5,9},{9,... | collective-permute-start | bytes 1572872 | tf_op jit(solution)/shard_map/ppermute | solution.py:997
  538.9 234.2 %shard_map.589 = (bf16[256,1024]{1,0:T(8,128)(2,1)}, bf16[1024,256]{1,0:T(8,128)(2,1)}, bf16[2048,256]{1,0:T(8,128)(2,1)}, bf16[1024,1024]{1,0:T(8,128)(2,1)}, b...) custom-call(bf16[256,1024]{1,0:T(8,128)(2,1)} %fusion.55.refs_0_, ...), custom_call_target="tpu_custom_call" | custom-call | flops 1000 | bytes 1000 | tf_op jit(solution)/shard_map/pallas_call | solution.py:860
  (1148 shorter events, 351.5 us)
Async XLA Ops:
  7.2 768.0 %all-reduce.5.cloned.1.call-start = ((), (), s32[]{:S(2)}) async-start(), calls=%async_computation | async-start | bytes 8388608 | tf_op jit(solution)/shard_map/psum | solution.py:1016
  9.7 27.3 %collective-permute-start = (bf16[2,512,256]{2,1,0:T(8,128)(2,1)S(1)}, bf16[2,512,256]{2,1,0:T(8,128)(2,1)S(1)}, u32[]{:S(2)}, u32[]{:S(2)}) collective-permute-start(bf16[2,512,256]{2,1,0:T(8,128)(2,1)S(1)} %fusion.76.here_ref), channel_id=1, source_target_pairs={{0,4},{4,8},{8,12},{12,16},{16,20},{20,24},{24,28},{1,5},{5,9},{9,... | collective-permute-start | bytes 1572872 | tf_op jit(solution)/shard_map/ppermute | solution.py:997
  14.6 22.4 %collective-permute-start.1 = (bf16[2,512,256]{2,1,0:T(8,128)(2,1)S(1)}, bf16[2,512,256]{2,1,0:T(8,128)(2,1)}, u32[]{:S(2)}, u32[]{:S(2)}) collective-permute-start(bf16[2,512,256]{2,1,0:T(8,128)(2,1)S(1)} %fusion.76.here_ref), channel_id=1, source_target_pairs={{4,0},{8,4},{12,8},{16,12},{20,16},{24,20},{28,24},{5,1},{9,5},{13... | collective-permute-start | bytes 1572872 | tf_op jit(solution)/shard_map/ppermute | solution.py:997
  101.1 20.7 %collective-permute-start.12 = (bf16[1,256,1024]{2,1,0:T(8,128)(2,1)}, bf16[1,256,1024]{2,1,0:T(8,128)(2,1)}, u32[]{:S(2)}, u32[]{:S(2)}) collective-permute-start(bf16[1,256,1024]{2,1,0:T(8,128)(2,1)} %fusion.79), channel_id=1, source_target_pairs={{0,1},{1,0},{2,3},{3,2},{4,5},{5,4},{6,7},{7,6},{8,9},{9,8},{10,11... | collective-permute-start | bytes 1572872 | tf_op jit(solution)/shard_map/ppermute | solution.py:911
  114.8 28.3 %collective-permute-start.13 = (bf16[2,512,256]{2,1,0:T(8,128)(2,1)S(1)}, bf16[2,512,256]{2,1,0:T(8,128)(2,1)S(1)}, u32[]{:S(2)}, u32[]{:S(2)}) collective-permute-start(bf16[2,512,256]{2,1,0:T(8,128)(2,1)S(1)} %fusion.67.here_ref), channel_id=1, source_target_pairs={{0,4},{4,8},{8,12},{12,16},{16,20},{20,24},{24,28},{1,5},{5,9},{9,... | collective-permute-start | bytes 1572872 | tf_op jit(solution)/shard_map/ppermute | solution.py:997
  120.3 22.8 %collective-permute-start.14 = (bf16[2,512,256]{2,1,0:T(8,128)(2,1)S(1)}, bf16[2,512,256]{2,1,0:T(8,128)(2,1)S(1)}, u32[]{:S(2)}, u32[]{:S(2)}) collective-permute-start(bf16[2,512,256]{2,1,0:T(8,128)(2,1)S(1)} %fusion.67.here_ref), channel_id=1, source_target_pairs={{4,0},{8,4},{12,8},{16,12},{20,16},{24,20},{28,24},{5,1},{9,5},{13... | collective-permute-start | bytes 1572872 | tf_op jit(solution)/shard_map/ppermute | solution.py:997
  124.8 25.4 %collective-permute-start.17 = (bf16[1,256,1024]{2,1,0:T(8,128)(2,1)S(1)}, bf16[1,256,1024]{2,1,0:T(8,128)(2,1)S(1)}, u32[]{:S(2)}, u32[]{:S(2)}) collective-permute-start(bf16[1,256,1024]{2,1,0:T(8,128)(2,1)S(1)} %add_convert_fusion.36), channel_id=1, source_target_pairs={{0,2},{1,3},{2,0},{3,1},{4,6},{5,7},{6,4},{7,5},{8,10},{9,11},{10,... | collective-permute-start | bytes 1572872 | tf_op jit(solution)/shard_map/ppermute | solution.py:917
  311.1 29.0 %collective-permute-start.45 = (bf16[1,256,1024]{2,1,0:T(8,128)(2,1)}, bf16[1,256,1024]{2,1,0:T(8,128)(2,1)S(1)}, u32[]{:S(2)}, u32[]{:S(2)}) collective-permute-start(bf16[1,256,1024]{2,1,0:T(8,128)(2,1)} %add_convert_fusion.23), channel_id=1, source_target_pairs={{0,2},{1,3},{2,0},{3,1},{4,6},{5,7},{6,4},{7,5},{8,10},{9,11},{10,... | collective-permute-start | bytes 1572872 | tf_op jit(solution)/shard_map/ppermute | solution.py:917
  328.3 44.4 %collective-permute-start.56 = (bf16[1,256,1024]{2,1,0:T(8,128)(2,1)S(1)}, bf16[1,256,1024]{2,1,0:T(8,128)(2,1)S(1)}, u32[]{:S(2)}, u32[]{:S(2)}) collective-permute-start(bf16[1,256,1024]{2,1,0:T(8,128)(2,1)S(1)} %add_convert_fusion.22), channel_id=1, source_target_pairs={{0,2},{1,3},{2,0},{3,1},{4,6},{5,7},{6,4},{7,5},{8,10},{9,11},{10,... | collective-permute-start | bytes 1572872 | tf_op jit(solution)/shard_map/ppermute | solution.py:917
  343.3 25.8 %collective-permute-start.40 = (bf16[1,256,1024]{2,1,0:T(8,128)(2,1)S(1)}, bf16[1,256,1024]{2,1,0:T(8,128)(2,1)S(1)}, u32[]{:S(2)}, u32[]{:S(2)}) collective-permute-start(bf16[1,256,1024]{2,1,0:T(8,128)(2,1)S(1)} %get-tuple-element.803), channel_id=1, source_target_pairs={{0,1},{1,0},{2,3},{3,2},{4,5},{5,4},{6,7},{7,6},{8,9},{9,8},{10,11... | collective-permute-start | bytes 1572872 | tf_op jit(solution)/shard_map/ppermute | solution.py:911
  355.6 37.8 %collective-permute-start.59 = (bf16[1,256,1024]{2,1,0:T(8,128)(2,1)S(1)}, bf16[1,256,1024]{2,1,0:T(8,128)(2,1)S(1)}, u32[]{:S(2)}, u32[]{:S(2)}) collective-permute-start(bf16[1,256,1024]{2,1,0:T(8,128)(2,1)S(1)} %add_convert_fusion.21), channel_id=1, source_target_pairs={{0,2},{1,3},{2,0},{3,1},{4,6},{5,7},{6,4},{7,5},{8,10},{9,11},{10,... | collective-permute-start | bytes 1572872 | tf_op jit(solution)/shard_map/ppermute | solution.py:917
  356.7 34.6 %collective-permute-start.55 = (bf16[2,512,256]{2,1,0:T(8,128)(2,1)S(1)}, bf16[2,512,256]{2,1,0:T(8,128)(2,1)S(1)}, u32[]{:S(2)}, u32[]{:S(2)}) collective-permute-start(bf16[2,512,256]{2,1,0:T(8,128)(2,1)S(1)} %add_convert_fusion.20), channel_id=1, source_target_pairs={{0,4},{4,8},{8,12},{12,16},{16,20},{20,24},{24,28},{1,5},{5,9},{9,... | collective-permute-start | bytes 1572872 | tf_op jit(solution)/shard_map/ppermute | solution.py:997
  369.1 22.2 %collective-permute-start.54 = (bf16[2,512,256]{2,1,0:T(8,128)(2,1)S(1)}, bf16[2,512,256]{2,1,0:T(8,128)(2,1)S(1)}, u32[]{:S(2)}, u32[]{:S(2)}) collective-permute-start(bf16[2,512,256]{2,1,0:T(8,128)(2,1)S(1)} %add_convert_fusion.18), channel_id=1, source_target_pairs={{4,0},{8,4},{12,8},{16,12},{20,16},{24,20},{28,24},{5,1},{9,5},{13... | collective-permute-start | bytes 1572872 | tf_op jit(solution)/shard_map/ppermute | solution.py:997
  379.3 50.7 %collective-permute-start.53 = (bf16[1,256,1024]{2,1,0:T(8,128)(2,1)S(1)}, bf16[1,256,1024]{2,1,0:T(8,128)(2,1)S(1)}, u32[]{:S(2)}, u32[]{:S(2)}) collective-permute-start(bf16[1,256,1024]{2,1,0:T(8,128)(2,1)S(1)} %add_convert_fusion.19), channel_id=1, source_target_pairs={{0,2},{1,3},{2,0},{3,1},{4,6},{5,7},{6,4},{7,5},{8,10},{9,11},{10,... | collective-permute-start | bytes 1572872 | tf_op jit(solution)/shard_map/ppermute | solution.py:917
  415.8 89.4 %collective-permute-start.68 = (bf16[1,256,1024]{2,1,0:T(8,128)(2,1)}, bf16[1,256,1024]{2,1,0:T(8,128)(2,1)}, u32[]{:S(2)}, u32[]{:S(2)}) collective-permute-start(bf16[1,256,1024]{2,1,0:T(8,128)(2,1)} %add_convert_fusion.15), channel_id=1, source_target_pairs={{0,2},{1,3},{2,0},{3,1},{4,6},{5,7},{6,4},{7,5},{8,10},{9,11},{10,... | collective-permute-start | bytes 1572872 | tf_op jit(solution)/shard_map/ppermute | solution.py:917
  449.0 20.0 %collective-permute-start.69 = (bf16[1,256,1024]{2,1,0:T(8,128)(2,1)S(1)}, bf16[1,256,1024]{2,1,0:T(8,128)(2,1)S(1)}, u32[]{:S(2)}, u32[]{:S(2)}) collective-permute-start(bf16[1,256,1024]{2,1,0:T(8,128)(2,1)S(1)} %add_convert_fusion.14), channel_id=1, source_target_pairs={{0,2},{1,3},{2,0},{3,1},{4,6},{5,7},{6,4},{7,5},{8,10},{9,11},{10,... | collective-permute-start | bytes 1572872 | tf_op jit(solution)/shard_map/ppermute | solution.py:917
  465.5 41.5 %collective-permute-start.72 = (bf16[2,512,256]{2,1,0:T(8,128)(2,1)}, bf16[2,512,256]{2,1,0:T(8,128)(2,1)}, u32[]{:S(2)}, u32[]{:S(2)}) collective-permute-start(bf16[2,512,256]{2,1,0:T(8,128)(2,1)} %add_convert_fusion.13), channel_id=1, source_target_pairs={{4,0},{8,4},{12,8},{16,12},{20,16},{24,20},{28,24},{5,1},{9,5},{13... | collective-permute-start | bytes 1572872 | tf_op jit(solution)/shard_map/ppermute | solution.py:997
  474.0 35.9 %collective-permute-start.67 = (bf16[1,256,1024]{2,1,0:T(8,128)(2,1)}, bf16[1,256,1024]{2,1,0:T(8,128)(2,1)S(1)}, u32[]{:S(2)}, u32[]{:S(2)}) collective-permute-start(bf16[1,256,1024]{2,1,0:T(8,128)(2,1)} %add_convert_fusion.12), channel_id=1, source_target_pairs={{0,2},{1,3},{2,0},{3,1},{4,6},{5,7},{6,4},{7,5},{8,10},{9,11},{10,... | collective-permute-start | bytes 1572872 | tf_op jit(solution)/shard_map/ppermute | solution.py:917
  488.0 35.7 %collective-permute-start.75 = (bf16[2,512,256]{2,1,0:T(8,128)(2,1)S(1)}, bf16[2,512,256]{2,1,0:T(8,128)(2,1)S(1)}, u32[]{:S(2)}, u32[]{:S(2)}) collective-permute-start(bf16[2,512,256]{2,1,0:T(8,128)(2,1)S(1)} %get-tuple-element.573), channel_id=1, source_target_pairs={{4,0},{8,4},{12,8},{16,12},{20,16},{24,20},{28,24},{5,1},{9,5},{13... | collective-permute-start | bytes 1572872 | tf_op jit(solution)/shard_map/ppermute | solution.py:997
  489.4 38.4 %collective-permute-start.76 = (bf16[2,512,256]{2,1,0:T(8,128)(2,1)S(1)}, bf16[2,512,256]{2,1,0:T(8,128)(2,1)S(1)}, u32[]{:S(2)}, u32[]{:S(2)}) collective-permute-start(bf16[2,512,256]{2,1,0:T(8,128)(2,1)S(1)} %get-tuple-element.574), channel_id=1, source_target_pairs={{0,4},{4,8},{8,12},{12,16},{16,20},{20,24},{24,28},{1,5},{5,9},{9,... | collective-permute-start | bytes 1572872 | tf_op jit(solution)/shard_map/ppermute | solution.py:997
  506.9 26.2 %collective-permute-start.71 = (bf16[1,256,1024]{2,1,0:T(8,128)(2,1)S(1)}, bf16[1,256,1024]{2,1,0:T(8,128)(2,1)S(1)}, u32[]{:S(2)}, u32[]{:S(2)}) collective-permute-start(bf16[1,256,1024]{2,1,0:T(8,128)(2,1)S(1)} %add_convert_fusion.11), channel_id=1, source_target_pairs={{0,1},{1,0},{2,3},{3,2},{4,5},{5,4},{6,7},{7,6},{8,9},{9,8},{10,11... | collective-permute-start | bytes 1572872 | tf_op jit(solution)/shard_map/ppermute | solution.py:911
  511.8 21.3 %collective-permute-start.74 = (bf16[1,256,1024]{2,1,0:T(8,128)(2,1)S(1)}, bf16[1,256,1024]{2,1,0:T(8,128)(2,1)S(1)}, u32[]{:S(2)}, u32[]{:S(2)}) collective-permute-start(bf16[1,256,1024]{2,1,0:T(8,128)(2,1)S(1)} %add_convert_fusion.8), channel_id=1, source_target_pairs={{0,1},{1,0},{2,3},{3,2},{4,5},{5,4},{6,7},{7,6},{8,9},{9,8},{10,11... | collective-permute-start | bytes 1572872 | tf_op jit(solution)/shard_map/ppermute | solution.py:911
  522.5 259.4 %collective-permute-start.77 = (bf16[1,256,1024]{2,1,0:T(8,128)(2,1)}, bf16[1,256,1024]{2,1,0:T(8,128)(2,1)}, u32[]{:S(2)}, u32[]{:S(2)}) collective-permute-start(bf16[1,256,1024]{2,1,0:T(8,128)(2,1)} %add_convert_fusion.9), channel_id=1, source_target_pairs={{0,2},{1,3},{2,0},{3,1},{4,6},{5,7},{6,4},{7,5},{8,10},{9,11},{10,... | collective-permute-start | bytes 1572872 | tf_op jit(solution)/shard_map/ppermute | solution.py:917
  535.3 265.6 %collective-permute-start.80 = (bf16[1,256,1024]{2,1,0:T(8,128)(2,1)}, bf16[1,256,1024]{2,1,0:T(8,128)(2,1)}, u32[]{:S(2)}, u32[]{:S(2)}) collective-permute-start(bf16[1,256,1024]{2,1,0:T(8,128)(2,1)} %add_convert_fusion.5), channel_id=1, source_target_pairs={{0,2},{1,3},{2,0},{3,1},{4,6},{5,7},{6,4},{7,5},{8,10},{9,11},{10,... | collective-permute-start | bytes 1572872 | tf_op jit(solution)/shard_map/ppermute | solution.py:917
  (366 other events, 2565.1 us)
Sparse Core Ops, SparseCore 0:
  310.9 183.8 all-reduce.4
